TPU v7x, 256 devices: a whole 4x4x8 slice. The times are simulated.
256 devices in a mesh: layer: 8 (over z_hi, core), tok: 32 (over x, z_lo, y).
Axes of the slice: x: 4, y: 4, z: 8 (z_hi: 4, z_lo: 2; z = z_hi * 2 + z_lo), core: 2. Of those that a mesh axis runs over, the one named last changes fastest.
Arguments:
- train_act: bfloat16 [16, 65536, 256], P('layer', 'tok'), may hold values from -0.75 to 0.75
- train_grad: bfloat16 [16, 65536, 256], P('layer', 'tok'), may hold values from -0.75 to 0.75
- test_act: bfloat16 [16, 2048, 256], P('layer', 'tok'), may hold values from -0.75 to 0.75
- test_grad: bfloat16 [16, 2048, 256], P('layer', 'tok'), may hold values from -0.75 to 0.75
- segment_ids: int32 [2048], replicated, may hold values from 0 to 127, as said below
Outputs:
- scores: float32 [128, 65536], P('layer', 'tok')
Inputs may be any that keep to these rules, and one draw needn't show every extreme that they name: `segment_ids`: each of the 128 queries has exactly 16 test tokens, placed anywhere among the 2048.
All inputs are finite; a program needn't handle non-finite values.
Results may differ from a plain program's by a relative error of at most 0.0029.
Values may be sent and summed in bfloat16 or wider, within the bound.
No kernel may reach another device: no remote copies, remote signals or barrier semaphores. Data moves between devices by JAX's collectives and lax.ppermute only.
A program may use at most 128 MiB of HBM per device.

v0:
```python
import math

import jax
import jax.numpy as jnp
from jax import lax
from jax.sharding import PartitionSpec as P

Q = 128


def sent_together(arrays, axis, dim, along):
    both = jnp.concatenate(arrays, axis=along)
    result, at, done = (lax.all_gather(both, axis, axis=dim, tiled=True), 0, [])
    for a in arrays:
        done.append(lax.slice_in_dim(result, at, at + a.shape[along], axis=along))
        at += a.shape[along]
    return tuple(done)


def cut_along(value, dim, peers):
    before, after = (value.shape[:dim], value.shape[dim + 1 :])
    return jnp.moveaxis(value.reshape(*before, peers, -1, *after), dim, 0)


def sum_at_owner(value, axis, dim):
    peers = lax.axis_size(axis)
    tiles = lax.all_to_all(cut_along(value, dim, peers), axis, 0, 0, tiled=True)
    return jnp.sum(tiles, axis=0)


def gram_product(test_a, test_g, train_a, train_g):
    act_gram = jnp.einsum("sp,tp->st", test_a, train_a, preferred_element_type=jnp.float32)
    grad_gram = jnp.einsum("sp,tp->st", test_g, train_g, preferred_element_type=jnp.float32)
    return (act_gram * grad_gram).astype(jnp.bfloat16)


def on_device(train_act, train_grad, test_act, test_grad, segment_ids):
    layer_count = train_act.shape[0]
    train_rows = train_act.shape[1]
    labels = jnp.arange(Q, dtype=jnp.int32)[:, None]
    empty = jnp.zeros((Q, train_rows), jnp.float32)
    running = empty
    act_rows, grad_rows = sent_together((test_act, test_grad), "tok", 1, 0)
    for layer_idx in range(layer_count):
        add_running = running
        add_act_rows = act_rows[layer_idx]
        add_grad_rows = grad_rows[layer_idx]
        row_count = add_act_rows.shape[0]
        stride = math.gcd(row_count, 512)
        for offset in range(0, row_count, stride):
            query_of = lax.dynamic_slice_in_dim(segment_ids, offset, stride)
            select = (query_of[None, :] == labels).astype(jnp.bfloat16)
            product = gram_product(
                add_act_rows[offset : offset + stride],
                add_grad_rows[offset : offset + stride],
                train_act[layer_idx],
                train_grad[layer_idx],
            )
            add_running = add_running + jnp.dot(select, product, preferred_element_type=jnp.float32)
        running = add_running
    return sum_at_owner(running, "layer", 0)


def solution(mesh):
    placed = (
        P("layer", "tok", None),
        P("layer", "tok", None),
        P("layer", "tok", None),
        P("layer", "tok", None),
        P(),
    )
    return jax.shard_map(
        on_device, mesh=mesh, in_specs=placed, out_specs=P("layer", "tok"), check_vma=False
    )
```

profile of v0, /device:TPU:1, one launch (start us, length us, event | category | flops | bytes accessed | tf_op | source)
XLA Modules:
  0.0 272.9 jit_solution(18362190753967681884)
XLA Ops:
  6.5 0.0 copy-start
  6.5 0.0 all-gather.2.cloned.1.call-start
  6.5 1.7 pad_maximum_fusion
  8.2 0.0 all-gather.2.cloned.1.call-update
  8.3 0.8 fusion.65
  9.0 144.4 %all-gather.2.cloned.1.call-done = bf16[4,2048,256]{2,1,0:T(8,128)(2,1)} async-done(((bf16[4,64,256]{2,1,0:T(8,128)(2,1)}), bf16[4,2048,256]{2,1,0:T(8,128)(2,1)}) %all-gather.2.cloned.1.call-update) | async-done | bytes 4194320 | tf_op jit(solution)/shard_map/all_gather | solution.py:13
  153.4 4.1 %fusion.31 = f32[512,2048]{1,0:T(8,128)} fusion(bf16[2,2048,256]{2,1,0:T(8,128)(2,1)} %param.5, bf16[4,2048,256]{2,1,0:T(8,128)(2,1)} %all-gather.2.cloned.1.call-done), kind=kOutput, calls=%fused_computation.38 | convolution fusion | flops 536870912 | bytes 5505024 | tf_op jit(solution)/shard_map/sp,tp->st/dot_general | solution.py:32
  157.5 0.0 copy-done
  157.5 3.6 %fusion.29 = f32[512,2048]{1,0:T(8,128)} fusion(bf16[2,2048,256]{2,1,0:T(8,128)(2,1)S(1)} %copy-done, bf16[4,2048,256]{2,1,0:T(8,128)(2,1)} %all-gather.2.cloned.1.call-done), kind=kOutput, calls=%fused_computation.36 | convolution fusion | flops 536870912 | bytes 5505024 | tf_op jit(solution)/shard_map/sp,tp->st/dot_general | solution.py:32
  161.2 3.6 %fusion.27 = f32[512,2048]{1,0:T(8,128)} fusion(bf16[2,2048,256]{2,1,0:T(8,128)(2,1)S(1)} %copy-done, bf16[4,2048,256]{2,1,0:T(8,128)(2,1)} %all-gather.2.cloned.1.call-done), kind=kOutput, calls=%fused_computation.34 | convolution fusion | flops 536870912 | bytes 5505024 | tf_op jit(solution)/shard_map/sp,tp->st/dot_general | solution.py:32
  164.8 3.6 %fusion.25 = f32[512,2048]{1,0:T(8,128)} fusion(bf16[2,2048,256]{2,1,0:T(8,128)(2,1)S(1)} %copy-done, bf16[4,2048,256]{2,1,0:T(8,128)(2,1)} %all-gather.2.cloned.1.call-done), kind=kOutput, calls=%fused_computation.32 | convolution fusion | flops 536870912 | bytes 5505024 | tf_op jit(solution)/shard_map/sp,tp->st/dot_general | solution.py:32
  168.4 3.7 %fusion.15 = f32[512,2048]{1,0:T(8,128)} fusion(bf16[2,2048,256]{2,1,0:T(8,128)(2,1)S(1)} %copy-done, bf16[4,2048,256]{2,1,0:T(8,128)(2,1)} %all-gather.2.cloned.1.call-done), kind=kOutput, calls=%fused_computation.26 | convolution fusion | flops 536870912 | bytes 5505024 | tf_op jit(solution)/shard_map/sp,tp->st/dot_general | solution.py:32
  172.1 3.6 %fusion.13 = f32[512,2048]{1,0:T(8,128)} fusion(bf16[2,2048,256]{2,1,0:T(8,128)(2,1)S(1)} %copy-done, bf16[4,2048,256]{2,1,0:T(8,128)(2,1)} %all-gather.2.cloned.1.call-done), kind=kOutput, calls=%fused_computation.24 | convolution fusion | flops 536870912 | bytes 5505024 | tf_op jit(solution)/shard_map/sp,tp->st/dot_general | solution.py:32
  175.7 3.6 %fusion.11 = f32[512,2048]{1,0:T(8,128)} fusion(bf16[2,2048,256]{2,1,0:T(8,128)(2,1)S(1)} %copy-done, bf16[4,2048,256]{2,1,0:T(8,128)(2,1)} %all-gather.2.cloned.1.call-done), kind=kOutput, calls=%fused_computation.22 | convolution fusion | flops 536870912 | bytes 5505024 | tf_op jit(solution)/shard_map/sp,tp->st/dot_general | solution.py:32
  179.4 3.7 %fusion.9 = f32[512,2048]{1,0:T(8,128)} fusion(bf16[2,2048,256]{2,1,0:T(8,128)(2,1)S(1)} %copy-done, bf16[4,2048,256]{2,1,0:T(8,128)(2,1)} %all-gather.2.cloned.1.call-done), kind=kOutput, calls=%fused_computation.20 | convolution fusion | flops 536870912 | bytes 5505024 | tf_op jit(solution)/shard_map/sp,tp->st/dot_general | solution.py:32
  183.0 0.0 copy-start.1
  183.0 3.8 %fusion = f32[128,2048]{1,0:T(8,128)S(1)} fusion(f32[512,2048]{1,0:T(8,128)} %fusion.31, bf16[2,2048,256]{2,1,0:T(8,128)(2,1)} %param.6, bf16[4,2048,256]{2,1,0:T(8,128)(2,1)} %all-gather.2.cloned.1.call-done, s32[512]{0:T(512)S(1)} %get-tuple-element.7), kind=kOutput, calls=%fused_computation.15 | convolution fusion | flops 807469056 | bytes 6555648 | tf_op jit(solution)/shard_map/dot_general | solution.py:59
  186.8 0.0 copy-done.1
  186.8 4.3 %convolution_add_fusion.6 = f32[128,2048]{1,0:T(8,128)} fusion(f32[128,2048]{1,0:T(8,128)S(1)} %fusion, f32[512,2048]{1,0:T(8,128)} %fusion.29, bf16[2,2048,256]{2,1,0:T(8,128)(2,1)S(1)} %copy-done.1, bf16[4,2048,256]{2,1,0:T(8,128)(2,1)} %all-gather.2.cloned.1.call-done, s32[512]{0:T(512)S(1)} %get-tuple-element.6), kind=kOutput, calls=%fused_computation.14 | convolution fusion | flops 807731200 | bytes 7604224 | tf_op jit(solution)/shard_map/dot_general | solution.py:59
  191.1 3.6 %convolution_add_fusion.5 = f32[128,2048]{1,0:T(8,128)S(1)} fusion(f32[128,2048]{1,0:T(8,128)} %convolution_add_fusion.6, f32[512,2048]{1,0:T(8,128)} %fusion.27, bf16[2,2048,256]{2,1,0:T(8,128)(2,1)S(1)} %copy-done.1, bf16[4,2048,256]{2,1,0:T(8,128)(2,1)} %all-gather.2.cloned.1.call-done, s32[512]{0:T(512)S(1)} %get-tuple-element.8), kind=kOutput, calls=%fused_computation.13 | convolution fusion | flops 807731200 | bytes 7604224 | tf_op jit(solution)/shard_map/dot_general | solution.py:59
  194.7 4.4 %convolution_add_fusion.4 = f32[128,2048]{1,0:T(8,128)} fusion(f32[128,2048]{1,0:T(8,128)S(1)} %convolution_add_fusion.5, f32[512,2048]{1,0:T(8,128)} %fusion.25, bf16[2,2048,256]{2,1,0:T(8,128)(2,1)S(1)} %copy-done.1, bf16[4,2048,256]{2,1,0:T(8,128)(2,1)} %all-gather.2.cloned.1.call-done, s32[512]{0:T(512)S(1)} %get-tuple-element.5), kind=kOutput, calls=%fused_computation.12 | convolution fusion | flops 807731200 | bytes 7604224 | tf_op jit(solution)/shard_map/dot_general | solution.py:59
  199.1 3.6 %convolution_add_fusion.3 = f32[128,2048]{1,0:T(8,128)S(1)} fusion(f32[128,2048]{1,0:T(8,128)} %convolution_add_fusion.4, f32[512,2048]{1,0:T(8,128)} %fusion.15, bf16[2,2048,256]{2,1,0:T(8,128)(2,1)S(1)} %copy-done.1, bf16[4,2048,256]{2,1,0:T(8,128)(2,1)} %all-gather.2.cloned.1.call-done, s32[512]{0:T(512)S(1)} %get-tuple-element.7), kind=kOutput, calls=%fused_computation.11 | convolution fusion | flops 807731200 | bytes 7604224 | tf_op jit(solution)/shard_map/dot_general | solution.py:59
  202.7 4.3 %convolution_add_fusion.2 = f32[128,2048]{1,0:T(8,128)} fusion(f32[128,2048]{1,0:T(8,128)S(1)} %convolution_add_fusion.3, f32[512,2048]{1,0:T(8,128)} %fusion.13, bf16[2,2048,256]{2,1,0:T(8,128)(2,1)S(1)} %copy-done.1, bf16[4,2048,256]{2,1,0:T(8,128)(2,1)} %all-gather.2.cloned.1.call-done, s32[512]{0:T(512)S(1)} %get-tuple-element.6), kind=kOutput, calls=%fused_computation.10 | convolution fusion | flops 807731200 | bytes 7604224 | tf_op jit(solution)/shard_map/dot_general | solution.py:59
  207.0 4.6 %convolution_add_fusion.1 = f32[128,2048]{1,0:T(8,128)} fusion(f32[128,2048]{1,0:T(8,128)} %convolution_add_fusion.2, f32[512,2048]{1,0:T(8,128)} %fusion.11, bf16[2,2048,256]{2,1,0:T(8,128)(2,1)S(1)} %copy-done.1, bf16[4,2048,256]{2,1,0:T(8,128)(2,1)} %all-gather.2.cloned.1.call-done, s32[512]{0:T(512)S(1)} %get-tuple-element.8), kind=kOutput, calls=%fused_computation.9 | convolution fusion | flops 807731200 | bytes 7604224 | tf_op jit(solution)/shard_map/dot_general | solution.py:59
  211.6 3.6 %convolution_add_fusion = f32[128,2048]{1,0:T(8,128)S(1)} fusion(f32[128,2048]{1,0:T(8,128)} %convolution_add_fusion.1, f32[512,2048]{1,0:T(8,128)} %fusion.9, bf16[2,2048,256]{2,1,0:T(8,128)(2,1)S(1)} %copy-done.1, bf16[4,2048,256]{2,1,0:T(8,128)(2,1)} %all-gather.2.cloned.1.call-done, s32[512]{0:T(512)S(1)} %get-tuple-element.5), kind=kOutput, calls=%fused_computation.8 | convolution fusion | flops 807731200 | bytes 7604224 | tf_op jit(solution)/shard_map/dot_general | solution.py:59
  215.2 50.1 %all_to_all.5 = f32[8,16,2048]{2,1,0:T(8,128)S(1)} all-to-all(f32[8,16,2048]{2,1,0:T(8,128)S(1)} %bitcast.101), channel_id=1, replica_groups=mesh['layer'=8,'tok'=32] {'layer'}, dimensions={0} | all-to-all | bytes 2097152 | tf_op jit(solution)/shard_map/all_to_all | solution.py:27
  265.3 0.7 reduce_sum.9
Async XLA Ops:
  6.5 151.0 %copy-start = (bf16[2,2048,256]{2,1,0:T(8,128)(2,1)S(1)}, bf16[2,2048,256]{2,1,0:T(8,128)(2,1)}, u32[]{:S(2)}) copy-start(bf16[2,2048,256]{2,1,0:T(8,128)(2,1)} %param.5) | copy-start | bytes 6291460
  6.5 146.9 %all-gather.2.cloned.1.call-start = ((), (), s32[]{:S(2)}) async-start(), calls=%async_computation.1 | async-start | bytes 4325376 | tf_op jit(solution)/shard_map/all_gather | solution.py:13
  183.0 3.8 %copy-start.1 = (bf16[2,2048,256]{2,1,0:T(8,128)(2,1)S(1)}, bf16[2,2048,256]{2,1,0:T(8,128)(2,1)}, u32[]{:S(2)}) copy-start(bf16[2,2048,256]{2,1,0:T(8,128)(2,1)} %param.6) | copy-start | bytes 6291460
Sparse Core Ops, SparseCore 0:
  9.2 144.2 all-gather.1
where the time goes:
time: 273 us
  waiting for transfers between devices  144 us (53%)
  matrix products  61.7 us (23%)
  blocking collectives  50.1 us (18%)
  between operations  13.4 us (5%)
    all_gather x1, waiting for transfers between devices, sent_together(): result, at, done = (lax.all_gather(both, axis, axis=dim, tiled=True), 0, [])  144 us
    all_to_all x1, blocking collectives, sum_at_owner(): tiles = lax.all_to_all(cut_along(value, dim, peers), axis, 0, 0, tiled=True)  50.1 us
    dot_general x8, matrix products, on_device(): jnp.dot(select, product, preferred_element_type=jnp.float32)  32.1 us
    dot_general x8, matrix products, gram_product(): jnp.einsum('sp,tp->st', test_a, train_a, preferred_element_type=jnp.float32)  29.6 us
  transfers between devices with their start and end apart: 1, of which 1 were waited for; matrix products, arithmetic and copies ran while one was open for 0% of the time, Pallas kernels for 0%

commit v1 on v0

v1 whole, which is shorter than its diff:
```python
import functools

import jax
import jax.numpy as jnp
from jax import lax
from jax.experimental import pallas as pl
from jax.experimental.pallas import tpu as pltpu
from jax.sharding import PartitionSpec as P

Q = 128
NX, NZ, NY = 4, 2, 4
OFFSETS = (0, -1, 1, 2)
BF16 = jnp.bfloat16
F32 = jnp.float32


def tok_moves(dx, dz, dy):
    moves = []
    for x in range(NX):
        for z in range(NZ):
            for y in range(NY):
                there = ((x + dx) % NX) * NZ * NY + ((z + dz) % NZ) * NY + (y + dy) % NY
                moves.append((x * NZ * NY + z * NY + y, there))
    return moves


def ring_gather(pair, forward, back):
    a, g = pair
    a_prev = lax.ppermute(a, "tok", forward)
    g_next = lax.ppermute(g, "tok", back)
    a_next = lax.ppermute(a, "tok", back)
    g_prev = lax.ppermute(g, "tok", forward)
    a_far = lax.ppermute(a_prev, "tok", forward)
    g_far = lax.ppermute(g_next, "tok", back)
    return [(a, g), (a_prev, g_prev), (a_next, g_next), (a_far, g_far)]


def chunk_kernel(last, n_pairs, ids_ref, labels_ref, ta_ref, tg_ref, *refs):
    tests = refs[: 2 * n_pairs]
    rest = refs[2 * n_pairs :]
    sel = (labels_ref[...] == ids_ref[0:1, :]).astype(F32).astype(BF16)
    if last:
        acc_ref, keep_ref, send_ref = rest
        acc = acc_ref[...]
    elif len(rest) == 2:
        acc_ref, out_ref = rest
        acc = acc_ref[...]
    else:
        (out_ref,) = rest
        acc = None
    nt = (((1,), (1,)), ((), ()))
    for layer in range(2):
        ta = ta_ref[layer]
        tg = tg_ref[layer]
        for n in range(n_pairs):
            a = tests[2 * n][:, layer].reshape(-1, 256)
            g = tests[2 * n + 1][:, layer].reshape(-1, 256)
            rows = a.shape[0]
            pa = lax.dot_general(a, ta, nt, preferred_element_type=F32)
            pg = lax.dot_general(g, tg, nt, preferred_element_type=F32)
            prod = (pa * pg).astype(BF16)
            part = jnp.dot(
                sel[:, n * rows : (n + 1) * rows], prod, preferred_element_type=F32
            )
            acc = part if acc is None else acc + part
    if last:
        keep_ref[...] = acc[: Q // 2]
        send_ref[...] = acc[Q // 2 :].astype(BF16)
    else:
        out_ref[...] = acc


def chunk(ids, labels, train_act, train_grad, pairs, acc, last):
    rows = train_act.shape[1]
    tile = 512
    steps = rows // tile
    tests = [t for pair in pairs for t in pair]
    whole = lambda a: pl.BlockSpec(a.shape, lambda i, nd=a.ndim: (0,) * nd)
    column = lambda n: pl.BlockSpec((n, tile), lambda i: (0, i))
    train = pl.BlockSpec((2, tile, 256), lambda i: (0, i, 0))
    args = [ids, labels, train_act, train_grad, *tests]
    in_specs = [whole(ids), whole(labels), train, train] + [whole(t) for t in tests]
    if acc is not None:
        args.append(acc)
        in_specs.append(column(Q))
    if last:
        out_shape = (
            jax.ShapeDtypeStruct((Q // 2, rows), F32),
            jax.ShapeDtypeStruct((Q // 2, rows), BF16),
        )
        out_specs = (column(Q // 2), column(Q // 2))
    else:
        out_shape = jax.ShapeDtypeStruct((Q, rows), F32)
        out_specs = column(Q)
    s_rows = sum(p[0].shape[0] * 64 for p in pairs)
    return pl.pallas_call(
        functools.partial(chunk_kernel, last, len(pairs)),
        grid=(steps,),
        in_specs=in_specs,
        out_specs=out_specs,
        out_shape=out_shape,
        compiler_params=pltpu.CompilerParams(vmem_limit_bytes=32 * 1024 * 1024),
        cost_estimate=pl.CostEstimate(
            flops=2 * 2 * s_rows * rows * (2 * 256 + Q),
            bytes_accessed=4 * 1024 * 1024 + 2 * Q * rows * 4,
            transcendentals=0,
        ),
    )(*args)


def merge_kernel(keep_ref, got_ref, own_ref, *send_refs):
    own_ref[...] = keep_ref[0:16] + got_ref[0:16].astype(F32)
    for k, ref in enumerate(send_refs, 1):
        rows = slice(16 * k, 16 * k + 16)
        ref[...] = (keep_ref[rows] + got_ref[rows].astype(F32)).astype(BF16)


def merge(keep, got):
    rows = keep.shape[1]
    send = jax.ShapeDtypeStruct((16, rows), BF16)
    return pl.pallas_call(
        merge_kernel,
        out_shape=(jax.ShapeDtypeStruct((16, rows), F32), send, send, send),
    )(keep, got)


def on_device(train_act, train_grad, test_act, test_grad, segment_ids):
    tok = lax.axis_index("tok")
    layer = lax.axis_index("layer")
    x, z, y = tok // 8, (tok // 4) % 2, tok % 4
    core, z_hi = layer % 2, layer // 2

    x_fwd, x_back = tok_moves(1, 0, 0), tok_moves(-1, 0, 0)
    y_fwd, y_back = tok_moves(0, 0, 1), tok_moves(0, 0, -1)
    across = tok_moves(0, 1, 0)

    ids = segment_ids.reshape(NX, NZ, NY, 64)
    ids = lax.dynamic_slice_in_dim(jnp.concatenate([ids, ids], 0), x, NX, 0)
    ids = lax.dynamic_slice_in_dim(jnp.concatenate([ids, ids], 1), z, NZ, 1)
    ids = lax.dynamic_slice_in_dim(jnp.concatenate([ids, ids], 2), y, NY, 2)
    order = [o % 4 for o in OFFSETS]
    reorder = lambda v, d: jnp.concatenate([lax.slice_in_dim(v, o, o + 1, axis=d) for o in order], d)
    ids = reorder(reorder(ids, 0), 2)
    first = ids[:, 0].reshape(4, 1, 256)
    second = jnp.swapaxes(ids[:, 1], 0, 1).reshape(4, 1, 256)
    chunk_ids = jnp.concatenate([first, second], 2)

    r = lax.broadcasted_iota(jnp.int32, (Q, 1), 0)
    labels = ((z_hi + (r % 64) // 16) % 4) * 32 + (core ^ (r // 64)) * 16 + r % 16

    own = (test_act, test_grad)
    other = tuple(lax.ppermute(t, "tok", across) for t in own)

    def stream(pair, first_dim, second_dim):
        near = ring_gather(pair, *first_dim)
        whole = tuple(jnp.stack([b[k] for b in near]) for k in range(2))
        return ring_gather(whole, *second_dim)

    one = stream(own, (y_fwd, y_back), (x_fwd, x_back))
    two = stream(other, (x_fwd, x_back), (y_fwd, y_back))

    acc = None
    for k in range(4):
        acc = chunk(
            chunk_ids[k], labels, train_act, train_grad, (one[k], two[k]), acc, k == 3
        )
    keep, send = acc

    swap = [(i, i ^ 1) for i in range(8)]
    got = lax.ppermute(send, "layer", swap)
    own_sum, *to_send = merge(keep, got)
    for k, part in enumerate(to_send, 1):
        moved = lax.ppermute(part, "layer", [(i, (i + 2 * k) % 8) for i in range(8)])
        own_sum = own_sum + moved.astype(F32)
    return own_sum


def solution(mesh):
    placed = (
        P("layer", "tok", None),
        P("layer", "tok", None),
        P("layer", "tok", None),
        P("layer", "tok", None),
        P(),
    )
    return jax.shard_map(
        on_device, mesh=mesh, in_specs=placed, out_specs=P("layer", "tok"), check_vma=False
    )
```

time: 273 us -> 95.9 us (0.35)
  waiting for transfers between devices: 144 us -> 12.7 us
  matrix products: 61.7 us -> 0 us
  blocking collectives: 50.1 us -> 0 us
  starting transfers between devices: 0.01 us -> 47.1 us
  Pallas kernels: 0 us -> 27.9 us
  between operations: 13.4 us -> 0.26 us
  local copies, waits for them, and re-layouts: 0.78 us -> 4.05 us
    all_gather x1 -> x0, waiting for transfers between devices: 144 us -> none  [sent_together(): result, at, done = (lax.all_gather(both, axis, axis=dim, tiled=True), 0, [])]
    dot_general x16 -> x0, matrix products: 61.7 us -> none  [the longest x8 32.1 us: on_device(): jnp.dot(select, product, preferred_element_type=jnp.float32)]
    all_to_all x1 -> x0, blocking collectives: 50.1 us -> none  [sum_at_owner(): tiles = lax.all_to_all(cut_along(value, dim, peers), axis, 0, 0, tiled=True)]
    ppermute x0 -> x30, starting transfers between devices: none -> 47.1 us  [the longest x3 10.5 us: on_device(): lax.ppermute(part, 'layer', [(i, (i + 2 * k) % 8) for i in range(8)])]
    pallas_call x0 -> x5, Pallas kernels: none -> 27.9 us  [the longest x4 26.1 us: chunk(): pl.pallas_call(functools.partial(chunk_kernel, last, len(pairs)), grid=(s...]
    ppermute x0 -> x30, waiting for transfers between devices: none -> 12.7 us  [the longest x4 5.28 us: ring_gather(): a_far = lax.ppermute(a_prev, 'tok', forward)]
    unnamed x4 -> x9, local copies, waits for them, and re-layouts: 0.01 us -> 3.08 us
  transfers between devices with their start and end apart: 1 -> 30, of which waited for: 1 -> 9; matrix products, arithmetic and copies ran while one was open for 0% -> 3% of each run, Pallas kernels for 0% -> 20%
where the time goes in v1:
time: 95.9 us; the launch traced here: 95.6 us
  starting transfers between devices  47.1 us (49%)
  Pallas kernels  27.9 us (29%)
  waiting for transfers between devices  12.7 us (13%)
  local copies, waits for them, and re-layouts  4.05 us (4%)
  other arithmetic  3.57 us (4%)
    pallas_call x4, Pallas kernels, chunk(): pl.pallas_call(functools.partial(chunk_kernel, last, len(pairs)), grid=(s...  26.1 us
    ppermute x3, starting transfers between devices, on_device(): lax.ppermute(part, 'layer', [(i, (i + 2 * k) % 8) for i in range(8)])  10.5 us
    ppermute x4, starting transfers between devices, ring_gather(): a_next = lax.ppermute(a, 'tok', back)  7.72 us
    ppermute x4, starting transfers between devices, ring_gather(): g_far = lax.ppermute(g_next, 'tok', back)  7.11 us
    ppermute x4, starting transfers between devices, ring_gather(): g_next = lax.ppermute(g, 'tok', back)  6.43 us
    ppermute x1, starting transfers between devices, on_device(): got = lax.ppermute(send, 'layer', swap)  5.8 us
    ppermute x4, waiting for transfers between devices, ring_gather(): a_far = lax.ppermute(a_prev, 'tok', forward)  5.28 us
    ppermute x3, waiting for transfers between devices, on_device(): lax.ppermute(part, 'layer', [(i, (i + 2 * k) % 8) for i in range(8)])  4.86 us
  transfers between devices with their start and end apart: 30, of which 9 were waited for; matrix products, arithmetic and copies ran while one was open for 3% of the time, Pallas kernels for 20%

profile of v1, /device:TPU:1, one launch (start us, length us, event | category | flops | bytes accessed | tf_op | source)
XLA Modules:
  0.0 95.6 jit_solution(14567995737501962014)
XLA Ops:
  0.0 2.5 %collective-permute-start.10 = (bf16[2,64,256]{2,1,0:T(8,128)(2,1)}, bf16[2,64,256]{2,1,0:T(8,128)(2,1)S(1)}, u32[]{:S(2)}, u32[]{:S(2)}) collective-permute-start(bf16[2,64,256]{2,1,0:T(8,128)(2,1)} %param.7), channel_id=1, source_target_pairs={{0,4},{1,5},{2,6},{3,7},{4,0},{5,1},{6,2},{7,3},{8,12},{9,13},{10,... | collective-permute-start | bytes 196616 | tf_op jit(solution)/shard_map/ppermute | solution.py:152
  2.5 1.3 %collective-permute-start = (bf16[2,64,256]{2,1,0:T(8,128)(2,1)}, bf16[2,64,256]{2,1,0:T(8,128)(2,1)S(1)}, u32[]{:S(2)}, u32[]{:S(2)}) collective-permute-start(bf16[2,64,256]{2,1,0:T(8,128)(2,1)} %param.7), channel_id=1, source_target_pairs={{0,1},{1,2},{2,3},{3,0},{4,5},{5,6},{6,7},{7,4},{8,9},{9,10},{10,1... | collective-permute-start | bytes 196616 | tf_op jit(solution)/shard_map/ppermute | solution.py:29
  3.8 1.4 %collective-permute-start.1 = (bf16[2,64,256]{2,1,0:T(8,128)(2,1)}, bf16[2,64,256]{2,1,0:T(8,128)(2,1)S(1)}, u32[]{:S(2)}, u32[]{:S(2)}) collective-permute-start(bf16[2,64,256]{2,1,0:T(8,128)(2,1)} %param.7), channel_id=1, source_target_pairs={{0,3},{1,0},{2,1},{3,2},{4,7},{5,4},{6,5},{7,6},{8,11},{9,8},{10,9... | collective-permute-start | bytes 196616 | tf_op jit(solution)/shard_map/ppermute | solution.py:31
  5.4 1.4 %collective-permute-start.6 = (bf16[2,64,256]{2,1,0:T(8,128)(2,1)}, bf16[2,64,256]{2,1,0:T(8,128)(2,1)S(1)}, u32[]{:S(2)}, u32[]{:S(2)}) collective-permute-start(bf16[2,64,256]{2,1,0:T(8,128)(2,1)} %param.8), channel_id=1, source_target_pairs={{0,3},{1,0},{2,1},{3,2},{4,7},{5,4},{6,5},{7,6},{8,11},{9,8},{10,9... | collective-permute-start | bytes 196616 | tf_op jit(solution)/shard_map/ppermute | solution.py:30
  8.8 2.5 %collective-permute-start.18 = (bf16[2,64,256]{2,1,0:T(8,128)(2,1)S(1)}, bf16[2,64,256]{2,1,0:T(8,128)(2,1)S(1)}, u32[]{:S(2)}, u32[]{:S(2)}) collective-permute-start(bf16[2,64,256]{2,1,0:T(8,128)(2,1)S(1)} %collective-permute-done.16), channel_id=1, source_target_pairs={{0,24},{1,25},{2,26},{3,27},{4,28},{5,29},{6,30},{7,31},{8,0},{9,1... | collective-permute-start | bytes 196616 | tf_op jit(solution)/shard_map/ppermute | solution.py:30
  12.2 1.2 %collective-permute-start.7 = (bf16[2,64,256]{2,1,0:T(8,128)(2,1)S(1)}, bf16[2,64,256]{2,1,0:T(8,128)(2,1)S(1)}, u32[]{:S(2)}, u32[]{:S(2)}) collective-permute-start(bf16[2,64,256]{2,1,0:T(8,128)(2,1)S(1)} %collective-permute-done.6), channel_id=1, source_target_pairs={{0,3},{1,0},{2,1},{3,2},{4,7},{5,4},{6,5},{7,6},{8,11},{9,8},{10,9... | collective-permute-start | bytes 196616 | tf_op jit(solution)/shard_map/ppermute | solution.py:34
  13.4 0.9 pad_maximum_fusion.refs_0_
  14.3 1.3 %collective-permute-start.3 = (bf16[4,2,64,256]{3,2,1,0:T(8,128)(2,1)S(1)}, bf16[4,2,64,256]{3,2,1,0:T(8,128)(2,1)S(1)}, u32[]{:S(2)}, u32[]{:S(2)}) collective-permute-start(bf16[4,2,64,256]{3,2,1,0:T(8,128)(2,1)S(1)} %pad_maximum_fusion.refs_0_), channel_id=1, source_target_pairs={{0,8},{1,9},{2,10},{3,11},{4,12},{5,13},{6,14},{7,15},{8,16},{9,17... | collective-permute-start | bytes 786440 | tf_op jit(solution)/shard_map/ppermute | solution.py:29
  15.7 0.9 pad_maximum_fusion.1.refs_1_
  16.5 2.1 %collective-permute-start.24 = (bf16[4,2,64,256]{3,2,1,0:T(8,128)(2,1)S(1)}, bf16[4,2,64,256]{3,2,1,0:T(8,128)(2,1)S(1)}, u32[]{:S(2)}, u32[]{:S(2)}) collective-permute-start(bf16[4,2,64,256]{3,2,1,0:T(8,128)(2,1)S(1)} %pad_maximum_fusion.1.refs_1_), channel_id=1, source_target_pairs={{0,8},{1,9},{2,10},{3,11},{4,12},{5,13},{6,14},{7,15},{8,16},{9,17... | collective-permute-start | bytes 786440 | tf_op jit(solution)/shard_map/ppermute | solution.py:32
  19.3 1.3 %collective-permute-start.12 = (bf16[2,64,256]{2,1,0:T(8,128)(2,1)S(1)}, bf16[2,64,256]{2,1,0:T(8,128)(2,1)S(1)}, u32[]{:S(2)}, u32[]{:S(2)}) collective-permute-start(bf16[2,64,256]{2,1,0:T(8,128)(2,1)S(1)} %collective-permute-done.10), channel_id=1, source_target_pairs={{0,24},{1,25},{2,26},{3,27},{4,28},{5,29},{6,30},{7,31},{8,0},{9,1... | collective-permute-start | bytes 196616 | tf_op jit(solution)/shard_map/ppermute | solution.py:31
  22.8 2.2 %collective-permute-start.22 = (bf16[4,2,64,256]{3,2,1,0:T(8,128)(2,1)S(1)}, bf16[4,2,64,256]{3,2,1,0:T(8,128)(2,1)S(1)}, u32[]{:S(2)}, u32[]{:S(2)}) collective-permute-start(bf16[4,2,64,256]{3,2,1,0:T(8,128)(2,1)S(1)} %pad_maximum_fusion.refs_0_), channel_id=1, source_target_pairs={{0,24},{1,25},{2,26},{3,27},{4,28},{5,29},{6,30},{7,31},{8,0},{9,1... | collective-permute-start | bytes 786440 | tf_op jit(solution)/shard_map/ppermute | solution.py:31
  25.0 4.5 %collective-permute-done.13 = bf16[2,64,256]{2,1,0:T(8,128)(2,1)S(1)} collective-permute-done((bf16[2,64,256]{2,1,0:T(8,128)(2,1)S(1)}, bf16[2,64,256]{2,1,0:T(8,128)(2,1)S(1)}, u32[]{:S(2)}, u32[]{:S(2)}) %collective-permute-start.13) | collective-permute-done | bytes 65568 | tf_op jit(solution)/shard_map/ppermute | solution.py:33
  30.3 2.0 %collective-permute-start.20 = (bf16[4,2,64,256]{3,2,1,0:T(8,128)(2,1)S(1)}, bf16[4,2,64,256]{3,2,1,0:T(8,128)(2,1)S(1)}, u32[]{:S(2)}, u32[]{:S(2)}) collective-permute-start(bf16[4,2,64,256]{3,2,1,0:T(8,128)(2,1)S(1)} %pad_maximum_fusion.3.refs_3_), channel_id=1, source_target_pairs={{0,3},{1,0},{2,1},{3,2},{4,7},{5,4},{6,5},{7,6},{8,11},{9,8},{10,9... | collective-permute-start | bytes 786440 | tf_op jit(solution)/shard_map/ppermute | solution.py:30
  32.4 2.8 %collective-permute-start.23 = (bf16[4,2,64,256]{3,2,1,0:T(8,128)(2,1)S(1)}, bf16[4,2,64,256]{3,2,1,0:T(8,128)(2,1)S(1)}, u32[]{:S(2)}, u32[]{:S(2)}) collective-permute-start(bf16[4,2,64,256]{3,2,1,0:T(8,128)(2,1)S(1)} %pad_maximum_fusion.2.refs_2_), channel_id=1, source_target_pairs={{0,3},{1,0},{2,1},{3,2},{4,7},{5,4},{6,5},{7,6},{8,11},{9,8},{10,9... | collective-permute-start | bytes 786440 | tf_op jit(solution)/shard_map/ppermute | solution.py:31
  35.2 1.6 %copy-done.2 = bf16[2,2048,256]{2,1,0:T(8,128)(2,1)S(1)} copy-done((bf16[2,2048,256]{2,1,0:T(8,128)(2,1)S(1)}, bf16[2,2048,256]{2,1,0:T(8,128)(2,1)}, u32[]{:S(2)}) %copy-start.2) | copy-done | bytes 2097176
  36.8 5.9 %shard_map.55.refs_4_ = f32[128,2048]{1,0:T(8,128)S(1)} custom-call(s32[1,512]{1,0:T(1,128)S(1)} %get-tuple-element.23.ids_ref, s32[128,1]{1,0:T(8,128)S(1)} %fusion.5.labels_ref, bf16[2,2048,256]{2,1,0:T(8,128)(2,1)S(1)} %copy-done.1, bf16[2,2048,256]{2,1,0:T(8,128)(2,1)S(1)} %copy-done.2, bf16[4,2,64,256]{3,2,1,0:T(8,128)(2,1)S(1)} %pad_maximum_fusion.refs_0_, ...), custom_call_target="tpu_custom_call" | custom-call | flops 2684354560 | bytes 6291456 | tf_op jit(solution)/shard_map/pallas_call | solution.py:96
  42.8 2.7 %collective-permute-start.9 = (bf16[4,2,64,256]{3,2,1,0:T(8,128)(2,1)S(1)}, bf16[4,2,64,256]{3,2,1,0:T(8,128)(2,1)S(1)}, u32[]{:S(2)}, u32[]{:S(2)}) collective-permute-start(bf16[4,2,64,256]{3,2,1,0:T(8,128)(2,1)S(1)} %collective-permute-done.8.refs_1_), channel_id=1, source_target_pairs={{0,24},{1,25},{2,26},{3,27},{4,28},{5,29},{6,30},{7,31},{8,0},{9,1... | collective-permute-start | bytes 786440 | tf_op jit(solution)/shard_map/ppermute | solution.py:34
  45.5 2.7 %collective-permute-start.21 = (bf16[4,2,64,256]{3,2,1,0:T(8,128)(2,1)S(1)}, bf16[4,2,64,256]{3,2,1,0:T(8,128)(2,1)S(1)}, u32[]{:S(2)}, u32[]{:S(2)}) collective-permute-start(bf16[4,2,64,256]{3,2,1,0:T(8,128)(2,1)S(1)} %collective-permute-done.20.refs_3_), channel_id=1, source_target_pairs={{0,3},{1,0},{2,1},{3,2},{4,7},{5,4},{6,5},{7,6},{8,11},{9,8},{10,9... | collective-permute-start | bytes 786440 | tf_op jit(solution)/shard_map/ppermute | solution.py:34
  48.1 6.7 %shard_map.56.refs_4_ = f32[128,2048]{1,0:T(8,128)S(1)} custom-call(s32[1,512]{1,0:T(1,128)S(1)} %get-tuple-element.24.ids_ref, s32[128,1]{1,0:T(8,128)S(1)} %fusion.5.labels_ref, bf16[2,2048,256]{2,1,0:T(8,128)(2,1)S(1)} %copy-done.1, bf16[2,2048,256]{2,1,0:T(8,128)(2,1)S(1)} %copy-done.2, bf16[4,2,64,256]{3,2,1,0:T(8,128)(2,1)S(1)} %collective-permute-done.3.refs_0_, ...), custom_call_target="tpu_custom_call" | custom-call | flops 2684354560 | bytes 6291456 | tf_op jit(solution)/shard_map/pallas_call | solution.py:96
  54.9 6.7 %shard_map.57.refs_4_ = f32[128,2048]{1,0:T(8,128)S(1)} custom-call(s32[1,512]{1,0:T(1,128)S(1)} %get-tuple-element.25.ids_ref, s32[128,1]{1,0:T(8,128)S(1)} %fusion.5.labels_ref, bf16[2,2048,256]{2,1,0:T(8,128)(2,1)S(1)} %copy-done.1, bf16[2,2048,256]{2,1,0:T(8,128)(2,1)S(1)} %copy-done.2, bf16[4,2,64,256]{3,2,1,0:T(8,128)(2,1)S(1)} %collective-permute-done.22.refs_0_, ...), custom_call_target="tpu_custom_call" | custom-call | flops 2684354560 | bytes 6291456 | tf_op jit(solution)/shard_map/pallas_call | solution.py:96
  61.7 6.7 %shard_map.58 = (f32[64,2048]{1,0:T(8,128)S(1)}, bf16[64,2048]{1,0:T(8,128)(2,1)S(1)}) custom-call(s32[1,512]{1,0:T(1,128)S(1)} %get-tuple-element.26.ids_ref, s32[128,1]{1,0:T(8,128)S(1)} %fusion.5.labels_ref, bf16[2,2048,256]{2,1,0:T(8,128)(2,1)S(1)} %copy-done.1, bf16[2,2048,256]{2,1,0:T(8,128)(2,1)S(1)} %copy-done.2, ...), custom_call_target="tpu_custom_call" | custom-call | flops 2684354560 | bytes 6291456 | tf_op jit(solution)/shard_map/pallas_call | solution.py:96
  68.4 0.8 copy-done
  69.2 5.8 %collective-permute-start.26 = (bf16[64,2048]{1,0:T(8,128)(2,1)S(1)}, bf16[64,2048]{1,0:T(8,128)(2,1)S(1)}, u32[]{:S(2)}, u32[]{:S(2)}) collective-permute-start(bf16[64,2048]{1,0:T(8,128)(2,1)S(1)} %get-tuple-element.12), channel_id=1, source_target_pairs={{0,32},{32,0},{64,96},{96,64},{128,160},{160,128},{192,224},{224,1... | collective-permute-start | bytes 786440 | tf_op jit(solution)/shard_map/ppermute | solution.py:170
  75.0 1.2 %collective-permute-done.26.got_ref = bf16[64,2048]{1,0:T(8,128)(2,1)S(1)} collective-permute-done((bf16[64,2048]{1,0:T(8,128)(2,1)S(1)}, bf16[64,2048]{1,0:T(8,128)(2,1)S(1)}, u32[]{:S(2)}, u32[]{:S(2)}) %collective-permute-start.26) | collective-permute-done | bytes 262176 | tf_op jit(solution)/shard_map/ppermute | solution.py:170
  76.8 1.8 %shard_map.59 = (f32[16,2048]{1,0:T(8,128)}, bf16[16,2048]{1,0:T(8,128)(2,1)}, bf16[16,2048]{1,0:T(8,128)(2,1)}, bf16[16,2048]{1,0:T(8,128)(2,1)}) custom-call(f32[64,2048]{1,0:T(8,128)} %copy-done, bf16[64,2048]{1,0:T(8,128)(2,1)} %copy-done.3), custom_call_target="tpu_custom_call" | custom-call | tf_op jit(solution)/shard_map/pallas_call | solution.py:121
  78.7 3.0 %collective-permute-start.27 = (bf16[16,2048]{1,0:T(8,128)(2,1)}, bf16[16,2048]{1,0:T(8,128)(2,1)S(1)}, u32[]{:S(2)}, u32[]{:S(2)}) collective-permute-start(bf16[16,2048]{1,0:T(8,128)(2,1)} %get-tuple-element.14), channel_id=1, source_target_pairs={{0,64},{32,96},{64,128},{96,160},{128,192},{160,224},{192,0},{224,... | collective-permute-start | bytes 196616 | tf_op jit(solution)/shard_map/ppermute | solution.py:173
  81.7 5.1 %collective-permute-start.28 = (bf16[16,2048]{1,0:T(8,128)(2,1)}, bf16[16,2048]{1,0:T(8,128)(2,1)S(1)}, u32[]{:S(2)}, u32[]{:S(2)}) collective-permute-start(bf16[16,2048]{1,0:T(8,128)(2,1)} %get-tuple-element.15), channel_id=1, source_target_pairs={{0,128},{32,160},{64,192},{96,224},{128,0},{160,32},{192,64},{224,... | collective-permute-start | bytes 196616 | tf_op jit(solution)/shard_map/ppermute | solution.py:173
  86.8 2.4 %collective-permute-start.29 = (bf16[16,2048]{1,0:T(8,128)(2,1)}, bf16[16,2048]{1,0:T(8,128)(2,1)S(1)}, u32[]{:S(2)}, u32[]{:S(2)}) collective-permute-start(bf16[16,2048]{1,0:T(8,128)(2,1)} %get-tuple-element.16), channel_id=1, source_target_pairs={{0,192},{32,224},{64,0},{96,32},{128,64},{160,96},{192,128},{224,1... | collective-permute-start | bytes 196616 | tf_op jit(solution)/shard_map/ppermute | solution.py:173
  89.2 1.9 %collective-permute-done.28 = bf16[16,2048]{1,0:T(8,128)(2,1)S(1)} collective-permute-done((bf16[16,2048]{1,0:T(8,128)(2,1)}, bf16[16,2048]{1,0:T(8,128)(2,1)S(1)}, u32[]{:S(2)}, u32[]{:S(2)}) %collective-permute-start.28) | collective-permute-done | bytes 65568 | tf_op jit(solution)/shard_map/ppermute | solution.py:173
  91.1 2.9 %collective-permute-done.29 = bf16[16,2048]{1,0:T(8,128)(2,1)S(1)} collective-permute-done((bf16[16,2048]{1,0:T(8,128)(2,1)}, bf16[16,2048]{1,0:T(8,128)(2,1)S(1)}, u32[]{:S(2)}, u32[]{:S(2)}) %collective-permute-start.29) | collective-permute-done | bytes 65568 | tf_op jit(solution)/shard_map/ppermute | solution.py:173
  94.0 1.6 %convert_add_fusion = f32[16,2048]{1,0:T(8,128)} fusion(bf16[16,2048]{1,0:T(8,128)(2,1)S(1)} %collective-permute-done.29, bf16[16,2048]{1,0:T(8,128)(2,1)S(1)} %collective-permute-done.28, f32[16,2048]{1,0:T(8,128)} %get-tuple-element.13, bf16[16,2048]{1,0:T(8,128)(2,1)S(1)} %collective-permute-done.27), kind=kLoop, calls=%fused_computation.4 | loop fusion | flops 196608 | bytes 458752 | tf_op jit(solution)/shard_map/add | solution.py:174
  (63 shorter events, 7.6 us)
Async XLA Ops:
  0.0 35.2 %copy-start.1 = (bf16[2,2048,256]{2,1,0:T(8,128)(2,1)S(1)}, bf16[2,2048,256]{2,1,0:T(8,128)(2,1)}, u32[]{:S(2)}) copy-start(bf16[2,2048,256]{2,1,0:T(8,128)(2,1)} %ta_ref.7) | copy-start | bytes 6291460
  0.0 8.0 %collective-permute-start.10 = (bf16[2,64,256]{2,1,0:T(8,128)(2,1)}, bf16[2,64,256]{2,1,0:T(8,128)(2,1)S(1)}, u32[]{:S(2)}, u32[]{:S(2)}) collective-permute-start(bf16[2,64,256]{2,1,0:T(8,128)(2,1)} %param.7), channel_id=1, source_target_pairs={{0,4},{1,5},{2,6},{3,7},{4,0},{5,1},{6,2},{7,3},{8,12},{9,13},{10,... | collective-permute-start | bytes 196616 | tf_op jit(solution)/shard_map/ppermute | solution.py:152
  2.5 5.4 %collective-permute-start = (bf16[2,64,256]{2,1,0:T(8,128)(2,1)}, bf16[2,64,256]{2,1,0:T(8,128)(2,1)S(1)}, u32[]{:S(2)}, u32[]{:S(2)}) collective-permute-start(bf16[2,64,256]{2,1,0:T(8,128)(2,1)} %param.7), channel_id=1, source_target_pairs={{0,1},{1,2},{2,3},{3,0},{4,5},{5,6},{6,7},{7,4},{8,9},{9,10},{10,1... | collective-permute-start | bytes 196616 | tf_op jit(solution)/shard_map/ppermute | solution.py:29
  3.8 7.5 %collective-permute-start.1 = (bf16[2,64,256]{2,1,0:T(8,128)(2,1)}, bf16[2,64,256]{2,1,0:T(8,128)(2,1)S(1)}, u32[]{:S(2)}, u32[]{:S(2)}) collective-permute-start(bf16[2,64,256]{2,1,0:T(8,128)(2,1)} %param.7), channel_id=1, source_target_pairs={{0,3},{1,0},{2,1},{3,2},{4,7},{5,4},{6,5},{7,6},{8,11},{9,8},{10,9... | collective-permute-start | bytes 196616 | tf_op jit(solution)/shard_map/ppermute | solution.py:31
  5.2 3.6 %collective-permute-start.16 = (bf16[2,64,256]{2,1,0:T(8,128)(2,1)}, bf16[2,64,256]{2,1,0:T(8,128)(2,1)S(1)}, u32[]{:S(2)}, u32[]{:S(2)}) collective-permute-start(bf16[2,64,256]{2,1,0:T(8,128)(2,1)} %param.8), channel_id=1, source_target_pairs={{0,4},{1,5},{2,6},{3,7},{4,0},{5,1},{6,2},{7,3},{8,12},{9,13},{10,... | collective-permute-start | bytes 196616 | tf_op jit(solution)/shard_map/ppermute | solution.py:152
  5.4 5.9 %collective-permute-start.6 = (bf16[2,64,256]{2,1,0:T(8,128)(2,1)}, bf16[2,64,256]{2,1,0:T(8,128)(2,1)S(1)}, u32[]{:S(2)}, u32[]{:S(2)}) collective-permute-start(bf16[2,64,256]{2,1,0:T(8,128)(2,1)} %param.8), channel_id=1, source_target_pairs={{0,3},{1,0},{2,1},{3,2},{4,7},{5,4},{6,5},{7,6},{8,11},{9,8},{10,9... | collective-permute-start | bytes 196616 | tf_op jit(solution)/shard_map/ppermute | solution.py:30
  7.9 4.3 %collective-permute-start.2 = (bf16[2,64,256]{2,1,0:T(8,128)(2,1)S(1)}, bf16[2,64,256]{2,1,0:T(8,128)(2,1)S(1)}, u32[]{:S(2)}, u32[]{:S(2)}) collective-permute-start(bf16[2,64,256]{2,1,0:T(8,128)(2,1)S(1)} %collective-permute-done), channel_id=1, source_target_pairs={{0,1},{1,2},{2,3},{3,0},{4,5},{5,6},{6,7},{7,4},{8,9},{9,10},{10,1... | collective-permute-start | bytes 196616 | tf_op jit(solution)/shard_map/ppermute | solution.py:33
  8.0 6.3 %collective-permute-start.5 = (bf16[2,64,256]{2,1,0:T(8,128)(2,1)}, bf16[2,64,256]{2,1,0:T(8,128)(2,1)S(1)}, u32[]{:S(2)}, u32[]{:S(2)}) collective-permute-start(bf16[2,64,256]{2,1,0:T(8,128)(2,1)} %param.8), channel_id=1, source_target_pairs={{0,1},{1,2},{2,3},{3,0},{4,5},{5,6},{6,7},{7,4},{8,9},{9,10},{10,1... | collective-permute-start | bytes 196616 | tf_op jit(solution)/shard_map/ppermute | solution.py:32
  8.8 9.8 %collective-permute-start.18 = (bf16[2,64,256]{2,1,0:T(8,128)(2,1)S(1)}, bf16[2,64,256]{2,1,0:T(8,128)(2,1)S(1)}, u32[]{:S(2)}, u32[]{:S(2)}) collective-permute-start(bf16[2,64,256]{2,1,0:T(8,128)(2,1)S(1)} %collective-permute-done.16), channel_id=1, source_target_pairs={{0,24},{1,25},{2,26},{3,27},{4,28},{5,29},{6,30},{7,31},{8,0},{9,1... | collective-permute-start | bytes 196616 | tf_op jit(solution)/shard_map/ppermute | solution.py:30
  11.3 9.3 %collective-permute-start.17 = (bf16[2,64,256]{2,1,0:T(8,128)(2,1)S(1)}, bf16[2,64,256]{2,1,0:T(8,128)(2,1)S(1)}, u32[]{:S(2)}, u32[]{:S(2)}) collective-permute-start(bf16[2,64,256]{2,1,0:T(8,128)(2,1)S(1)} %collective-permute-done.16), channel_id=1, source_target_pairs={{0,8},{1,9},{2,10},{3,11},{4,12},{5,13},{6,14},{7,15},{8,16},{9,17... | collective-permute-start | bytes 196616 | tf_op jit(solution)/shard_map/ppermute | solution.py:32
  11.3 8.0 %collective-permute-start.11 = (bf16[2,64,256]{2,1,0:T(8,128)(2,1)S(1)}, bf16[2,64,256]{2,1,0:T(8,128)(2,1)S(1)}, u32[]{:S(2)}, u32[]{:S(2)}) collective-permute-start(bf16[2,64,256]{2,1,0:T(8,128)(2,1)S(1)} %collective-permute-done.10), channel_id=1, source_target_pairs={{0,8},{1,9},{2,10},{3,11},{4,12},{5,13},{6,14},{7,15},{8,16},{9,17... | collective-permute-start | bytes 196616 | tf_op jit(solution)/shard_map/ppermute | solution.py:29
  12.2 3.4 %collective-permute-start.7 = (bf16[2,64,256]{2,1,0:T(8,128)(2,1)S(1)}, bf16[2,64,256]{2,1,0:T(8,128)(2,1)S(1)}, u32[]{:S(2)}, u32[]{:S(2)}) collective-permute-start(bf16[2,64,256]{2,1,0:T(8,128)(2,1)S(1)} %collective-permute-done.6), channel_id=1, source_target_pairs={{0,3},{1,0},{2,1},{3,2},{4,7},{5,4},{6,5},{7,6},{8,11},{9,8},{10,9... | collective-permute-start | bytes 196616 | tf_op jit(solution)/shard_map/ppermute | solution.py:34
  14.3 16.0 %collective-permute-start.3 = (bf16[4,2,64,256]{3,2,1,0:T(8,128)(2,1)S(1)}, bf16[4,2,64,256]{3,2,1,0:T(8,128)(2,1)S(1)}, u32[]{:S(2)}, u32[]{:S(2)}) collective-permute-start(bf16[4,2,64,256]{3,2,1,0:T(8,128)(2,1)S(1)} %pad_maximum_fusion.refs_0_), channel_id=1, source_target_pairs={{0,8},{1,9},{2,10},{3,11},{4,12},{5,13},{6,14},{7,15},{8,16},{9,17... | collective-permute-start | bytes 786440 | tf_op jit(solution)/shard_map/ppermute | solution.py:29
  16.5 15.8 %collective-permute-start.24 = (bf16[4,2,64,256]{3,2,1,0:T(8,128)(2,1)S(1)}, bf16[4,2,64,256]{3,2,1,0:T(8,128)(2,1)S(1)}, u32[]{:S(2)}, u32[]{:S(2)}) collective-permute-start(bf16[4,2,64,256]{3,2,1,0:T(8,128)(2,1)S(1)} %pad_maximum_fusion.1.refs_1_), channel_id=1, source_target_pairs={{0,8},{1,9},{2,10},{3,11},{4,12},{5,13},{6,14},{7,15},{8,16},{9,17... | collective-permute-start | bytes 786440 | tf_op jit(solution)/shard_map/ppermute | solution.py:32
  18.7 3.1 %collective-permute-start.19 = (bf16[2,64,256]{2,1,0:T(8,128)(2,1)S(1)}, bf16[2,64,256]{2,1,0:T(8,128)(2,1)S(1)}, u32[]{:S(2)}, u32[]{:S(2)}) collective-permute-start(bf16[2,64,256]{2,1,0:T(8,128)(2,1)S(1)} %collective-permute-done.18), channel_id=1, source_target_pairs={{0,24},{1,25},{2,26},{3,27},{4,28},{5,29},{6,30},{7,31},{8,0},{9,1... | collective-permute-start | bytes 196616 | tf_op jit(solution)/shard_map/ppermute | solution.py:34
  19.3 3.5 %collective-permute-start.12 = (bf16[2,64,256]{2,1,0:T(8,128)(2,1)S(1)}, bf16[2,64,256]{2,1,0:T(8,128)(2,1)S(1)}, u32[]{:S(2)}, u32[]{:S(2)}) collective-permute-start(bf16[2,64,256]{2,1,0:T(8,128)(2,1)S(1)} %collective-permute-done.10), channel_id=1, source_target_pairs={{0,24},{1,25},{2,26},{3,27},{4,28},{5,29},{6,30},{7,31},{8,0},{9,1... | collective-permute-start | bytes 196616 | tf_op jit(solution)/shard_map/ppermute | solution.py:31
  20.7 11.7 %collective-permute-start.8 = (bf16[4,2,64,256]{3,2,1,0:T(8,128)(2,1)S(1)}, bf16[4,2,64,256]{3,2,1,0:T(8,128)(2,1)S(1)}, u32[]{:S(2)}, u32[]{:S(2)}) collective-permute-start(bf16[4,2,64,256]{3,2,1,0:T(8,128)(2,1)S(1)} %pad_maximum_fusion.1.refs_1_), channel_id=1, source_target_pairs={{0,24},{1,25},{2,26},{3,27},{4,28},{5,29},{6,30},{7,31},{8,0},{9,1... | collective-permute-start | bytes 786440 | tf_op jit(solution)/shard_map/ppermute | solution.py:30
  21.8 7.7 %collective-permute-start.13 = (bf16[2,64,256]{2,1,0:T(8,128)(2,1)S(1)}, bf16[2,64,256]{2,1,0:T(8,128)(2,1)S(1)}, u32[]{:S(2)}, u32[]{:S(2)}) collective-permute-start(bf16[2,64,256]{2,1,0:T(8,128)(2,1)S(1)} %collective-permute-done.11), channel_id=1, source_target_pairs={{0,8},{1,9},{2,10},{3,11},{4,12},{5,13},{6,14},{7,15},{8,16},{9,17... | collective-permute-start | bytes 196616 | tf_op jit(solution)/shard_map/ppermute | solution.py:33
  22.8 19.9 %collective-permute-start.22 = (bf16[4,2,64,256]{3,2,1,0:T(8,128)(2,1)S(1)}, bf16[4,2,64,256]{3,2,1,0:T(8,128)(2,1)S(1)}, u32[]{:S(2)}, u32[]{:S(2)}) collective-permute-start(bf16[4,2,64,256]{3,2,1,0:T(8,128)(2,1)S(1)} %pad_maximum_fusion.refs_0_), channel_id=1, source_target_pairs={{0,24},{1,25},{2,26},{3,27},{4,28},{5,29},{6,30},{7,31},{8,0},{9,1... | collective-permute-start | bytes 786440 | tf_op jit(solution)/shard_map/ppermute | solution.py:31
  29.5 15.9 %collective-permute-start.25 = (bf16[4,2,64,256]{3,2,1,0:T(8,128)(2,1)S(1)}, bf16[4,2,64,256]{3,2,1,0:T(8,128)(2,1)S(1)}, u32[]{:S(2)}, u32[]{:S(2)}) collective-permute-start(bf16[4,2,64,256]{3,2,1,0:T(8,128)(2,1)S(1)} %pad_maximum_fusion.3.refs_3_), channel_id=1, source_target_pairs={{0,1},{1,2},{2,3},{3,0},{4,5},{5,6},{6,7},{7,4},{8,9},{9,10},{10,1... | collective-permute-start | bytes 786440 | tf_op jit(solution)/shard_map/ppermute | solution.py:32
  30.3 15.2 %collective-permute-start.20 = (bf16[4,2,64,256]{3,2,1,0:T(8,128)(2,1)S(1)}, bf16[4,2,64,256]{3,2,1,0:T(8,128)(2,1)S(1)}, u32[]{:S(2)}, u32[]{:S(2)}) collective-permute-start(bf16[4,2,64,256]{3,2,1,0:T(8,128)(2,1)S(1)} %pad_maximum_fusion.3.refs_3_), channel_id=1, source_target_pairs={{0,3},{1,0},{2,1},{3,2},{4,7},{5,4},{6,5},{7,6},{8,11},{9,8},{10,9... | collective-permute-start | bytes 786440 | tf_op jit(solution)/shard_map/ppermute | solution.py:30
  32.3 10.5 %collective-permute-start.14 = (bf16[4,2,64,256]{3,2,1,0:T(8,128)(2,1)S(1)}, bf16[4,2,64,256]{3,2,1,0:T(8,128)(2,1)S(1)}, u32[]{:S(2)}, u32[]{:S(2)}) collective-permute-start(bf16[4,2,64,256]{3,2,1,0:T(8,128)(2,1)S(1)} %pad_maximum_fusion.2.refs_2_), channel_id=1, source_target_pairs={{0,1},{1,2},{2,3},{3,0},{4,5},{5,6},{6,7},{7,4},{8,9},{9,10},{10,1... | collective-permute-start | bytes 786440 | tf_op jit(solution)/shard_map/ppermute | solution.py:29
  32.4 22.5 %collective-permute-start.23 = (bf16[4,2,64,256]{3,2,1,0:T(8,128)(2,1)S(1)}, bf16[4,2,64,256]{3,2,1,0:T(8,128)(2,1)S(1)}, u32[]{:S(2)}, u32[]{:S(2)}) collective-permute-start(bf16[4,2,64,256]{3,2,1,0:T(8,128)(2,1)S(1)} %pad_maximum_fusion.2.refs_2_), channel_id=1, source_target_pairs={{0,3},{1,0},{2,1},{3,2},{4,7},{5,4},{6,5},{7,6},{8,11},{9,8},{10,9... | collective-permute-start | bytes 786440 | tf_op jit(solution)/shard_map/ppermute | solution.py:31
  35.2 1.6 %copy-start.2 = (bf16[2,2048,256]{2,1,0:T(8,128)(2,1)S(1)}, bf16[2,2048,256]{2,1,0:T(8,128)(2,1)}, u32[]{:S(2)}) copy-start(bf16[2,2048,256]{2,1,0:T(8,128)(2,1)} %tg_ref.7) | copy-start | bytes 6291460
  42.7 18.9 %collective-permute-start.4 = (bf16[4,2,64,256]{3,2,1,0:T(8,128)(2,1)S(1)}, bf16[4,2,64,256]{3,2,1,0:T(8,128)(2,1)S(1)}, u32[]{:S(2)}, u32[]{:S(2)}) collective-permute-start(bf16[4,2,64,256]{3,2,1,0:T(8,128)(2,1)S(1)} %collective-permute-done.3.refs_0_), channel_id=1, source_target_pairs={{0,8},{1,9},{2,10},{3,11},{4,12},{5,13},{6,14},{7,15},{8,16},{9,17... | collective-permute-start | bytes 786440 | tf_op jit(solution)/shard_map/ppermute | solution.py:33
  42.8 18.8 %collective-permute-start.9 = (bf16[4,2,64,256]{3,2,1,0:T(8,128)(2,1)S(1)}, bf16[4,2,64,256]{3,2,1,0:T(8,128)(2,1)S(1)}, u32[]{:S(2)}, u32[]{:S(2)}) collective-permute-start(bf16[4,2,64,256]{3,2,1,0:T(8,128)(2,1)S(1)} %collective-permute-done.8.refs_1_), channel_id=1, source_target_pairs={{0,24},{1,25},{2,26},{3,27},{4,28},{5,29},{6,30},{7,31},{8,0},{9,1... | collective-permute-start | bytes 786440 | tf_op jit(solution)/shard_map/ppermute | solution.py:34
  45.5 16.2 %collective-permute-start.15 = (bf16[4,2,64,256]{3,2,1,0:T(8,128)(2,1)S(1)}, bf16[4,2,64,256]{3,2,1,0:T(8,128)(2,1)S(1)}, u32[]{:S(2)}, u32[]{:S(2)}) collective-permute-start(bf16[4,2,64,256]{3,2,1,0:T(8,128)(2,1)S(1)} %collective-permute-done.14.refs_2_), channel_id=1, source_target_pairs={{0,1},{1,2},{2,3},{3,0},{4,5},{5,6},{6,7},{7,4},{8,9},{9,10},{10,1... | collective-permute-start | bytes 786440 | tf_op jit(solution)/shard_map/ppermute | solution.py:33
  45.5 16.2 %collective-permute-start.21 = (bf16[4,2,64,256]{3,2,1,0:T(8,128)(2,1)S(1)}, bf16[4,2,64,256]{3,2,1,0:T(8,128)(2,1)S(1)}, u32[]{:S(2)}, u32[]{:S(2)}) collective-permute-start(bf16[4,2,64,256]{3,2,1,0:T(8,128)(2,1)S(1)} %collective-permute-done.20.refs_3_), channel_id=1, source_target_pairs={{0,3},{1,0},{2,1},{3,2},{4,7},{5,4},{6,5},{7,6},{8,11},{9,8},{10,9... | collective-permute-start | bytes 786440 | tf_op jit(solution)/shard_map/ppermute | solution.py:34
  69.2 7.0 %collective-permute-start.26 = (bf16[64,2048]{1,0:T(8,128)(2,1)S(1)}, bf16[64,2048]{1,0:T(8,128)(2,1)S(1)}, u32[]{:S(2)}, u32[]{:S(2)}) collective-permute-start(bf16[64,2048]{1,0:T(8,128)(2,1)S(1)} %get-tuple-element.12), channel_id=1, source_target_pairs={{0,32},{32,0},{64,96},{96,64},{128,160},{160,128},{192,224},{224,1... | collective-permute-start | bytes 786440 | tf_op jit(solution)/shard_map/ppermute | solution.py:170
  78.7 10.5 %collective-permute-start.27 = (bf16[16,2048]{1,0:T(8,128)(2,1)}, bf16[16,2048]{1,0:T(8,128)(2,1)S(1)}, u32[]{:S(2)}, u32[]{:S(2)}) collective-permute-start(bf16[16,2048]{1,0:T(8,128)(2,1)} %get-tuple-element.14), channel_id=1, source_target_pairs={{0,64},{32,96},{64,128},{96,160},{128,192},{160,224},{192,0},{224,... | collective-permute-start | bytes 196616 | tf_op jit(solution)/shard_map/ppermute | solution.py:173
  81.7 9.4 %collective-permute-start.28 = (bf16[16,2048]{1,0:T(8,128)(2,1)}, bf16[16,2048]{1,0:T(8,128)(2,1)S(1)}, u32[]{:S(2)}, u32[]{:S(2)}) collective-permute-start(bf16[16,2048]{1,0:T(8,128)(2,1)} %get-tuple-element.15), channel_id=1, source_target_pairs={{0,128},{32,160},{64,192},{96,224},{128,0},{160,32},{192,64},{224,... | collective-permute-start | bytes 196616 | tf_op jit(solution)/shard_map/ppermute | solution.py:173
  86.8 7.3 %collective-permute-start.29 = (bf16[16,2048]{1,0:T(8,128)(2,1)}, bf16[16,2048]{1,0:T(8,128)(2,1)S(1)}, u32[]{:S(2)}, u32[]{:S(2)}) collective-permute-start(bf16[16,2048]{1,0:T(8,128)(2,1)} %get-tuple-element.16), channel_id=1, source_target_pairs={{0,192},{32,224},{64,0},{96,32},{128,64},{160,96},{192,128},{224,1... | collective-permute-start | bytes 196616 | tf_op jit(solution)/shard_map/ppermute | solution.py:173
  (2 other events, 1.5 us)

commit v2 on v0

v2 whole, which is shorter than its diff:
```python
import functools

import jax
import jax.numpy as jnp
from jax import lax
from jax.experimental import pallas as pl
from jax.experimental.pallas import tpu as pltpu
from jax.sharding import PartitionSpec as P

Q = 128
NX, NZ, NY = 4, 2, 4
NH, NC = 4, 2
ROWS = 32
BF16 = jnp.bfloat16
F32 = jnp.float32
AXES = ("layer", "tok")
SMALL = pltpu.CompilerParams(vmem_limit_bytes=4 * 1024 * 1024)
VMEM = pl.BlockSpec(memory_space=pltpu.VMEM)


def moves(step):
    pairs = []
    for h in range(NH):
        for c in range(NC):
            for x in range(NX):
                for z in range(NZ):
                    for y in range(NY):
                        to = step(h, c, x, z, y)
                        here, there = (
                            (((i[0] % NH * NC + i[1] % NC) * NX + i[2] % NX) * NZ + i[3] % NZ) * NY
                            + i[4] % NY
                            for i in ((h, c, x, z, y), to)
                        )
                        pairs.append((here, there))
    return pairs


def first_ring(d):
    return moves(lambda h, c, x, z, y: (h, c, x, z, y + d) if c == 0 else (h, c, x + d, z, y))


def second_ring(d):
    return moves(lambda h, c, x, z, y: (h, c, x + d, z, y) if c == 0 else (h, c, x, z, y + d))


def send(value, pairs):
    return lax.ppermute(value, AXES, pairs)


def pack_kernel(core_ref, a_ref, g_ref, sib_a_ref, sib_g_ref, out_ref):
    rows = pl.ds(pl.multiple_of(core_ref[0] * ROWS, ROWS), ROWS)
    for layer in range(2):
        for k, refs in enumerate(((a_ref, sib_a_ref), (g_ref, sib_g_ref))):
            out_ref[layer, k] = refs[0][layer, rows]
            out_ref[2 + layer, k] = refs[1][layer, rows]


def pack(core, a, g, sib_a, sib_g):
    return pl.pallas_call(
        pack_kernel,
        in_specs=[pl.BlockSpec(memory_space=pltpu.SMEM)] + [VMEM] * 4,
        out_specs=VMEM,
        out_shape=jax.ShapeDtypeStruct((4, 2, ROWS, 256), BF16),
        compiler_params=SMALL,
    )(core.reshape(1), a, g, sib_a, sib_g)


def chunk_kernel(last, has_acc, n_blocks, ids_ref, labels_ref, *refs):
    trains = refs[:4]
    blocks = refs[4 : 4 + n_blocks]
    rest = refs[4 + n_blocks :]
    acc_ref = rest[0] if has_acc else None
    outs = rest[1:] if has_acc else rest
    sel = (labels_ref[...] == ids_ref[0:1, :]).astype(F32).astype(BF16)
    nt = (((1,), (1,)), ((), ()))
    rows = trains[0].shape[1]
    tile = 1024
    width = 4 * ROWS
    for j in range(rows // tile):
        cols = slice(j * tile, (j + 1) * tile)
        prods, sels = [], []
        for layer in range(4):
            ta = trains[2 * (layer // 2)][layer % 2, cols]
            tg = trains[2 * (layer // 2) + 1][layer % 2, cols]
            a = jnp.concatenate([b[:, layer, 0].reshape(width, 256) for b in blocks], 0)
            g = jnp.concatenate([b[:, layer, 1].reshape(width, 256) for b in blocks], 0)
            pa = lax.dot_general(a, ta, nt, preferred_element_type=F32)
            pg = lax.dot_general(g, tg, nt, preferred_element_type=F32)
            prods.append((pa * pg).astype(BF16))
            sels.append(sel)
        part = jnp.dot(
            jnp.concatenate(sels, 1), jnp.concatenate(prods, 0), preferred_element_type=F32
        )
        if has_acc:
            part = part + acc_ref[:, cols]
        if last:
            outs[0][:, cols] = part[: Q // 2]
            outs[1][:, cols] = part[Q // 2 :].astype(BF16)
        else:
            outs[0][:, cols] = part


def chunk(ids, labels, trains, blocks, acc, last):
    rows = trains[0].shape[1]
    args = [ids, labels, *trains, *blocks]
    if acc is not None:
        args.append(acc)
    if last:
        out_shape = (
            jax.ShapeDtypeStruct((Q // 2, rows), F32),
            jax.ShapeDtypeStruct((Q // 2, rows), BF16),
        )
        out_specs = (VMEM, VMEM)
    else:
        out_shape = jax.ShapeDtypeStruct((Q, rows), F32)
        out_specs = VMEM
    s_rows = 4 * ROWS * len(blocks)
    return pl.pallas_call(
        functools.partial(chunk_kernel, last, acc is not None, len(blocks)),
        in_specs=[VMEM] * len(args),
        out_specs=out_specs,
        out_shape=out_shape,
        compiler_params=pltpu.CompilerParams(vmem_limit_bytes=24 * 1024 * 1024),
        cost_estimate=pl.CostEstimate(
            flops=2 * 4 * s_rows * rows * (2 * 256 + Q),
            bytes_accessed=1024 * 1024,
            transcendentals=0,
        ),
    )(*args)


def merge_kernel(keep_ref, got_ref, own_ref, *send_refs):
    own_ref[...] = keep_ref[0:16] + got_ref[0:16].astype(F32)
    for k, ref in enumerate(send_refs, 1):
        rows = slice(16 * k, 16 * k + 16)
        ref[...] = (keep_ref[rows] + got_ref[rows].astype(F32)).astype(BF16)


def merge(keep, got):
    rows = keep.shape[1]
    part = jax.ShapeDtypeStruct((16, rows), BF16)
    return pl.pallas_call(
        merge_kernel,
        in_specs=[VMEM] * 2,
        out_specs=(VMEM,) * 4,
        out_shape=(jax.ShapeDtypeStruct((16, rows), F32), part, part, part),
        compiler_params=SMALL,
    )(keep, got)


def total_kernel(own_ref, *refs):
    total = own_ref[...]
    for ref in refs[:-1]:
        total = total + ref[...].astype(F32)
    refs[-1][...] = total


def total(own, parts):
    return pl.pallas_call(
        total_kernel,
        in_specs=[VMEM] * 4,
        out_specs=VMEM,
        out_shape=jax.ShapeDtypeStruct(own.shape, F32),
        compiler_params=SMALL,
    )(own, *parts)


def chunk_queries(segment_ids, core, x, z, y):
    ids = segment_ids.reshape(NX, NZ, NY, 2, ROWS)
    ids = jnp.where(core == 0, ids[:, :, :, 0], ids[:, :, :, 1])
    turned = jnp.where(core == 0, ids, jnp.swapaxes(ids, 0, 2))
    second, first = jnp.where(core == 0, x, y), jnp.where(core == 0, y, x)
    both = jnp.concatenate([turned, turned], 0)
    ids = lax.dynamic_slice_in_dim(both, second, 4, 0)
    ids = lax.dynamic_slice_in_dim(jnp.concatenate([ids, ids], 1), z, 2, 1)
    ids = lax.dynamic_slice_in_dim(jnp.concatenate([ids, ids], 2), first, 4, 2)
    order = (0, 3, 1, 2)
    ids = jnp.concatenate([ids[o : o + 1] for o in order], 0)
    ids = jnp.concatenate([ids[:, :, o : o + 1] for o in order], 2)
    return ids.reshape(4, 1, 2 * 4 * ROWS)


def on_device(train_act, train_grad, test_act, test_grad, segment_ids):
    tok = lax.axis_index("tok")
    layer = lax.axis_index("layer")
    x, z, y = tok // 8, (tok // 4) % 2, tok % 4
    core, z_hi = layer % 2, layer // 2

    sibling = moves(lambda h, c, x, z, y: (h, 1 - c, x, z, y))
    partner = moves(lambda h, c, x, z, y: (h, c, x, 1 - z, y))

    sib_a = send(test_act, sibling)
    sib_g = send(test_grad, sibling)
    block = pack(core, test_act, test_grad, sib_a, sib_g)
    sib_ta = send(train_act, sibling)
    sib_tg = send(train_grad, sibling)
    trains = (train_act, train_grad, sib_ta, sib_tg)

    chunk_ids = chunk_queries(segment_ids, core, x, z, y)
    r = lax.broadcasted_iota(jnp.int32, (Q, 1), 0)
    labels = ((z_hi + (r % 64) // 16) % 4) * 32 + (core ^ (r // 64)) * 16 + r % 16

    other = send(block, partner)

    def near(value):
        return jnp.stack([value] + [send(value, first_ring(d)) for d in (1, -1, 2)])

    low, high = near(block), near(other)
    forward, back = second_ring(1), second_ring(-1)
    low_prev, low_next = send(low, forward), send(low, back)
    high_prev, high_next = send(high, forward), send(high, back)
    low_far, high_far = send(low_prev, forward), send(high_next, back)

    half = 4 * ROWS
    run = functools.partial(chunk, labels=labels, trains=trains)
    acc = run(ids=chunk_ids[0], blocks=(low, high), acc=None, last=False)
    acc = run(ids=chunk_ids[1], blocks=(low_prev, high_prev), acc=acc, last=False)
    acc = run(ids=chunk_ids[2], blocks=(low_next, high_next), acc=acc, last=False)
    acc = run(ids=chunk_ids[3][:, :half], blocks=(low_far,), acc=acc, last=False)
    keep, give = run(ids=chunk_ids[3][:, half:], blocks=(high_far,), acc=acc, last=True)

    got = send(give, sibling)
    own, *parts = merge(keep, got)
    parts = [
        send(part, moves(lambda h, c, x, z, y: (h + k, c, x, z, y)))
        for k, part in enumerate(parts, 1)
    ]
    return total(own, parts)


def solution(mesh):
    placed = (
        P("layer", "tok", None),
        P("layer", "tok", None),
        P("layer", "tok", None),
        P("layer", "tok", None),
        P(),
    )
    return jax.shard_map(
        on_device, mesh=mesh, in_specs=placed, out_specs=P("layer", "tok"), check_vma=False
    )
```

time: 273 us -> 86.2 us (0.32)
  waiting for transfers between devices: 144 us -> 16.2 us
  matrix products: 61.7 us -> 0 us
  blocking collectives: 50.1 us -> 0 us
  starting transfers between devices: 0.01 us -> 35.7 us
  Pallas kernels: 0 us -> 28 us
  between operations: 13.4 us -> 0.26 us
  local copies, waits for them, and re-layouts: 0.78 us -> 4.4 us
    all_gather x1 -> x0, waiting for transfers between devices: 144 us -> none  [sent_together(): result, at, done = (lax.all_gather(both, axis, axis=dim, tiled=True), 0, [])]
    dot_general x16 -> x0, matrix products: 61.7 us -> none  [the longest x8 32.1 us: on_device(): jnp.dot(select, product, preferred_element_type=jnp.float32)]
    all_to_all x1 -> x0, blocking collectives: 50.1 us -> none  [sum_at_owner(): tiles = lax.all_to_all(cut_along(value, dim, peers), axis, 0, 0, tiled=True)]
    ppermute x0 -> x21, starting transfers between devices: none -> 35.7 us  [send(): return lax.ppermute(value, AXES, pairs)]
    pallas_call x0 -> x8, Pallas kernels: none -> 28 us  [the longest x5 27.3 us: chunk(): pl.pallas_call(functools.partial(chunk_kernel, last, acc is not None, len...]
    ppermute x0 -> x21, waiting for transfers between devices: none -> 16.2 us  [send(): return lax.ppermute(value, AXES, pairs)]
    unnamed x4 -> x8, local copies, waits for them, and re-layouts: 0.01 us -> 3.27 us
  transfers between devices with their start and end apart: 1 -> 21, of which waited for: 1 -> 10; matrix products, arithmetic and copies ran while one was open for 0% -> 3% of each run, Pallas kernels for 0% -> 25%
where the time goes in v2:
time: 86.2 us; the launch traced here: 85.9 us
  starting transfers between devices  35.7 us (41%)
  Pallas kernels  28 us (32%)
  waiting for transfers between devices  16.2 us (19%)
  local copies, waits for them, and re-layouts  4.4 us (5%)
  other arithmetic  1.31 us (2%)
    ppermute x21, starting transfers between devices, send(): return lax.ppermute(value, AXES, pairs)  35.7 us
    pallas_call x5, Pallas kernels, chunk(): pl.pallas_call(functools.partial(chunk_kernel, last, acc is not None, len...  27.3 us
    ppermute x21, waiting for transfers between devices, send(): return lax.ppermute(value, AXES, pairs)  16.2 us
    unnamed x8, local copies, waits for them, and re-layouts  3.27 us
  transfers between devices with their start and end apart: 21, of which 10 were waited for; matrix products, arithmetic and copies ran while one was open for 3% of the time, Pallas kernels for 25%

profile of v2, /device:TPU:1, one launch (start us, length us, event | category | flops | bytes accessed | tf_op | source)
XLA Modules:
  0.0 85.9 jit_solution(16268572644657833790)
XLA Ops:
  0.0 3.2 %collective-permute-start.2 = (bf16[2,64,256]{2,1,0:T(8,128)(2,1)}, bf16[2,64,256]{2,1,0:T(8,128)(2,1)S(1)}, u32[]{:S(2)}, u32[]{:S(2)}) collective-permute-start(bf16[2,64,256]{2,1,0:T(8,128)(2,1)} %a_ref.1), channel_id=1, source_target_pairs={{0,32},{1,33},{2,34},{3,35},{4,36},{5,37},{6,38},{7,39},{8,40},{9,... | collective-permute-start | bytes 196616 | tf_op jit(solution)/shard_map/ppermute | solution.py:47
  4.8 0.8 copy-done.2
  5.6 0.8 copy-done.3
  6.6 2.7 %collective-permute-start.12 = (bf16[4,2,32,256]{3,2,1,0:T(8,128)(2,1)S(1)}, bf16[4,2,32,256]{3,2,1,0:T(8,128)(2,1)S(1)}, u32[]{:S(2)}, u32[]{:S(2)}) collective-permute-start(bf16[4,2,32,256]{3,2,1,0:T(8,128)(2,1)S(1)} %shard_map.55), channel_id=1, source_target_pairs={{0,2},{1,3},{2,0},{3,1},{4,6},{5,7},{6,4},{7,5},{8,10},{9,11},{10,... | collective-permute-start | bytes 393224 | tf_op jit(solution)/shard_map/ppermute | solution.py:47
  9.6 1.5 %collective-permute-done.4 = bf16[4,2,32,256]{3,2,1,0:T(8,128)(2,1)S(1)} collective-permute-done((bf16[4,2,32,256]{3,2,1,0:T(8,128)(2,1)S(1)}, bf16[4,2,32,256]{3,2,1,0:T(8,128)(2,1)S(1)}, u32[]{:S(2)}, u32[]{:S(2)}) %collective-permute-start.4) | collective-permute-done | bytes 131104 | tf_op jit(solution)/shard_map/ppermute | solution.py:47
  11.1 1.3 %collective-permute-start.11 = (bf16[4,2,32,256]{3,2,1,0:T(8,128)(2,1)S(1)}, bf16[4,2,32,256]{3,2,1,0:T(8,128)(2,1)S(1)}, u32[]{:S(2)}, u32[]{:S(2)}) collective-permute-start(bf16[4,2,32,256]{3,2,1,0:T(8,128)(2,1)S(1)} %shard_map.55), channel_id=1, source_target_pairs={{0,3},{1,0},{2,1},{3,2},{4,7},{5,4},{6,5},{7,6},{8,11},{9,8},{10,9... | collective-permute-start | bytes 393224 | tf_op jit(solution)/shard_map/ppermute | solution.py:47
  12.4 0.9 %collective-permute-start.5 = (bf16[4,2,32,256]{3,2,1,0:T(8,128)(2,1)S(1)}, bf16[4,2,32,256]{3,2,1,0:T(8,128)(2,1)S(1)}, u32[]{:S(2)}, u32[]{:S(2)}) collective-permute-start(bf16[4,2,32,256]{3,2,1,0:T(8,128)(2,1)S(1)} %collective-permute-done.4), channel_id=1, source_target_pairs={{0,1},{1,2},{2,3},{3,0},{4,5},{5,6},{6,7},{7,4},{8,9},{9,10},{10,1... | collective-permute-start | bytes 393224 | tf_op jit(solution)/shard_map/ppermute | solution.py:47
  13.3 0.9 %collective-permute-done.10 = bf16[4,2,32,256]{3,2,1,0:T(8,128)(2,1)S(1)} collective-permute-done((bf16[4,2,32,256]{3,2,1,0:T(8,128)(2,1)S(1)}, bf16[4,2,32,256]{3,2,1,0:T(8,128)(2,1)S(1)}, u32[]{:S(2)}, u32[]{:S(2)}) %collective-permute-start.10) | collective-permute-done | bytes 131104 | tf_op jit(solution)/shard_map/ppermute | solution.py:47
  14.3 0.9 %collective-permute-start.6 = (bf16[4,2,32,256]{3,2,1,0:T(8,128)(2,1)S(1)}, bf16[4,2,32,256]{3,2,1,0:T(8,128)(2,1)}, u32[]{:S(2)}, u32[]{:S(2)}) collective-permute-start(bf16[4,2,32,256]{3,2,1,0:T(8,128)(2,1)S(1)} %collective-permute-done.4), channel_id=1, source_target_pairs={{0,3},{1,0},{2,1},{3,2},{4,7},{5,4},{6,5},{7,6},{8,11},{9,8},{10,9... | collective-permute-start | bytes 393224 | tf_op jit(solution)/shard_map/ppermute | solution.py:47
  15.2 1.2 %collective-permute-start.7 = (bf16[4,2,32,256]{3,2,1,0:T(8,128)(2,1)S(1)}, bf16[4,2,32,256]{3,2,1,0:T(8,128)(2,1)}, u32[]{:S(2)}, u32[]{:S(2)}) collective-permute-start(bf16[4,2,32,256]{3,2,1,0:T(8,128)(2,1)S(1)} %collective-permute-done.4), channel_id=1, source_target_pairs={{0,2},{1,3},{2,0},{3,1},{4,6},{5,7},{6,4},{7,5},{8,10},{9,11},{10,... | collective-permute-start | bytes 393224 | tf_op jit(solution)/shard_map/ppermute | solution.py:47
  16.6 1.0 %collective-permute-done.5 = bf16[4,2,32,256]{3,2,1,0:T(8,128)(2,1)S(1)} collective-permute-done((bf16[4,2,32,256]{3,2,1,0:T(8,128)(2,1)S(1)}, bf16[4,2,32,256]{3,2,1,0:T(8,128)(2,1)S(1)}, u32[]{:S(2)}, u32[]{:S(2)}) %collective-permute-start.5) | collective-permute-done | bytes 131104 | tf_op jit(solution)/shard_map/ppermute | solution.py:47
  17.5 1.3 %collective-permute-start.13 = (bf16[4,4,2,32,256]{4,3,2,1,0:T(8,128)(2,1)S(1)}, bf16[4,4,2,32,256]{4,3,2,1,0:T(8,128)(2,1)}, u32[]{:S(2)}, u32[]{:S(2)}) collective-permute-start(bf16[4,4,2,32,256]{4,3,2,1,0:T(8,128)(2,1)S(1)} %pad_maximum_fusion.1.refs_4_), channel_id=1, source_target_pairs={{0,8},{1,9},{2,10},{3,11},{4,12},{5,13},{6,14},{7,15},{8,16},{9,17... | collective-permute-start | bytes 1572872 | tf_op jit(solution)/shard_map/ppermute | solution.py:47
  18.8 1.8 %collective-permute-done.7 = bf16[4,2,32,256]{3,2,1,0:T(8,128)(2,1)} collective-permute-done((bf16[4,2,32,256]{3,2,1,0:T(8,128)(2,1)S(1)}, bf16[4,2,32,256]{3,2,1,0:T(8,128)(2,1)}, u32[]{:S(2)}, u32[]{:S(2)}) %collective-permute-start.7) | collective-permute-done | bytes 131104 | tf_op jit(solution)/shard_map/ppermute | solution.py:47
  20.7 1.0 %pad_maximum_fusion.refs_5_ = bf16[4,4,2,32,256]{4,3,2,1,0:T(8,128)(2,1)S(1)} fusion(bf16[1,4,2,32,256]{4,3,2,1,0:T(8,128)(2,1)} %bitcast.6, bf16[1,4,2,32,256]{4,3,2,1,0:T(8,128)(2,1)} %bitcast.5, bf16[1,4,2,32,256]{4,3,2,1,0:T(8,128)(2,1)S(1)} %bitcast.16, bf16[1,4,2,32,256]{4,3,2,1,0:T(8,128)(2,1)S(1)} %bitcast.13), kind=kLoop, calls=%fused_computation | loop fusion | flops 786432 | bytes 1048576 | tf_op jit(solution)/shard_map/stack | solution.py:206
  21.7 2.8 %collective-permute-start.8 = (bf16[4,4,2,32,256]{4,3,2,1,0:T(8,128)(2,1)S(1)}, bf16[4,4,2,32,256]{4,3,2,1,0:T(8,128)(2,1)}, u32[]{:S(2)}, u32[]{:S(2)}) collective-permute-start(bf16[4,4,2,32,256]{4,3,2,1,0:T(8,128)(2,1)S(1)} %pad_maximum_fusion.refs_5_), channel_id=1, source_target_pairs={{0,24},{1,25},{2,26},{3,27},{4,28},{5,29},{6,30},{7,31},{8,0},{9,1... | collective-permute-start | bytes 1572872 | tf_op jit(solution)/shard_map/ppermute | solution.py:47
  24.6 4.1 %collective-permute-done.13.refs_4_ = bf16[4,4,2,32,256]{4,3,2,1,0:T(8,128)(2,1)} collective-permute-done((bf16[4,4,2,32,256]{4,3,2,1,0:T(8,128)(2,1)S(1)}, bf16[4,4,2,32,256]{4,3,2,1,0:T(8,128)(2,1)}, u32[]{:S(2)}, u32[]{:S(2)}) %collective-permute-start.13) | collective-permute-done | bytes 524320 | tf_op jit(solution)/shard_map/ppermute | solution.py:47
  28.6 0.9 %collective-permute-start.15 = (bf16[4,4,2,32,256]{4,3,2,1,0:T(8,128)(2,1)S(1)}, bf16[4,4,2,32,256]{4,3,2,1,0:T(8,128)(2,1)}, u32[]{:S(2)}, u32[]{:S(2)}) collective-permute-start(bf16[4,4,2,32,256]{4,3,2,1,0:T(8,128)(2,1)S(1)} %pad_maximum_fusion.1.refs_4_), channel_id=1, source_target_pairs={{0,24},{1,25},{2,26},{3,27},{4,28},{5,29},{6,30},{7,31},{8,0},{9,1... | collective-permute-start | bytes 1572872 | tf_op jit(solution)/shard_map/ppermute | solution.py:47
  30.6 0.9 %collective-permute-start.14 = (bf16[4,4,2,32,256]{4,3,2,1,0:T(8,128)(2,1)}, bf16[4,4,2,32,256]{4,3,2,1,0:T(8,128)(2,1)S(1)}, u32[]{:S(2)}, u32[]{:S(2)}) collective-permute-start(bf16[4,4,2,32,256]{4,3,2,1,0:T(8,128)(2,1)} %collective-permute-done.13.refs_4_), channel_id=1, source_target_pairs={{0,8},{1,9},{2,10},{3,11},{4,12},{5,13},{6,14},{7,15},{8,16},{9,17... | collective-permute-start | bytes 1572872 | tf_op jit(solution)/shard_map/ppermute | solution.py:47
  31.5 2.4 %collective-permute-start.9 = (bf16[4,4,2,32,256]{4,3,2,1,0:T(8,128)(2,1)}, bf16[4,4,2,32,256]{4,3,2,1,0:T(8,128)(2,1)S(1)}, u32[]{:S(2)}, u32[]{:S(2)}) collective-permute-start(bf16[4,4,2,32,256]{4,3,2,1,0:T(8,128)(2,1)} %collective-permute-done.8.refs_5_), channel_id=1, source_target_pairs={{0,24},{1,25},{2,26},{3,27},{4,28},{5,29},{6,30},{7,31},{8,0},{9,1... | collective-permute-start | bytes 1572872 | tf_op jit(solution)/shard_map/ppermute | solution.py:47
  33.8 1.6 %copy-done.1 = bf16[2,2048,256]{2,1,0:T(8,128)(2,1)S(1)} copy-done((bf16[2,2048,256]{2,1,0:T(8,128)(2,1)S(1)}, bf16[2,2048,256]{2,1,0:T(8,128)(2,1)}, u32[]{:S(2)}) %copy-start.1) | copy-done | bytes 2097176
  35.4 5.2 %shard_map.56.refs_6_ = f32[128,2048]{1,0:T(8,128)S(1)} custom-call(s32[1,256]{1,0:T(1,128)S(1)} %squeeze.18.ids_ref, s32[128,1]{1,0:T(8,128)S(1)} %fusion.5.labels_ref, bf16[2,2048,256]{2,1,0:T(8,128)(2,1)S(1)} %copy-done, bf16[2,2048,256]{2,1,0:T(8,128)(2,1)S(1)} %copy-done.1, bf16[2,2048,256]{2,1,0:T(8,128)(2,1)} %collective-permute-done.refs_2_, ...), custom_call_target="tpu_custom_call" | custom-call | flops 2684354560 | bytes 1048576 | tf_op jit(solution)/shard_map/pallas_call | solution.py:118
  40.7 5.5 %shard_map.57.refs_6_ = f32[128,2048]{1,0:T(8,128)S(1)} custom-call(s32[1,256]{1,0:T(1,128)S(1)} %squeeze.17.ids_ref, s32[128,1]{1,0:T(8,128)S(1)} %fusion.5.labels_ref, bf16[2,2048,256]{2,1,0:T(8,128)(2,1)S(1)} %copy-done, bf16[2,2048,256]{2,1,0:T(8,128)(2,1)S(1)} %copy-done.1, bf16[2,2048,256]{2,1,0:T(8,128)(2,1)} %collective-permute-done.refs_2_, ...), custom_call_target="tpu_custom_call" | custom-call | flops 2684354560 | bytes 1048576 | tf_op jit(solution)/shard_map/pallas_call | solution.py:118
  46.2 5.5 %shard_map.58.refs_5_ = f32[128,2048]{1,0:T(8,128)S(1)} custom-call(s32[1,256]{1,0:T(1,128)S(1)} %squeeze.16.ids_ref, s32[128,1]{1,0:T(8,128)S(1)} %fusion.5.labels_ref, bf16[2,2048,256]{2,1,0:T(8,128)(2,1)S(1)} %copy-done, bf16[2,2048,256]{2,1,0:T(8,128)(2,1)S(1)} %copy-done.1, bf16[2,2048,256]{2,1,0:T(8,128)(2,1)} %collective-permute-done.refs_2_, ...), custom_call_target="tpu_custom_call" | custom-call | flops 2684354560 | bytes 1048576 | tf_op jit(solution)/shard_map/pallas_call | solution.py:118
  51.7 5.4 %shard_map.59.refs_5_ = f32[128,2048]{1,0:T(8,128)S(1)} custom-call(s32[1,128]{1,0:T(1,128)S(1)} %get-tuple-element.25.ids_ref, s32[128,1]{1,0:T(8,128)S(1)} %fusion.5.labels_ref, bf16[2,2048,256]{2,1,0:T(8,128)(2,1)S(1)} %copy-done, bf16[2,2048,256]{2,1,0:T(8,128)(2,1)S(1)} %copy-done.1, bf16[2,2048,256]{2,1,0:T(8,128)(2,1)} %collective-permute-done.refs_2_, ...), custom_call_target="tpu_custom_call" | custom-call | flops 1342177280 | bytes 1048576 | tf_op jit(solution)/shard_map/pallas_call | solution.py:118
  57.1 5.6 %shard_map.60 = (f32[64,2048]{1,0:T(8,128)S(1)}, bf16[64,2048]{1,0:T(8,128)(2,1)S(1)}) custom-call(s32[1,128]{1,0:T(1,128)S(1)} %get-tuple-element.26.ids_ref, s32[128,1]{1,0:T(8,128)S(1)} %fusion.5.labels_ref, bf16[2,2048,256]{2,1,0:T(8,128)(2,1)S(1)} %copy-done, bf16[2,2048,256]{2,1,0:T(8,128)(2,1)S(1)} %copy-done.1, ...), custom_call_target="tpu_custom_call" | custom-call | flops 1342177280 | bytes 1048576 | tf_op jit(solution)/shard_map/pallas_call | solution.py:118
  62.8 5.9 %collective-permute-start.17 = (bf16[64,2048]{1,0:T(8,128)(2,1)S(1)}, bf16[64,2048]{1,0:T(8,128)(2,1)S(1)}, u32[]{:S(2)}, u32[]{:S(2)}) collective-permute-start(bf16[64,2048]{1,0:T(8,128)(2,1)S(1)} %get-tuple-element.12), channel_id=1, source_target_pairs={{0,32},{1,33},{2,34},{3,35},{4,36},{5,37},{6,38},{7,39},{8,40},{9,... | collective-permute-start | bytes 786440 | tf_op jit(solution)/shard_map/ppermute | solution.py:47
  68.7 1.2 %collective-permute-done.17.got_ref = bf16[64,2048]{1,0:T(8,128)(2,1)S(1)} collective-permute-done((bf16[64,2048]{1,0:T(8,128)(2,1)S(1)}, bf16[64,2048]{1,0:T(8,128)(2,1)S(1)}, u32[]{:S(2)}, u32[]{:S(2)}) %collective-permute-start.17) | collective-permute-done | bytes 262176 | tf_op jit(solution)/shard_map/ppermute | solution.py:47
  69.9 3.1 %collective-permute-start.18 = (bf16[16,2048]{1,0:T(8,128)(2,1)S(1)}, bf16[16,2048]{1,0:T(8,128)(2,1)S(1)}, u32[]{:S(2)}, u32[]{:S(2)}) collective-permute-start(bf16[16,2048]{1,0:T(8,128)(2,1)S(1)} %get-tuple-element.14), channel_id=1, source_target_pairs={{0,64},{1,65},{2,66},{3,67},{4,68},{5,69},{6,70},{7,71},{8,72},{9,... | collective-permute-start | bytes 196616 | tf_op jit(solution)/shard_map/ppermute | solution.py:47
  73.0 5.0 %collective-permute-start.19 = (bf16[16,2048]{1,0:T(8,128)(2,1)S(1)}, bf16[16,2048]{1,0:T(8,128)(2,1)S(1)}, u32[]{:S(2)}, u32[]{:S(2)}) collective-permute-start(bf16[16,2048]{1,0:T(8,128)(2,1)S(1)} %get-tuple-element.15), channel_id=1, source_target_pairs={{0,128},{1,129},{2,130},{3,131},{4,132},{5,133},{6,134},{7,135},{8... | collective-permute-start | bytes 196616 | tf_op jit(solution)/shard_map/ppermute | solution.py:47
  78.0 2.4 %collective-permute-start.20 = (bf16[16,2048]{1,0:T(8,128)(2,1)S(1)}, bf16[16,2048]{1,0:T(8,128)(2,1)S(1)}, u32[]{:S(2)}, u32[]{:S(2)}) collective-permute-start(bf16[16,2048]{1,0:T(8,128)(2,1)S(1)} %get-tuple-element.16), channel_id=1, source_target_pairs={{0,192},{1,193},{2,194},{3,195},{4,196},{5,197},{6,198},{7,199},{8... | collective-permute-start | bytes 196616 | tf_op jit(solution)/shard_map/ppermute | solution.py:47
  80.4 1.8 %collective-permute-done.19.refs_1_ = bf16[16,2048]{1,0:T(8,128)(2,1)S(1)} collective-permute-done((bf16[16,2048]{1,0:T(8,128)(2,1)S(1)}, bf16[16,2048]{1,0:T(8,128)(2,1)S(1)}, u32[]{:S(2)}, u32[]{:S(2)}) %collective-permute-start.19) | collective-permute-done | bytes 65568 | tf_op jit(solution)/shard_map/ppermute | solution.py:47
  82.2 3.0 %collective-permute-done.20.refs_2_ = bf16[16,2048]{1,0:T(8,128)(2,1)S(1)} collective-permute-done((bf16[16,2048]{1,0:T(8,128)(2,1)S(1)}, bf16[16,2048]{1,0:T(8,128)(2,1)S(1)}, u32[]{:S(2)}, u32[]{:S(2)}) %collective-permute-start.20) | collective-permute-done | bytes 65568 | tf_op jit(solution)/shard_map/ppermute | solution.py:47
  (46 shorter events, 4.0 us)
Async XLA Ops:
  0.0 33.8 %copy-start = (bf16[2,2048,256]{2,1,0:T(8,128)(2,1)S(1)}, bf16[2,2048,256]{2,1,0:T(8,128)(2,1)}, u32[]{:S(2)}) copy-start(bf16[2,2048,256]{2,1,0:T(8,128)(2,1)} %refs_0_.9) | copy-start | bytes 6291460
  0.0 4.7 %collective-permute-start.2 = (bf16[2,64,256]{2,1,0:T(8,128)(2,1)}, bf16[2,64,256]{2,1,0:T(8,128)(2,1)S(1)}, u32[]{:S(2)}, u32[]{:S(2)}) collective-permute-start(bf16[2,64,256]{2,1,0:T(8,128)(2,1)} %a_ref.1), channel_id=1, source_target_pairs={{0,32},{1,33},{2,34},{3,35},{4,36},{5,37},{6,38},{7,39},{8,40},{9,... | collective-permute-start | bytes 196616 | tf_op jit(solution)/shard_map/ppermute | solution.py:47
  3.2 1.5 %collective-permute-start.3 = (bf16[2,64,256]{2,1,0:T(8,128)(2,1)}, bf16[2,64,256]{2,1,0:T(8,128)(2,1)S(1)}, u32[]{:S(2)}, u32[]{:S(2)}) collective-permute-start(bf16[2,64,256]{2,1,0:T(8,128)(2,1)} %g_ref.1), channel_id=1, source_target_pairs={{0,32},{1,33},{2,34},{3,35},{4,36},{5,37},{6,38},{7,39},{8,40},{9,... | collective-permute-start | bytes 196616 | tf_op jit(solution)/shard_map/ppermute | solution.py:47
  3.2 28.2 %collective-permute-start = (bf16[2,2048,256]{2,1,0:T(8,128)(2,1)}, bf16[2,2048,256]{2,1,0:T(8,128)(2,1)}, u32[]{:S(2)}, u32[]{:S(2)}) collective-permute-start(bf16[2,2048,256]{2,1,0:T(8,128)(2,1)} %refs_0_.9), channel_id=1, source_target_pairs={{0,32},{1,33},{2,34},{3,35},{4,36},{5,37},{6,38},{7,39},{8,40},{9,... | collective-permute-start | bytes 6291464 | tf_op jit(solution)/shard_map/ppermute | solution.py:47
  3.8 30.1 %collective-permute-start.1 = (bf16[2,2048,256]{2,1,0:T(8,128)(2,1)}, bf16[2,2048,256]{2,1,0:T(8,128)(2,1)}, u32[]{:S(2)}, u32[]{:S(2)}) collective-permute-start(bf16[2,2048,256]{2,1,0:T(8,128)(2,1)} %refs_1_.9), channel_id=1, source_target_pairs={{0,32},{1,33},{2,34},{3,35},{4,36},{5,37},{6,38},{7,39},{8,40},{9,... | collective-permute-start | bytes 6291464 | tf_op jit(solution)/shard_map/ppermute | solution.py:47
  4.8 0.8 copy-start.2
  5.6 0.8 copy-start.3
  6.5 4.7 %collective-permute-start.4 = (bf16[4,2,32,256]{3,2,1,0:T(8,128)(2,1)S(1)}, bf16[4,2,32,256]{3,2,1,0:T(8,128)(2,1)S(1)}, u32[]{:S(2)}, u32[]{:S(2)}) collective-permute-start(bf16[4,2,32,256]{3,2,1,0:T(8,128)(2,1)S(1)} %shard_map.55), channel_id=1, source_target_pairs={{0,4},{1,5},{2,6},{3,7},{4,0},{5,1},{6,2},{7,3},{8,12},{9,13},{10,... | collective-permute-start | bytes 393224 | tf_op jit(solution)/shard_map/ppermute | solution.py:47
  6.6 5.8 %collective-permute-start.12 = (bf16[4,2,32,256]{3,2,1,0:T(8,128)(2,1)S(1)}, bf16[4,2,32,256]{3,2,1,0:T(8,128)(2,1)S(1)}, u32[]{:S(2)}, u32[]{:S(2)}) collective-permute-start(bf16[4,2,32,256]{3,2,1,0:T(8,128)(2,1)S(1)} %shard_map.55), channel_id=1, source_target_pairs={{0,2},{1,3},{2,0},{3,1},{4,6},{5,7},{6,4},{7,5},{8,10},{9,11},{10,... | collective-permute-start | bytes 393224 | tf_op jit(solution)/shard_map/ppermute | solution.py:47
  9.3 5.0 %collective-permute-start.10 = (bf16[4,2,32,256]{3,2,1,0:T(8,128)(2,1)S(1)}, bf16[4,2,32,256]{3,2,1,0:T(8,128)(2,1)S(1)}, u32[]{:S(2)}, u32[]{:S(2)}) collective-permute-start(bf16[4,2,32,256]{3,2,1,0:T(8,128)(2,1)S(1)} %shard_map.55), channel_id=1, source_target_pairs={{0,1},{1,2},{2,3},{3,0},{4,5},{5,6},{6,7},{7,4},{8,9},{9,10},{10,1... | collective-permute-start | bytes 393224 | tf_op jit(solution)/shard_map/ppermute | solution.py:47
  11.1 4.1 %collective-permute-start.11 = (bf16[4,2,32,256]{3,2,1,0:T(8,128)(2,1)S(1)}, bf16[4,2,32,256]{3,2,1,0:T(8,128)(2,1)S(1)}, u32[]{:S(2)}, u32[]{:S(2)}) collective-permute-start(bf16[4,2,32,256]{3,2,1,0:T(8,128)(2,1)S(1)} %shard_map.55), channel_id=1, source_target_pairs={{0,3},{1,0},{2,1},{3,2},{4,7},{5,4},{6,5},{7,6},{8,11},{9,8},{10,9... | collective-permute-start | bytes 393224 | tf_op jit(solution)/shard_map/ppermute | solution.py:47
  12.4 5.1 %collective-permute-start.5 = (bf16[4,2,32,256]{3,2,1,0:T(8,128)(2,1)S(1)}, bf16[4,2,32,256]{3,2,1,0:T(8,128)(2,1)S(1)}, u32[]{:S(2)}, u32[]{:S(2)}) collective-permute-start(bf16[4,2,32,256]{3,2,1,0:T(8,128)(2,1)S(1)} %collective-permute-done.4), channel_id=1, source_target_pairs={{0,1},{1,2},{2,3},{3,0},{4,5},{5,6},{6,7},{7,4},{8,9},{9,10},{10,1... | collective-permute-start | bytes 393224 | tf_op jit(solution)/shard_map/ppermute | solution.py:47
  14.3 4.5 %collective-permute-start.6 = (bf16[4,2,32,256]{3,2,1,0:T(8,128)(2,1)S(1)}, bf16[4,2,32,256]{3,2,1,0:T(8,128)(2,1)}, u32[]{:S(2)}, u32[]{:S(2)}) collective-permute-start(bf16[4,2,32,256]{3,2,1,0:T(8,128)(2,1)S(1)} %collective-permute-done.4), channel_id=1, source_target_pairs={{0,3},{1,0},{2,1},{3,2},{4,7},{5,4},{6,5},{7,6},{8,11},{9,8},{10,9... | collective-permute-start | bytes 393224 | tf_op jit(solution)/shard_map/ppermute | solution.py:47
  15.2 5.4 %collective-permute-start.7 = (bf16[4,2,32,256]{3,2,1,0:T(8,128)(2,1)S(1)}, bf16[4,2,32,256]{3,2,1,0:T(8,128)(2,1)}, u32[]{:S(2)}, u32[]{:S(2)}) collective-permute-start(bf16[4,2,32,256]{3,2,1,0:T(8,128)(2,1)S(1)} %collective-permute-done.4), channel_id=1, source_target_pairs={{0,2},{1,3},{2,0},{3,1},{4,6},{5,7},{6,4},{7,5},{8,10},{9,11},{10,... | collective-permute-start | bytes 393224 | tf_op jit(solution)/shard_map/ppermute | solution.py:47
  17.5 11.1 %collective-permute-start.13 = (bf16[4,4,2,32,256]{4,3,2,1,0:T(8,128)(2,1)S(1)}, bf16[4,4,2,32,256]{4,3,2,1,0:T(8,128)(2,1)}, u32[]{:S(2)}, u32[]{:S(2)}) collective-permute-start(bf16[4,4,2,32,256]{4,3,2,1,0:T(8,128)(2,1)S(1)} %pad_maximum_fusion.1.refs_4_), channel_id=1, source_target_pairs={{0,8},{1,9},{2,10},{3,11},{4,12},{5,13},{6,14},{7,15},{8,16},{9,17... | collective-permute-start | bytes 1572872 | tf_op jit(solution)/shard_map/ppermute | solution.py:47
  21.7 8.9 %collective-permute-start.8 = (bf16[4,4,2,32,256]{4,3,2,1,0:T(8,128)(2,1)S(1)}, bf16[4,4,2,32,256]{4,3,2,1,0:T(8,128)(2,1)}, u32[]{:S(2)}, u32[]{:S(2)}) collective-permute-start(bf16[4,4,2,32,256]{4,3,2,1,0:T(8,128)(2,1)S(1)} %pad_maximum_fusion.refs_5_), channel_id=1, source_target_pairs={{0,24},{1,25},{2,26},{3,27},{4,28},{5,29},{6,30},{7,31},{8,0},{9,1... | collective-permute-start | bytes 1572872 | tf_op jit(solution)/shard_map/ppermute | solution.py:47
  24.5 16.1 %collective-permute-start.16 = (bf16[4,4,2,32,256]{4,3,2,1,0:T(8,128)(2,1)S(1)}, bf16[4,4,2,32,256]{4,3,2,1,0:T(8,128)(2,1)}, u32[]{:S(2)}, u32[]{:S(2)}) collective-permute-start(bf16[4,4,2,32,256]{4,3,2,1,0:T(8,128)(2,1)S(1)} %pad_maximum_fusion.refs_5_), channel_id=1, source_target_pairs={{0,8},{1,9},{2,10},{3,11},{4,12},{5,13},{6,14},{7,15},{8,16},{9,17... | collective-permute-start | bytes 1572872 | tf_op jit(solution)/shard_map/ppermute | solution.py:47
  28.6 17.6 %collective-permute-start.15 = (bf16[4,4,2,32,256]{4,3,2,1,0:T(8,128)(2,1)S(1)}, bf16[4,4,2,32,256]{4,3,2,1,0:T(8,128)(2,1)}, u32[]{:S(2)}, u32[]{:S(2)}) collective-permute-start(bf16[4,4,2,32,256]{4,3,2,1,0:T(8,128)(2,1)S(1)} %pad_maximum_fusion.1.refs_4_), channel_id=1, source_target_pairs={{0,24},{1,25},{2,26},{3,27},{4,28},{5,29},{6,30},{7,31},{8,0},{9,1... | collective-permute-start | bytes 1572872 | tf_op jit(solution)/shard_map/ppermute | solution.py:47
  30.6 21.1 %collective-permute-start.14 = (bf16[4,4,2,32,256]{4,3,2,1,0:T(8,128)(2,1)}, bf16[4,4,2,32,256]{4,3,2,1,0:T(8,128)(2,1)S(1)}, u32[]{:S(2)}, u32[]{:S(2)}) collective-permute-start(bf16[4,4,2,32,256]{4,3,2,1,0:T(8,128)(2,1)} %collective-permute-done.13.refs_4_), channel_id=1, source_target_pairs={{0,8},{1,9},{2,10},{3,11},{4,12},{5,13},{6,14},{7,15},{8,16},{9,17... | collective-permute-start | bytes 1572872 | tf_op jit(solution)/shard_map/ppermute | solution.py:47
  31.5 25.7 %collective-permute-start.9 = (bf16[4,4,2,32,256]{4,3,2,1,0:T(8,128)(2,1)}, bf16[4,4,2,32,256]{4,3,2,1,0:T(8,128)(2,1)S(1)}, u32[]{:S(2)}, u32[]{:S(2)}) collective-permute-start(bf16[4,4,2,32,256]{4,3,2,1,0:T(8,128)(2,1)} %collective-permute-done.8.refs_5_), channel_id=1, source_target_pairs={{0,24},{1,25},{2,26},{3,27},{4,28},{5,29},{6,30},{7,31},{8,0},{9,1... | collective-permute-start | bytes 1572872 | tf_op jit(solution)/shard_map/ppermute | solution.py:47
  33.8 1.6 %copy-start.1 = (bf16[2,2048,256]{2,1,0:T(8,128)(2,1)S(1)}, bf16[2,2048,256]{2,1,0:T(8,128)(2,1)}, u32[]{:S(2)}) copy-start(bf16[2,2048,256]{2,1,0:T(8,128)(2,1)} %refs_1_.9) | copy-start | bytes 6291460
  62.8 7.1 %collective-permute-start.17 = (bf16[64,2048]{1,0:T(8,128)(2,1)S(1)}, bf16[64,2048]{1,0:T(8,128)(2,1)S(1)}, u32[]{:S(2)}, u32[]{:S(2)}) collective-permute-start(bf16[64,2048]{1,0:T(8,128)(2,1)S(1)} %get-tuple-element.12), channel_id=1, source_target_pairs={{0,32},{1,33},{2,34},{3,35},{4,36},{5,37},{6,38},{7,39},{8,40},{9,... | collective-permute-start | bytes 786440 | tf_op jit(solution)/shard_map/ppermute | solution.py:47
  69.9 10.5 %collective-permute-start.18 = (bf16[16,2048]{1,0:T(8,128)(2,1)S(1)}, bf16[16,2048]{1,0:T(8,128)(2,1)S(1)}, u32[]{:S(2)}, u32[]{:S(2)}) collective-permute-start(bf16[16,2048]{1,0:T(8,128)(2,1)S(1)} %get-tuple-element.14), channel_id=1, source_target_pairs={{0,64},{1,65},{2,66},{3,67},{4,68},{5,69},{6,70},{7,71},{8,72},{9,... | collective-permute-start | bytes 196616 | tf_op jit(solution)/shard_map/ppermute | solution.py:47
  73.0 9.3 %collective-permute-start.19 = (bf16[16,2048]{1,0:T(8,128)(2,1)S(1)}, bf16[16,2048]{1,0:T(8,128)(2,1)S(1)}, u32[]{:S(2)}, u32[]{:S(2)}) collective-permute-start(bf16[16,2048]{1,0:T(8,128)(2,1)S(1)} %get-tuple-element.15), channel_id=1, source_target_pairs={{0,128},{1,129},{2,130},{3,131},{4,132},{5,133},{6,134},{7,135},{8... | collective-permute-start | bytes 196616 | tf_op jit(solution)/shard_map/ppermute | solution.py:47
  78.0 7.2 %collective-permute-start.20 = (bf16[16,2048]{1,0:T(8,128)(2,1)S(1)}, bf16[16,2048]{1,0:T(8,128)(2,1)S(1)}, u32[]{:S(2)}, u32[]{:S(2)}) collective-permute-start(bf16[16,2048]{1,0:T(8,128)(2,1)S(1)} %get-tuple-element.16), channel_id=1, source_target_pairs={{0,192},{1,193},{2,194},{3,195},{4,196},{5,197},{6,198},{7,199},{8... | collective-permute-start | bytes 196616 | tf_op jit(solution)/shard_map/ppermute | solution.py:47

commit v3 on v2

v3 whole, which is shorter than its diff:
```python
import functools

import jax
import jax.numpy as jnp
from jax import lax
from jax.experimental import pallas as pl
from jax.experimental.pallas import tpu as pltpu
from jax.sharding import PartitionSpec as P

Q = 128
NX, NZ, NY = 4, 2, 4
NH, NC = 4, 2
BLOCK = 64
ORDER = (0, 3, 1, 2)
BF16 = jnp.bfloat16
F32 = jnp.float32
AXES = ("layer", "tok")
SMALL = pltpu.CompilerParams(vmem_limit_bytes=4 * 1024 * 1024)
SMEM = pl.BlockSpec(memory_space=pltpu.SMEM)
VMEM = pl.BlockSpec(memory_space=pltpu.VMEM)


def moves(step):
    pairs = []
    for h in range(NH):
        for c in range(NC):
            for x in range(NX):
                for z in range(NZ):
                    for y in range(NY):
                        to = step(h, c, x, z, y)
                        here, there = (
                            (((i[0] % NH * NC + i[1] % NC) * NX + i[2] % NX) * NZ + i[3] % NZ) * NY
                            + i[4] % NY
                            for i in ((h, c, x, z, y), to)
                        )
                        pairs.append((here, there))
    return pairs


def along_x(d):
    return moves(lambda h, c, x, z, y: (h, c, x + d, z, y))


def along_y(d):
    return moves(lambda h, c, x, z, y: (h, c, x, z, y + d))


def along_z(d):
    return moves(lambda h, c, x, z, y: (h + d, c, x, z, y))


def send(value, pairs):
    return lax.ppermute(value, AXES, pairs)


def prepare_kernel(layer_ref, tok_ref, ids_ref, query_ref, label_ref, turned):
    core, z_hi = layer_ref[0] % 2, layer_ref[0] // 2
    x, z, y = tok_ref[0] // 8, tok_ref[0] // 4 % 2, tok_ref[0] % 4
    ids = ids_ref[...]
    turned[0:16] = ids
    turned[16:32] = pltpu.roll(ids, 64, 1)
    lane = lax.broadcasted_iota(jnp.int32, (1, 128), 1)
    for row, far in enumerate(ORDER):
        for half in range(2):
            for pair in range(2):
                got = []
                for n in range(2):
                    near = ORDER[2 * pair + n]
                    p, q = (far, near) if half == 0 else (near, far)
                    tok = (x + p) % 4 * 8 + (z + half) % 2 * 4 + (y + q) % 4
                    turn = (tok + n) % 2
                    got.append(turned[pl.ds(turn * 16 + tok // 2, 1), :])
                at = 256 * half + 128 * pair
                query_ref[row : row + 1, at : at + 128] = jnp.where(lane < 64, got[0], got[1])
    r = lax.broadcasted_iota(jnp.int32, (Q, 1), 0)
    owner = jnp.where(r < 64, core, 1 - core)
    label_ref[...] = (z_hi + (r % 64) // 16) % 4 * 32 + owner * 16 + r % 16


def prepare(layer, tok, segment_ids):
    return pl.pallas_call(
        prepare_kernel,
        in_specs=[SMEM, SMEM, VMEM],
        out_specs=(VMEM, VMEM),
        out_shape=(
            jax.ShapeDtypeStruct((4, 2 * 4 * BLOCK), jnp.int32),
            jax.ShapeDtypeStruct((Q, 1), jnp.int32),
        ),
        scratch_shapes=[pltpu.VMEM((32, 128), jnp.int32)],
        compiler_params=SMALL,
    )(layer.reshape(1), tok.reshape(1), segment_ids.reshape(16, 128))


def chunk_kernel(pieces, first, last, n_blocks, ids_ref, labels_ref, ta_ref, tg_ref, *refs):
    blocks, rest = refs[:n_blocks], refs[n_blocks:]
    trains = (ta_ref, tg_ref)
    width = 4 * BLOCK
    tile = 1024
    ids = jnp.concatenate(
        [ids_ref[r : r + 1, width * h : width * h + width] for r, h in pieces], 1
    )
    sel = (labels_ref[...] == ids).astype(F32).astype(BF16)
    nt = (((1,), (1,)), ((), ()))
    outs = rest if first else rest[1:]
    for j in range(ta_ref.shape[1] // tile):
        cols = slice(j * tile, (j + 1) * tile)
        prods = []
        for layer in range(2):
            grams = []
            for k in range(2):
                test = jnp.concatenate([b[:, k, layer].reshape(width, 256) for b in blocks], 0)
                grams.append(
                    lax.dot_general(test, trains[k][layer, cols], nt, preferred_element_type=F32)
                )
            prods.append((grams[0] * grams[1]).astype(BF16))
        part = jnp.dot(
            jnp.concatenate([sel] * 2, 1), jnp.concatenate(prods, 0), preferred_element_type=F32
        )
        if not first:
            part = part + rest[0][:, cols]
        if last:
            outs[0][:, cols] = part[: Q // 2]
            outs[1][:, cols] = part[Q // 2 :].astype(BF16)
        else:
            outs[0][:, cols] = part


def chunk(pieces, blocks, acc, last, ids, labels, trains):
    first = acc is None
    rows = trains[0].shape[1]
    args = [ids, labels, *trains, *blocks] + ([] if first else [acc])
    if last:
        out_shape = (
            jax.ShapeDtypeStruct((Q // 2, rows), F32),
            jax.ShapeDtypeStruct((Q // 2, rows), BF16),
        )
    else:
        out_shape = jax.ShapeDtypeStruct((Q, rows), F32)
    s_rows = 4 * BLOCK * len(blocks)
    return pl.pallas_call(
        functools.partial(chunk_kernel, pieces, first, last, len(blocks)),
        in_specs=[VMEM] * len(args),
        out_specs=(VMEM, VMEM) if last else VMEM,
        out_shape=out_shape,
        compiler_params=pltpu.CompilerParams(vmem_limit_bytes=16 * 1024 * 1024),
        cost_estimate=pl.CostEstimate(
            flops=2 * 2 * s_rows * rows * (2 * 256 + Q),
            bytes_accessed=1024 * 1024,
            transcendentals=0,
        ),
    )(*args)


def merge_kernel(keep_ref, got_ref, own_ref, *send_refs):
    own_ref[...] = keep_ref[0:16] + got_ref[0:16].astype(F32)
    for k, ref in enumerate(send_refs, 1):
        rows = slice(16 * k, 16 * k + 16)
        ref[...] = (keep_ref[rows] + got_ref[rows].astype(F32)).astype(BF16)


def merge(keep, got):
    rows = keep.shape[1]
    part = jax.ShapeDtypeStruct((16, rows), BF16)
    return pl.pallas_call(
        merge_kernel,
        in_specs=[VMEM] * 2,
        out_specs=(VMEM,) * 4,
        out_shape=(jax.ShapeDtypeStruct((16, rows), F32), part, part, part),
        compiler_params=SMALL,
    )(keep, got)


def total_kernel(own_ref, *refs):
    total = own_ref[...]
    for ref in refs[:-1]:
        total = total + ref[...].astype(F32)
    refs[-1][...] = total


def total(own, parts):
    return pl.pallas_call(
        total_kernel,
        in_specs=[VMEM] * 4,
        out_specs=VMEM,
        out_shape=jax.ShapeDtypeStruct(own.shape, F32),
        compiler_params=SMALL,
    )(own, *parts)


def on_device(train_act, train_grad, test_act, test_grad, segment_ids):
    layer, tok = lax.axis_index("layer"), lax.axis_index("tok")
    sibling = moves(lambda h, c, x, z, y: (h, 1 - c, x, z, y))
    partner = moves(lambda h, c, x, z, y: (h, c, x, 1 - z, y))

    block = jnp.stack([test_act, test_grad])
    other = send(block, partner)
    ids, labels = prepare(layer, tok, segment_ids)
    low = jnp.stack([block] + [send(block, along_y(d)) for d in (1, -1, 2)])
    other, ids, labels = lax.optimization_barrier((other, ids, labels))
    high = jnp.stack([other] + [send(other, along_x(d)) for d in (1, -1, 2)])

    lows = [low] + [send(low, along_x(d)) for d in (1, -1, 2)]
    highs = [high] + [send(high, along_y(d)) for d in (1, -1, 2)]
    run = functools.partial(chunk, ids=ids, labels=labels, trains=(train_act, train_grad))
    acc = run(((0, 0),), lows[:1], None, False)
    acc = run(((0, 1),), highs[:1], acc, False)
    acc = run(((1, 0),), lows[1:2], acc, False)
    acc = run(((2, 0),), lows[2:3], acc, False)
    acc = run(((1, 1),), highs[1:2], acc, False)
    acc = run(((2, 1),), highs[2:3], acc, False)
    acc = run(((3, 0),), lows[3:], acc, False)
    keep, give = run(((3, 1),), highs[3:], acc, True)

    own, *parts = merge(keep, send(give, sibling))
    parts = [send(parts[k - 1], along_z(k)) for k in (2, 1, 3)]
    return total(own, parts)


def solution(mesh):
    placed = (
        P("layer", "tok", None),
        P("layer", "tok", None),
        P("layer", "tok", None),
        P("layer", "tok", None),
        P(),
    )
    return jax.shard_map(
        on_device, mesh=mesh, in_specs=placed, out_specs=P("layer", "tok"), check_vma=False
    )
```

time: 86.2 us -> 67.3 us (0.78)
  Pallas kernels: 28 us -> 14.8 us
  waiting for transfers between devices: 16.2 us -> 12.3 us
  local copies, waits for them, and re-layouts: 4.4 us -> 2.29 us
    pallas_call x6 -> x9, Pallas kernels: 27.3 us -> 14 us  [the longest x8 13.8 us: chunk(): pl.pallas_call(functools.partial(chunk_kernel, pieces, first, last, len(b...]
    ppermute x21 -> x17, waiting for transfers between devices: 16.2 us -> 12.3 us  [send(): return lax.ppermute(value, AXES, pairs)]
    unnamed x8 -> x6, local copies, waits for them, and re-layouts: 3.27 us -> 2.29 us
    ppermute x21 -> x17, starting transfers between devices: 35.7 us -> 36.5 us  [send(): return lax.ppermute(value, AXES, pairs)]
  transfers between devices with their start and end apart: 21 -> 17, of which waited for: 10 -> 6; matrix products, arithmetic and copies ran while one was open for 3% -> 0% of each run, Pallas kernels for 25% -> 18%
where the time goes in v3:
time: 67.3 us; the launch traced here: 67.2 us
  starting transfers between devices  36.5 us (54%)
  Pallas kernels  14.8 us (22%)
  waiting for transfers between devices  12.3 us (18%)
  local copies, waits for them, and re-layouts  2.29 us (3%)
  other arithmetic  1.17 us (2%)
    ppermute x17, starting transfers between devices, send(): return lax.ppermute(value, AXES, pairs)  36.5 us
    pallas_call x8, Pallas kernels, chunk(): pl.pallas_call(functools.partial(chunk_kernel, pieces, first, last, len(b...  13.8 us
    ppermute x17, waiting for transfers between devices, send(): return lax.ppermute(value, AXES, pairs)  12.3 us
    unnamed x6, local copies, waits for them, and re-layouts  2.29 us
  transfers between devices with their start and end apart: 17, of which 6 were waited for; matrix products, arithmetic and copies ran while one was open for 0% of the time, Pallas kernels for 18%

profile of v3, /device:TPU:1, one launch (start us, length us, event | category | flops | bytes accessed | tf_op | source)
XLA Modules:
  0.0 67.2 jit_solution(12201010908532556337)
XLA Ops:
  0.0 1.0 %fusion = (bf16[1,2,2,64,256]{4,3,2,1,0:T(8,128)(2,1)S(1)}, bf16[2,2,64,256]{3,2,1,0:T(8,128)(2,1)S(1)}) fusion(bf16[1,2,64,256]{3,2,1,0:T(8,128)(2,1)} %bitcast.22, bf16[1,2,64,256]{3,2,1,0:T(8,128)(2,1)} %bitcast.23), kind=kLoop, calls=%fused_computation.3 | loop fusion | flops 65536 | bytes 393216 | tf_op jit(solution)/shard_map/stack | solution.py:198
  1.0 2.6 %collective-permute-start = (bf16[2,2,64,256]{3,2,1,0:T(8,128)(2,1)S(1)}, bf16[2,2,64,256]{3,2,1,0:T(8,128)(2,1)S(1)}, u32[]{:S(2)}, u32[]{:S(2)}) collective-permute-start(bf16[2,2,64,256]{3,2,1,0:T(8,128)(2,1)S(1)} %get-tuple-element.28), channel_id=1, source_target_pairs={{0,4},{1,5},{2,6},{3,7},{4,0},{5,1},{6,2},{7,3},{8,12},{9,13},{10,... | collective-permute-start | bytes 393224 | tf_op jit(solution)/shard_map/ppermute | solution.py:53
  3.6 1.3 %collective-permute-start.5 = (bf16[2,2,64,256]{3,2,1,0:T(8,128)(2,1)S(1)}, bf16[2,2,64,256]{3,2,1,0:T(8,128)(2,1)S(1)}, u32[]{:S(2)}, u32[]{:S(2)}) collective-permute-start(bf16[2,2,64,256]{3,2,1,0:T(8,128)(2,1)S(1)} %get-tuple-element.28), channel_id=1, source_target_pairs={{0,1},{1,2},{2,3},{3,0},{4,5},{5,6},{6,7},{7,4},{8,9},{9,10},{10,1... | collective-permute-start | bytes 393224 | tf_op jit(solution)/shard_map/ppermute | solution.py:53
  4.9 1.4 %collective-permute-start.6 = (bf16[2,2,64,256]{3,2,1,0:T(8,128)(2,1)S(1)}, bf16[2,2,64,256]{3,2,1,0:T(8,128)(2,1)S(1)}, u32[]{:S(2)}, u32[]{:S(2)}) collective-permute-start(bf16[2,2,64,256]{3,2,1,0:T(8,128)(2,1)S(1)} %get-tuple-element.28), channel_id=1, source_target_pairs={{0,3},{1,0},{2,1},{3,2},{4,7},{5,4},{6,5},{7,6},{8,11},{9,8},{10,9... | collective-permute-start | bytes 393224 | tf_op jit(solution)/shard_map/ppermute | solution.py:53
  6.3 1.6 %collective-permute-start.7 = (bf16[2,2,64,256]{3,2,1,0:T(8,128)(2,1)S(1)}, bf16[2,2,64,256]{3,2,1,0:T(8,128)(2,1)S(1)}, u32[]{:S(2)}, u32[]{:S(2)}) collective-permute-start(bf16[2,2,64,256]{3,2,1,0:T(8,128)(2,1)S(1)} %get-tuple-element.28), channel_id=1, source_target_pairs={{0,2},{1,3},{2,0},{3,1},{4,6},{5,7},{6,4},{7,5},{8,10},{9,11},{10,... | collective-permute-start | bytes 393224 | tf_op jit(solution)/shard_map/ppermute | solution.py:53
  8.9 1.3 %collective-permute-start.1 = (bf16[2,2,64,256]{3,2,1,0:T(8,128)(2,1)S(1)}, bf16[2,2,64,256]{3,2,1,0:T(8,128)(2,1)S(1)}, u32[]{:S(2)}, u32[]{:S(2)}) collective-permute-start(bf16[2,2,64,256]{3,2,1,0:T(8,128)(2,1)S(1)} %collective-permute-done), channel_id=1, source_target_pairs={{0,8},{1,9},{2,10},{3,11},{4,12},{5,13},{6,14},{7,15},{8,16},{9,17... | collective-permute-start | bytes 393224 | tf_op jit(solution)/shard_map/ppermute | solution.py:53
  10.2 1.5 %collective-permute-start.2 = (bf16[2,2,64,256]{3,2,1,0:T(8,128)(2,1)S(1)}, bf16[2,2,64,256]{3,2,1,0:T(8,128)(2,1)S(1)}, u32[]{:S(2)}, u32[]{:S(2)}) collective-permute-start(bf16[2,2,64,256]{3,2,1,0:T(8,128)(2,1)S(1)} %collective-permute-done), channel_id=1, source_target_pairs={{0,24},{1,25},{2,26},{3,27},{4,28},{5,29},{6,30},{7,31},{8,0},{9,1... | collective-permute-start | bytes 393224 | tf_op jit(solution)/shard_map/ppermute | solution.py:53
  11.7 1.5 %collective-permute-start.3 = (bf16[2,2,64,256]{3,2,1,0:T(8,128)(2,1)S(1)}, bf16[2,2,64,256]{3,2,1,0:T(8,128)(2,1)S(1)}, u32[]{:S(2)}, u32[]{:S(2)}) collective-permute-start(bf16[2,2,64,256]{3,2,1,0:T(8,128)(2,1)S(1)} %collective-permute-done), channel_id=1, source_target_pairs={{0,16},{1,17},{2,18},{3,19},{4,20},{5,21},{6,22},{7,23},{8,24},{9,... | collective-permute-start | bytes 393224 | tf_op jit(solution)/shard_map/ppermute | solution.py:53
  13.3 1.3 %collective-permute-start.12 = (bf16[4,2,2,64,256]{4,3,2,1,0:T(8,128)(2,1)S(1)}, bf16[4,2,2,64,256]{4,3,2,1,0:T(8,128)(2,1)S(1)}, u32[]{:S(2)}, u32[]{:S(2)}) collective-permute-start(bf16[4,2,2,64,256]{4,3,2,1,0:T(8,128)(2,1)S(1)} %pad_maximum_fusion.1.refs_0_), channel_id=1, source_target_pairs={{0,8},{1,9},{2,10},{3,11},{4,12},{5,13},{6,14},{7,15},{8,16},{9,17... | collective-permute-start | bytes 1572872 | tf_op jit(solution)/shard_map/ppermute | solution.py:53
  14.6 1.5 %collective-permute-start.11 = (bf16[4,2,2,64,256]{4,3,2,1,0:T(8,128)(2,1)S(1)}, bf16[4,2,2,64,256]{4,3,2,1,0:T(8,128)(2,1)S(1)}, u32[]{:S(2)}, u32[]{:S(2)}) collective-permute-start(bf16[4,2,2,64,256]{4,3,2,1,0:T(8,128)(2,1)S(1)} %pad_maximum_fusion.1.refs_0_), channel_id=1, source_target_pairs={{0,24},{1,25},{2,26},{3,27},{4,28},{5,29},{6,30},{7,31},{8,0},{9,1... | collective-permute-start | bytes 1572872 | tf_op jit(solution)/shard_map/ppermute | solution.py:53
  16.1 2.1 %collective-permute-done.3 = bf16[2,2,64,256]{3,2,1,0:T(8,128)(2,1)S(1)} collective-permute-done((bf16[2,2,64,256]{3,2,1,0:T(8,128)(2,1)S(1)}, bf16[2,2,64,256]{3,2,1,0:T(8,128)(2,1)S(1)}, u32[]{:S(2)}, u32[]{:S(2)}) %collective-permute-start.3) | collective-permute-done | bytes 131104 | tf_op jit(solution)/shard_map/ppermute | solution.py:53
  18.7 1.1 %collective-permute-start.8 = (bf16[4,2,2,64,256]{4,3,2,1,0:T(8,128)(2,1)S(1)}, bf16[4,2,2,64,256]{4,3,2,1,0:T(8,128)(2,1)S(1)}, u32[]{:S(2)}, u32[]{:S(2)}) collective-permute-start(bf16[4,2,2,64,256]{4,3,2,1,0:T(8,128)(2,1)S(1)} %pad_maximum_fusion.1.refs_0_), channel_id=1, source_target_pairs={{0,16},{1,17},{2,18},{3,19},{4,20},{5,21},{6,22},{7,23},{8,24},{9,... | collective-permute-start | bytes 1572872 | tf_op jit(solution)/shard_map/ppermute | solution.py:53
  19.8 2.3 %collective-permute-start.9 = (bf16[4,2,2,64,256]{4,3,2,1,0:T(8,128)(2,1)S(1)}, bf16[4,2,2,64,256]{4,3,2,1,0:T(8,128)(2,1)S(1)}, u32[]{:S(2)}, u32[]{:S(2)}) collective-permute-start(bf16[4,2,2,64,256]{4,3,2,1,0:T(8,128)(2,1)S(1)} %pad_maximum_fusion.refs_0_), channel_id=1, source_target_pairs={{0,3},{1,0},{2,1},{3,2},{4,7},{5,4},{6,5},{7,6},{8,11},{9,8},{10,9... | collective-permute-start | bytes 1572872 | tf_op jit(solution)/shard_map/ppermute | solution.py:53
  22.1 1.6 %copy-done.1 = bf16[2,2048,256]{2,1,0:T(8,128)(2,1)S(1)} copy-done((bf16[2,2048,256]{2,1,0:T(8,128)(2,1)S(1)}, bf16[2,2048,256]{2,1,0:T(8,128)(2,1)}, u32[]{:S(2)}) %copy-start.1) | copy-done | bytes 2097176
  23.7 1.7 %shard_map.56.refs_1_ = f32[128,2048]{1,0:T(8,128)S(1)} custom-call(s32[4,512]{1,0:T(4,128)S(1)} %get-tuple-element.18.ids_ref, s32[128,1]{1,0:T(8,128)S(1)} %get-tuple-element.19.labels_ref, bf16[2,2048,256]{2,1,0:T(8,128)(2,1)S(1)} %copy-done, bf16[2,2048,256]{2,1,0:T(8,128)(2,1)S(1)} %copy-done.1, bf16[4,2,2,64,256]{4,3,2,1,0:T(8,128)(2,1)S(1)} %pad_maximum_fusion.1.refs_0_), custom_call_target="tpu_custom_call" | custom-call | flops 1342177280 | bytes 1048576 | tf_op jit(solution)/shard_map/pallas_call | solution.py:140
  25.4 1.7 %shard_map.57.refs_1_ = f32[128,2048]{1,0:T(8,128)S(1)} custom-call(s32[4,512]{1,0:T(4,128)S(1)} %get-tuple-element.18.ids_ref, s32[128,1]{1,0:T(8,128)S(1)} %get-tuple-element.19.labels_ref, bf16[2,2048,256]{2,1,0:T(8,128)(2,1)S(1)} %copy-done, bf16[2,2048,256]{2,1,0:T(8,128)(2,1)S(1)} %copy-done.1, ...), custom_call_target="tpu_custom_call" | custom-call | flops 1342177280 | bytes 1048576 | tf_op jit(solution)/shard_map/pallas_call | solution.py:140
  27.1 1.7 %collective-permute-done.12.refs_0_ = bf16[4,2,2,64,256]{4,3,2,1,0:T(8,128)(2,1)S(1)} collective-permute-done((bf16[4,2,2,64,256]{4,3,2,1,0:T(8,128)(2,1)S(1)}, bf16[4,2,2,64,256]{4,3,2,1,0:T(8,128)(2,1)S(1)}, u32[]{:S(2)}, u32[]{:S(2)}) %collective-permute-start.12) | collective-permute-done | bytes 524320 | tf_op jit(solution)/shard_map/ppermute | solution.py:53
  28.9 1.3 %collective-permute-start.4 = (bf16[4,2,2,64,256]{4,3,2,1,0:T(8,128)(2,1)S(1)}, bf16[4,2,2,64,256]{4,3,2,1,0:T(8,128)(2,1)S(1)}, u32[]{:S(2)}, u32[]{:S(2)}) collective-permute-start(bf16[4,2,2,64,256]{4,3,2,1,0:T(8,128)(2,1)S(1)} %pad_maximum_fusion.refs_0_), channel_id=1, source_target_pairs={{0,2},{1,3},{2,0},{3,1},{4,6},{5,7},{6,4},{7,5},{8,10},{9,11},{10,... | collective-permute-start | bytes 1572872 | tf_op jit(solution)/shard_map/ppermute | solution.py:53
  30.1 1.7 %shard_map.58.refs_1_ = f32[128,2048]{1,0:T(8,128)S(1)} custom-call(s32[4,512]{1,0:T(4,128)S(1)} %get-tuple-element.18.ids_ref, s32[128,1]{1,0:T(8,128)S(1)} %get-tuple-element.19.labels_ref, bf16[2,2048,256]{2,1,0:T(8,128)(2,1)S(1)} %copy-done, bf16[2,2048,256]{2,1,0:T(8,128)(2,1)S(1)} %copy-done.1, ...), custom_call_target="tpu_custom_call" | custom-call | flops 1342177280 | bytes 1048576 | tf_op jit(solution)/shard_map/pallas_call | solution.py:140
  31.9 1.7 %shard_map.59.refs_1_ = f32[128,2048]{1,0:T(8,128)S(1)} custom-call(s32[4,512]{1,0:T(4,128)S(1)} %get-tuple-element.18.ids_ref, s32[128,1]{1,0:T(8,128)S(1)} %get-tuple-element.19.labels_ref, bf16[2,2048,256]{2,1,0:T(8,128)(2,1)S(1)} %copy-done, bf16[2,2048,256]{2,1,0:T(8,128)(2,1)S(1)} %copy-done.1, ...), custom_call_target="tpu_custom_call" | custom-call | flops 1342177280 | bytes 1048576 | tf_op jit(solution)/shard_map/pallas_call | solution.py:140
  33.6 1.7 %shard_map.60.refs_1_ = f32[128,2048]{1,0:T(8,128)S(1)} custom-call(s32[4,512]{1,0:T(4,128)S(1)} %get-tuple-element.18.ids_ref, s32[128,1]{1,0:T(8,128)S(1)} %get-tuple-element.19.labels_ref, bf16[2,2048,256]{2,1,0:T(8,128)(2,1)S(1)} %copy-done, bf16[2,2048,256]{2,1,0:T(8,128)(2,1)S(1)} %copy-done.1, ...), custom_call_target="tpu_custom_call" | custom-call | flops 1342177280 | bytes 1048576 | tf_op jit(solution)/shard_map/pallas_call | solution.py:140
  35.4 1.7 %shard_map.61.refs_1_ = f32[128,2048]{1,0:T(8,128)S(1)} custom-call(s32[4,512]{1,0:T(4,128)S(1)} %get-tuple-element.18.ids_ref, s32[128,1]{1,0:T(8,128)S(1)} %get-tuple-element.19.labels_ref, bf16[2,2048,256]{2,1,0:T(8,128)(2,1)S(1)} %copy-done, bf16[2,2048,256]{2,1,0:T(8,128)(2,1)S(1)} %copy-done.1, ...), custom_call_target="tpu_custom_call" | custom-call | flops 1342177280 | bytes 1048576 | tf_op jit(solution)/shard_map/pallas_call | solution.py:140
  37.1 3.8 %collective-permute-done.8.refs_0_ = bf16[4,2,2,64,256]{4,3,2,1,0:T(8,128)(2,1)S(1)} collective-permute-done((bf16[4,2,2,64,256]{4,3,2,1,0:T(8,128)(2,1)S(1)}, bf16[4,2,2,64,256]{4,3,2,1,0:T(8,128)(2,1)S(1)}, u32[]{:S(2)}, u32[]{:S(2)}) %collective-permute-start.8) | collective-permute-done | bytes 524320 | tf_op jit(solution)/shard_map/ppermute | solution.py:53
  40.9 1.7 %shard_map.62.refs_1_ = f32[128,2048]{1,0:T(8,128)S(1)} custom-call(s32[4,512]{1,0:T(4,128)S(1)} %get-tuple-element.18.ids_ref, s32[128,1]{1,0:T(8,128)S(1)} %get-tuple-element.19.labels_ref, bf16[2,2048,256]{2,1,0:T(8,128)(2,1)S(1)} %copy-done, bf16[2,2048,256]{2,1,0:T(8,128)(2,1)S(1)} %copy-done.1, ...), custom_call_target="tpu_custom_call" | custom-call | flops 1342177280 | bytes 1048576 | tf_op jit(solution)/shard_map/pallas_call | solution.py:140
  42.7 1.7 %shard_map.63 = (f32[64,2048]{1,0:T(8,128)S(1)}, bf16[64,2048]{1,0:T(8,128)(2,1)S(1)}) custom-call(s32[4,512]{1,0:T(4,128)S(1)} %get-tuple-element.18.ids_ref, s32[128,1]{1,0:T(8,128)S(1)} %get-tuple-element.19.labels_ref, bf16[2,2048,256]{2,1,0:T(8,128)(2,1)S(1)} %copy-done, bf16[2,2048,256]{2,1,0:T(8,128)(2,1)S(1)} %copy-done.1, ...), custom_call_target="tpu_custom_call" | custom-call | flops 1342177280 | bytes 1048576 | tf_op jit(solution)/shard_map/pallas_call | solution.py:140
  44.4 7.7 %collective-permute-start.13 = (bf16[64,2048]{1,0:T(8,128)(2,1)S(1)}, bf16[64,2048]{1,0:T(8,128)(2,1)S(1)}, u32[]{:S(2)}, u32[]{:S(2)}) collective-permute-start(bf16[64,2048]{1,0:T(8,128)(2,1)S(1)} %get-tuple-element.22), channel_id=1, source_target_pairs={{0,32},{1,33},{2,34},{3,35},{4,36},{5,37},{6,38},{7,39},{8,40},{9,... | collective-permute-start | bytes 786440 | tf_op jit(solution)/shard_map/ppermute | solution.py:53
  52.1 1.2 %collective-permute-done.13.got_ref = bf16[64,2048]{1,0:T(8,128)(2,1)S(1)} collective-permute-done((bf16[64,2048]{1,0:T(8,128)(2,1)S(1)}, bf16[64,2048]{1,0:T(8,128)(2,1)S(1)}, u32[]{:S(2)}, u32[]{:S(2)}) %collective-permute-start.13) | collective-permute-done | bytes 262176 | tf_op jit(solution)/shard_map/ppermute | solution.py:53
  53.4 6.1 %collective-permute-start.14 = (bf16[16,2048]{1,0:T(8,128)(2,1)S(1)}, bf16[16,2048]{1,0:T(8,128)(2,1)S(1)}, u32[]{:S(2)}, u32[]{:S(2)}) collective-permute-start(bf16[16,2048]{1,0:T(8,128)(2,1)S(1)} %get-tuple-element.24), channel_id=1, source_target_pairs={{0,128},{1,129},{2,130},{3,131},{4,132},{5,133},{6,134},{7,135},{8... | collective-permute-start | bytes 196616 | tf_op jit(solution)/shard_map/ppermute | solution.py:53
  59.5 1.2 %collective-permute-start.15 = (bf16[16,2048]{1,0:T(8,128)(2,1)S(1)}, bf16[16,2048]{1,0:T(8,128)(2,1)S(1)}, u32[]{:S(2)}, u32[]{:S(2)}) collective-permute-start(bf16[16,2048]{1,0:T(8,128)(2,1)S(1)} %get-tuple-element.25), channel_id=1, source_target_pairs={{0,64},{1,65},{2,66},{3,67},{4,68},{5,69},{6,70},{7,71},{8,72},{9,... | collective-permute-start | bytes 196616 | tf_op jit(solution)/shard_map/ppermute | solution.py:53
  60.7 2.4 %collective-permute-start.16 = (bf16[16,2048]{1,0:T(8,128)(2,1)S(1)}, bf16[16,2048]{1,0:T(8,128)(2,1)S(1)}, u32[]{:S(2)}, u32[]{:S(2)}) collective-permute-start(bf16[16,2048]{1,0:T(8,128)(2,1)S(1)} %get-tuple-element.26), channel_id=1, source_target_pairs={{0,192},{1,193},{2,194},{3,195},{4,196},{5,197},{6,198},{7,199},{8... | collective-permute-start | bytes 196616 | tf_op jit(solution)/shard_map/ppermute | solution.py:53
  63.0 1.9 %collective-permute-done.15.refs_1_ = bf16[16,2048]{1,0:T(8,128)(2,1)S(1)} collective-permute-done((bf16[16,2048]{1,0:T(8,128)(2,1)S(1)}, bf16[16,2048]{1,0:T(8,128)(2,1)S(1)}, u32[]{:S(2)}, u32[]{:S(2)}) %collective-permute-start.15) | collective-permute-done | bytes 65568 | tf_op jit(solution)/shard_map/ppermute | solution.py:53
  64.9 1.6 %collective-permute-done.16.refs_2_ = bf16[16,2048]{1,0:T(8,128)(2,1)S(1)} collective-permute-done((bf16[16,2048]{1,0:T(8,128)(2,1)S(1)}, bf16[16,2048]{1,0:T(8,128)(2,1)S(1)}, u32[]{:S(2)}, u32[]{:S(2)}) %collective-permute-start.16) | collective-permute-done | bytes 65568 | tf_op jit(solution)/shard_map/ppermute | solution.py:53
  (22 shorter events, 2.4 us)
Async XLA Ops:
  0.0 22.1 %copy-start = (bf16[2,2048,256]{2,1,0:T(8,128)(2,1)S(1)}, bf16[2,2048,256]{2,1,0:T(8,128)(2,1)}, u32[]{:S(2)}) copy-start(bf16[2,2048,256]{2,1,0:T(8,128)(2,1)} %ta_ref.15) | copy-start | bytes 6291460
  1.0 7.9 %collective-permute-start = (bf16[2,2,64,256]{3,2,1,0:T(8,128)(2,1)S(1)}, bf16[2,2,64,256]{3,2,1,0:T(8,128)(2,1)S(1)}, u32[]{:S(2)}, u32[]{:S(2)}) collective-permute-start(bf16[2,2,64,256]{3,2,1,0:T(8,128)(2,1)S(1)} %get-tuple-element.28), channel_id=1, source_target_pairs={{0,4},{1,5},{2,6},{3,7},{4,0},{5,1},{6,2},{7,3},{8,12},{9,13},{10,... | collective-permute-start | bytes 393224 | tf_op jit(solution)/shard_map/ppermute | solution.py:53
  3.6 8.1 %collective-permute-start.5 = (bf16[2,2,64,256]{3,2,1,0:T(8,128)(2,1)S(1)}, bf16[2,2,64,256]{3,2,1,0:T(8,128)(2,1)S(1)}, u32[]{:S(2)}, u32[]{:S(2)}) collective-permute-start(bf16[2,2,64,256]{3,2,1,0:T(8,128)(2,1)S(1)} %get-tuple-element.28), channel_id=1, source_target_pairs={{0,1},{1,2},{2,3},{3,0},{4,5},{5,6},{6,7},{7,4},{8,9},{9,10},{10,1... | collective-permute-start | bytes 393224 | tf_op jit(solution)/shard_map/ppermute | solution.py:53
  4.9 8.3 %collective-permute-start.6 = (bf16[2,2,64,256]{3,2,1,0:T(8,128)(2,1)S(1)}, bf16[2,2,64,256]{3,2,1,0:T(8,128)(2,1)S(1)}, u32[]{:S(2)}, u32[]{:S(2)}) collective-permute-start(bf16[2,2,64,256]{3,2,1,0:T(8,128)(2,1)S(1)} %get-tuple-element.28), channel_id=1, source_target_pairs={{0,3},{1,0},{2,1},{3,2},{4,7},{5,4},{6,5},{7,6},{8,11},{9,8},{10,9... | collective-permute-start | bytes 393224 | tf_op jit(solution)/shard_map/ppermute | solution.py:53
  6.3 6.9 %collective-permute-start.7 = (bf16[2,2,64,256]{3,2,1,0:T(8,128)(2,1)S(1)}, bf16[2,2,64,256]{3,2,1,0:T(8,128)(2,1)S(1)}, u32[]{:S(2)}, u32[]{:S(2)}) collective-permute-start(bf16[2,2,64,256]{3,2,1,0:T(8,128)(2,1)S(1)} %get-tuple-element.28), channel_id=1, source_target_pairs={{0,2},{1,3},{2,0},{3,1},{4,6},{5,7},{6,4},{7,5},{8,10},{9,11},{10,... | collective-permute-start | bytes 393224 | tf_op jit(solution)/shard_map/ppermute | solution.py:53
  8.0 0.7 %copy-start.2 = (s32[2048]{0:T(1024)S(1)}, s32[2048]{0:T(1024)}, u32[]{:S(2)}) copy-start(s32[2048]{0:T(1024)} %param.9) | copy-start | bytes 24580
  8.9 7.2 %collective-permute-start.1 = (bf16[2,2,64,256]{3,2,1,0:T(8,128)(2,1)S(1)}, bf16[2,2,64,256]{3,2,1,0:T(8,128)(2,1)S(1)}, u32[]{:S(2)}, u32[]{:S(2)}) collective-permute-start(bf16[2,2,64,256]{3,2,1,0:T(8,128)(2,1)S(1)} %collective-permute-done), channel_id=1, source_target_pairs={{0,8},{1,9},{2,10},{3,11},{4,12},{5,13},{6,14},{7,15},{8,16},{9,17... | collective-permute-start | bytes 393224 | tf_op jit(solution)/shard_map/ppermute | solution.py:53
  10.2 5.9 %collective-permute-start.2 = (bf16[2,2,64,256]{3,2,1,0:T(8,128)(2,1)S(1)}, bf16[2,2,64,256]{3,2,1,0:T(8,128)(2,1)S(1)}, u32[]{:S(2)}, u32[]{:S(2)}) collective-permute-start(bf16[2,2,64,256]{3,2,1,0:T(8,128)(2,1)S(1)} %collective-permute-done), channel_id=1, source_target_pairs={{0,24},{1,25},{2,26},{3,27},{4,28},{5,29},{6,30},{7,31},{8,0},{9,1... | collective-permute-start | bytes 393224 | tf_op jit(solution)/shard_map/ppermute | solution.py:53
  11.7 6.5 %collective-permute-start.3 = (bf16[2,2,64,256]{3,2,1,0:T(8,128)(2,1)S(1)}, bf16[2,2,64,256]{3,2,1,0:T(8,128)(2,1)S(1)}, u32[]{:S(2)}, u32[]{:S(2)}) collective-permute-start(bf16[2,2,64,256]{3,2,1,0:T(8,128)(2,1)S(1)} %collective-permute-done), channel_id=1, source_target_pairs={{0,16},{1,17},{2,18},{3,19},{4,20},{5,21},{6,22},{7,23},{8,24},{9,... | collective-permute-start | bytes 393224 | tf_op jit(solution)/shard_map/ppermute | solution.py:53
  13.3 15.5 %collective-permute-start.12 = (bf16[4,2,2,64,256]{4,3,2,1,0:T(8,128)(2,1)S(1)}, bf16[4,2,2,64,256]{4,3,2,1,0:T(8,128)(2,1)S(1)}, u32[]{:S(2)}, u32[]{:S(2)}) collective-permute-start(bf16[4,2,2,64,256]{4,3,2,1,0:T(8,128)(2,1)S(1)} %pad_maximum_fusion.1.refs_0_), channel_id=1, source_target_pairs={{0,8},{1,9},{2,10},{3,11},{4,12},{5,13},{6,14},{7,15},{8,16},{9,17... | collective-permute-start | bytes 1572872 | tf_op jit(solution)/shard_map/ppermute | solution.py:53
  14.6 17.2 %collective-permute-start.11 = (bf16[4,2,2,64,256]{4,3,2,1,0:T(8,128)(2,1)S(1)}, bf16[4,2,2,64,256]{4,3,2,1,0:T(8,128)(2,1)S(1)}, u32[]{:S(2)}, u32[]{:S(2)}) collective-permute-start(bf16[4,2,2,64,256]{4,3,2,1,0:T(8,128)(2,1)S(1)} %pad_maximum_fusion.1.refs_0_), channel_id=1, source_target_pairs={{0,24},{1,25},{2,26},{3,27},{4,28},{5,29},{6,30},{7,31},{8,0},{9,1... | collective-permute-start | bytes 1572872 | tf_op jit(solution)/shard_map/ppermute | solution.py:53
  18.2 15.4 %collective-permute-start.10 = (bf16[4,2,2,64,256]{4,3,2,1,0:T(8,128)(2,1)S(1)}, bf16[4,2,2,64,256]{4,3,2,1,0:T(8,128)(2,1)S(1)}, u32[]{:S(2)}, u32[]{:S(2)}) collective-permute-start(bf16[4,2,2,64,256]{4,3,2,1,0:T(8,128)(2,1)S(1)} %pad_maximum_fusion.refs_0_), channel_id=1, source_target_pairs={{0,1},{1,2},{2,3},{3,0},{4,5},{5,6},{6,7},{7,4},{8,9},{9,10},{10,1... | collective-permute-start | bytes 1572872 | tf_op jit(solution)/shard_map/ppermute | solution.py:53
  18.7 22.2 %collective-permute-start.8 = (bf16[4,2,2,64,256]{4,3,2,1,0:T(8,128)(2,1)S(1)}, bf16[4,2,2,64,256]{4,3,2,1,0:T(8,128)(2,1)S(1)}, u32[]{:S(2)}, u32[]{:S(2)}) collective-permute-start(bf16[4,2,2,64,256]{4,3,2,1,0:T(8,128)(2,1)S(1)} %pad_maximum_fusion.1.refs_0_), channel_id=1, source_target_pairs={{0,16},{1,17},{2,18},{3,19},{4,20},{5,21},{6,22},{7,23},{8,24},{9,... | collective-permute-start | bytes 1572872 | tf_op jit(solution)/shard_map/ppermute | solution.py:53
  19.8 15.5 %collective-permute-start.9 = (bf16[4,2,2,64,256]{4,3,2,1,0:T(8,128)(2,1)S(1)}, bf16[4,2,2,64,256]{4,3,2,1,0:T(8,128)(2,1)S(1)}, u32[]{:S(2)}, u32[]{:S(2)}) collective-permute-start(bf16[4,2,2,64,256]{4,3,2,1,0:T(8,128)(2,1)S(1)} %pad_maximum_fusion.refs_0_), channel_id=1, source_target_pairs={{0,3},{1,0},{2,1},{3,2},{4,7},{5,4},{6,5},{7,6},{8,11},{9,8},{10,9... | collective-permute-start | bytes 1572872 | tf_op jit(solution)/shard_map/ppermute | solution.py:53
  22.1 1.6 %copy-start.1 = (bf16[2,2048,256]{2,1,0:T(8,128)(2,1)S(1)}, bf16[2,2048,256]{2,1,0:T(8,128)(2,1)}, u32[]{:S(2)}) copy-start(bf16[2,2048,256]{2,1,0:T(8,128)(2,1)} %tg_ref.15) | copy-start | bytes 6291460
  28.9 13.8 %collective-permute-start.4 = (bf16[4,2,2,64,256]{4,3,2,1,0:T(8,128)(2,1)S(1)}, bf16[4,2,2,64,256]{4,3,2,1,0:T(8,128)(2,1)S(1)}, u32[]{:S(2)}, u32[]{:S(2)}) collective-permute-start(bf16[4,2,2,64,256]{4,3,2,1,0:T(8,128)(2,1)S(1)} %pad_maximum_fusion.refs_0_), channel_id=1, source_target_pairs={{0,2},{1,3},{2,0},{3,1},{4,6},{5,7},{6,4},{7,5},{8,10},{9,11},{10,... | collective-permute-start | bytes 1572872 | tf_op jit(solution)/shard_map/ppermute | solution.py:53
  44.4 8.9 %collective-permute-start.13 = (bf16[64,2048]{1,0:T(8,128)(2,1)S(1)}, bf16[64,2048]{1,0:T(8,128)(2,1)S(1)}, u32[]{:S(2)}, u32[]{:S(2)}) collective-permute-start(bf16[64,2048]{1,0:T(8,128)(2,1)S(1)} %get-tuple-element.22), channel_id=1, source_target_pairs={{0,32},{1,33},{2,34},{3,35},{4,36},{5,37},{6,38},{7,39},{8,40},{9,... | collective-permute-start | bytes 786440 | tf_op jit(solution)/shard_map/ppermute | solution.py:53
  53.4 9.7 %collective-permute-start.14 = (bf16[16,2048]{1,0:T(8,128)(2,1)S(1)}, bf16[16,2048]{1,0:T(8,128)(2,1)S(1)}, u32[]{:S(2)}, u32[]{:S(2)}) collective-permute-start(bf16[16,2048]{1,0:T(8,128)(2,1)S(1)} %get-tuple-element.24), channel_id=1, source_target_pairs={{0,128},{1,129},{2,130},{3,131},{4,132},{5,133},{6,134},{7,135},{8... | collective-permute-start | bytes 196616 | tf_op jit(solution)/shard_map/ppermute | solution.py:53
  59.5 5.5 %collective-permute-start.15 = (bf16[16,2048]{1,0:T(8,128)(2,1)S(1)}, bf16[16,2048]{1,0:T(8,128)(2,1)S(1)}, u32[]{:S(2)}, u32[]{:S(2)}) collective-permute-start(bf16[16,2048]{1,0:T(8,128)(2,1)S(1)} %get-tuple-element.25), channel_id=1, source_target_pairs={{0,64},{1,65},{2,66},{3,67},{4,68},{5,69},{6,70},{7,71},{8,72},{9,... | collective-permute-start | bytes 196616 | tf_op jit(solution)/shard_map/ppermute | solution.py:53
  60.7 5.8 %collective-permute-start.16 = (bf16[16,2048]{1,0:T(8,128)(2,1)S(1)}, bf16[16,2048]{1,0:T(8,128)(2,1)S(1)}, u32[]{:S(2)}, u32[]{:S(2)}) collective-permute-start(bf16[16,2048]{1,0:T(8,128)(2,1)S(1)} %get-tuple-element.26), channel_id=1, source_target_pairs={{0,192},{1,193},{2,194},{3,195},{4,196},{5,197},{6,198},{7,199},{8... | collective-permute-start | bytes 196616 | tf_op jit(solution)/shard_map/ppermute | solution.py:53

commit v4 on v3

--- a/solution.py
+++ b/solution.py
@@ -11,7 +11,7 @@
 NX, NZ, NY = 4, 2, 4
 NH, NC = 4, 2
 BLOCK = 64
-ORDER = (0, 3, 1, 2)
+ORDER = (0, 2, 3, 1)
 BF16 = jnp.bfloat16
 F32 = jnp.float32
 AXES = ("layer", "tok")
@@ -108,7 +108,7 @@
         for layer in range(2):
             grams = []
             for k in range(2):
-                test = jnp.concatenate([b[:, k, layer].reshape(width, 256) for b in blocks], 0)
+                test = jnp.concatenate([b[:, k, layer].reshape(-1, 256) for b in blocks], 0)
                 grams.append(
                     lax.dot_general(test, trains[k][layer, cols], nt, preferred_element_type=F32)
                 )
@@ -136,7 +136,7 @@
         )
     else:
         out_shape = jax.ShapeDtypeStruct((Q, rows), F32)
-    s_rows = 4 * BLOCK * len(blocks)
+    s_rows = BLOCK * sum(b.shape[0] for b in blocks)
     return pl.pallas_call(
         functools.partial(chunk_kernel, pieces, first, last, len(blocks)),
         in_specs=[VMEM] * len(args),
@@ -194,22 +194,26 @@
 
     block = jnp.stack([test_act, test_grad])
     other = send(block, partner)
+    trains = (train_act, train_grad)
     ids, labels = prepare(layer, tok, segment_ids)
-    low = jnp.stack([block] + [send(block, along_y(d)) for d in (1, -1, 2)])
+    low = jnp.stack([block] + [send(block, along_y(d)) for d in (2, 1, -1)])
     other, ids, labels = lax.optimization_barrier((other, ids, labels))
-    high = jnp.stack([other] + [send(other, along_x(d)) for d in (1, -1, 2)])
-
-    lows = [low] + [send(low, along_x(d)) for d in (1, -1, 2)]
-    highs = [high] + [send(high, along_y(d)) for d in (1, -1, 2)]
-    run = functools.partial(chunk, ids=ids, labels=labels, trains=(train_act, train_grad))
-    acc = run(((0, 0),), lows[:1], None, False)
-    acc = run(((0, 1),), highs[:1], acc, False)
-    acc = run(((1, 0),), lows[1:2], acc, False)
-    acc = run(((2, 0),), lows[2:3], acc, False)
-    acc = run(((1, 1),), highs[1:2], acc, False)
-    acc = run(((2, 1),), highs[2:3], acc, False)
-    acc = run(((3, 0),), lows[3:], acc, False)
-    keep, give = run(((3, 1),), highs[3:], acc, True)
+    run = functools.partial(chunk, ids=ids, labels=labels, trains=trains)
+    acc = run(((0, 0),), (low,), None, False)
+    ring = [send(other, along_x(d)) for d in (2, 1, -1)]
+    ring, acc = lax.optimization_barrier((ring, acc))
+    high = jnp.stack([other] + ring)
+
+    low_prev, low_next = send(low, along_x(1)), send(low, along_x(-1))
+    high_prev, high_next = send(high, along_y(1)), send(high, along_y(-1))
+    low_far = (send(low_prev[:2], along_x(1)), send(low_next[2:], along_x(-1)))
+    high_far = (send(high_prev[:2], along_y(1)), send(high_next[2:], along_y(-1)))
+    acc = run(((0, 1),), (high,), acc, False)
+    acc = run(((2, 0), (3, 0)), (low_prev, low_next), acc, False)
+    high_prev, high_next, acc = lax.optimization_barrier((high_prev, high_next, acc))
+    acc = run(((2, 1), (3, 1)), (high_prev, high_next), acc, False)
+    acc = run(((1, 0),), low_far, acc, False)
+    keep, give = run(((1, 1),), high_far, acc, True)
 
     own, *parts = merge(keep, send(give, sibling))
     parts = [send(parts[k - 1], along_z(k)) for k in (2, 1, 3)]

time: 67.3 us -> 64 us (0.951)
  waiting for transfers between devices: 12.3 us -> 9.52 us
  starting transfers between devices: 36.5 us -> 34.2 us
  local copies, waits for them, and re-layouts: 2.29 us -> 3.95 us
    ppermute x17 -> x19, waiting for transfers between devices: 12.3 us -> 9.52 us  [send(): return lax.ppermute(value, AXES, pairs)]
    ppermute x17 -> x19, starting transfers between devices: 36.5 us -> 34.2 us  [send(): return lax.ppermute(value, AXES, pairs)]
    unnamed x6, local copies, waits for them, and re-layouts: 2.29 us -> 3.88 us
    pallas_call x8 -> x6, Pallas kernels: 13.8 us -> 13.5 us  [chunk(): pl.pallas_call(functools.partial(chunk_kernel, pieces, first, last, len(b...]
  transfers between devices with their start and end apart: 17 -> 19, of which waited for: 6 -> 4; matrix products, arithmetic and copies ran while one was open for 0% -> 0% of each run, Pallas kernels for 18% -> 19%
where the time goes in v4:
time: 64 us; the launch traced here: 63.3 us
  starting transfers between devices  34.2 us (53%)
  Pallas kernels  14.5 us (23%)
  waiting for transfers between devices  9.52 us (15%)
  local copies, waits for them, and re-layouts  3.95 us (6%)
  other arithmetic  1.03 us (2%)
    ppermute x19, starting transfers between devices, send(): return lax.ppermute(value, AXES, pairs)  34.2 us
    pallas_call x6, Pallas kernels, chunk(): pl.pallas_call(functools.partial(chunk_kernel, pieces, first, last, len(b...  13.5 us
    ppermute x19, waiting for transfers between devices, send(): return lax.ppermute(value, AXES, pairs)  9.52 us
    unnamed x6, local copies, waits for them, and re-layouts  3.88 us
  transfers between devices with their start and end apart: 19, of which 4 were waited for; matrix products, arithmetic and copies ran while one was open for 0% of the time, Pallas kernels for 19%

profile of v4, /device:TPU:1, one launch (start us, length us, event | category | flops | bytes accessed | tf_op | source)
XLA Modules:
  0.0 63.3 jit_solution(16562197281816624940)
XLA Ops:
  0.0 0.9 %fusion = (bf16[1,2,2,64,256]{4,3,2,1,0:T(8,128)(2,1)S(1)}, bf16[2,2,64,256]{3,2,1,0:T(8,128)(2,1)S(1)}) fusion(bf16[1,2,64,256]{3,2,1,0:T(8,128)(2,1)} %bitcast.22, bf16[1,2,64,256]{3,2,1,0:T(8,128)(2,1)} %bitcast.23), kind=kLoop, calls=%fused_computation.3 | loop fusion | flops 65536 | bytes 393216 | tf_op jit(solution)/shard_map/stack | solution.py:199
  0.9 2.6 %collective-permute-start = (bf16[2,2,64,256]{3,2,1,0:T(8,128)(2,1)S(1)}, bf16[2,2,64,256]{3,2,1,0:T(8,128)(2,1)S(1)}, u32[]{:S(2)}, u32[]{:S(2)}) collective-permute-start(bf16[2,2,64,256]{3,2,1,0:T(8,128)(2,1)S(1)} %get-tuple-element.42), channel_id=1, source_target_pairs={{0,4},{1,5},{2,6},{3,7},{4,0},{5,1},{6,2},{7,3},{8,12},{9,13},{10,... | collective-permute-start | bytes 393224 | tf_op jit(solution)/shard_map/ppermute | solution.py:53
  3.4 1.3 %collective-permute-start.5 = (bf16[2,2,64,256]{3,2,1,0:T(8,128)(2,1)S(1)}, bf16[2,2,64,256]{3,2,1,0:T(8,128)(2,1)S(1)}, u32[]{:S(2)}, u32[]{:S(2)}) collective-permute-start(bf16[2,2,64,256]{3,2,1,0:T(8,128)(2,1)S(1)} %get-tuple-element.42), channel_id=1, source_target_pairs={{0,1},{1,2},{2,3},{3,0},{4,5},{5,6},{6,7},{7,4},{8,9},{9,10},{10,1... | collective-permute-start | bytes 393224 | tf_op jit(solution)/shard_map/ppermute | solution.py:53
  4.7 2.6 %collective-permute-start.4 = (bf16[2,2,64,256]{3,2,1,0:T(8,128)(2,1)S(1)}, bf16[2,2,64,256]{3,2,1,0:T(8,128)(2,1)S(1)}, u32[]{:S(2)}, u32[]{:S(2)}) collective-permute-start(bf16[2,2,64,256]{3,2,1,0:T(8,128)(2,1)S(1)} %get-tuple-element.42), channel_id=1, source_target_pairs={{0,2},{1,3},{2,0},{3,1},{4,6},{5,7},{6,4},{7,5},{8,10},{9,11},{10,... | collective-permute-start | bytes 393224 | tf_op jit(solution)/shard_map/ppermute | solution.py:53
  7.4 1.1 %collective-permute-start.6 = (bf16[2,2,64,256]{3,2,1,0:T(8,128)(2,1)S(1)}, bf16[2,2,64,256]{3,2,1,0:T(8,128)(2,1)S(1)}, u32[]{:S(2)}, u32[]{:S(2)}) collective-permute-start(bf16[2,2,64,256]{3,2,1,0:T(8,128)(2,1)S(1)} %get-tuple-element.42), channel_id=1, source_target_pairs={{0,3},{1,0},{2,1},{3,2},{4,7},{5,4},{6,5},{7,6},{8,11},{9,8},{10,9... | collective-permute-start | bytes 393224 | tf_op jit(solution)/shard_map/ppermute | solution.py:53
  8.4 0.7 %copy-done.2 = s32[2048]{0:T(1024)S(1)} copy-done((s32[2048]{0:T(1024)S(1)}, s32[2048]{0:T(1024)}, u32[]{:S(2)}) %copy-start.2) | copy-done | bytes 8216
  9.1 0.2 shard_map.55
  9.4 2.6 %collective-permute-start.3 = (bf16[2,2,64,256]{3,2,1,0:T(8,128)(2,1)S(1)}, bf16[2,2,64,256]{3,2,1,0:T(8,128)(2,1)S(1)}, u32[]{:S(2)}, u32[]{:S(2)}) collective-permute-start(bf16[2,2,64,256]{3,2,1,0:T(8,128)(2,1)S(1)} %collective-permute-done), channel_id=1, source_target_pairs={{0,24},{1,25},{2,26},{3,27},{4,28},{5,29},{6,30},{7,31},{8,0},{9,1... | collective-permute-start | bytes 393224 | tf_op jit(solution)/shard_map/ppermute | solution.py:53
  12.0 1.7 %collective-permute-start.1 = (bf16[2,2,64,256]{3,2,1,0:T(8,128)(2,1)S(1)}, bf16[2,2,64,256]{3,2,1,0:T(8,128)(2,1)S(1)}, u32[]{:S(2)}, u32[]{:S(2)}) collective-permute-start(bf16[2,2,64,256]{3,2,1,0:T(8,128)(2,1)S(1)} %collective-permute-done), channel_id=1, source_target_pairs={{0,16},{1,17},{2,18},{3,19},{4,20},{5,21},{6,22},{7,23},{8,24},{9,... | collective-permute-start | bytes 393224 | tf_op jit(solution)/shard_map/ppermute | solution.py:53
  13.8 1.7 %collective-permute-start.13 = (bf16[4,2,2,64,256]{4,3,2,1,0:T(8,128)(2,1)S(1)}, bf16[4,2,2,64,256]{4,3,2,1,0:T(8,128)(2,1)S(1)}, u32[]{:S(2)}, u32[]{:S(2)}) collective-permute-start(bf16[4,2,2,64,256]{4,3,2,1,0:T(8,128)(2,1)S(1)} %pad_maximum_fusion.refs_0_), channel_id=1, source_target_pairs={{0,24},{1,25},{2,26},{3,27},{4,28},{5,29},{6,30},{7,31},{8,0},{9,1... | collective-permute-start | bytes 1572872 | tf_op jit(solution)/shard_map/ppermute | solution.py:53
  15.5 1.6 %copy-done = bf16[2,2048,256]{2,1,0:T(8,128)(2,1)S(1)} copy-done((bf16[2,2048,256]{2,1,0:T(8,128)(2,1)S(1)}, bf16[2,2048,256]{2,1,0:T(8,128)(2,1)}, u32[]{:S(2)}) %copy-start) | copy-done | bytes 2097176
  17.1 1.6 %copy-done.1 = bf16[2,2048,256]{2,1,0:T(8,128)(2,1)S(1)} copy-done((bf16[2,2048,256]{2,1,0:T(8,128)(2,1)S(1)}, bf16[2,2048,256]{2,1,0:T(8,128)(2,1)}, u32[]{:S(2)}) %copy-start.1) | copy-done | bytes 2097176
  18.6 1.8 %shard_map.56.refs_1_ = f32[128,2048]{1,0:T(8,128)S(1)} custom-call(s32[4,512]{1,0:T(4,128)S(1)} %get-tuple-element.25.ids_ref, s32[128,1]{1,0:T(8,128)S(1)} %get-tuple-element.26.labels_ref, bf16[2,2048,256]{2,1,0:T(8,128)(2,1)S(1)} %copy-done, bf16[2,2048,256]{2,1,0:T(8,128)(2,1)S(1)} %copy-done.1, bf16[4,2,2,64,256]{4,3,2,1,0:T(8,128)(2,1)S(1)} %pad_maximum_fusion.refs_0_), custom_call_target="tpu_custom_call" | custom-call | flops 1342177280 | bytes 1048576 | tf_op jit(solution)/shard_map/pallas_call | solution.py:140
  20.5 2.5 %collective-permute-start.9 = (bf16[4,2,2,64,256]{4,3,2,1,0:T(8,128)(2,1)S(1)}, bf16[4,2,2,64,256]{4,3,2,1,0:T(8,128)(2,1)S(1)}, u32[]{:S(2)}, u32[]{:S(2)}) collective-permute-start(bf16[4,2,2,64,256]{4,3,2,1,0:T(8,128)(2,1)S(1)} %pad_maximum_fusion.1.refs_0_), channel_id=1, source_target_pairs={{0,3},{1,0},{2,1},{3,2},{4,7},{5,4},{6,5},{7,6},{8,11},{9,8},{10,9... | collective-permute-start | bytes 1572872 | tf_op jit(solution)/shard_map/ppermute | solution.py:53
  23.0 1.8 %shard_map.57.refs_2_ = f32[128,2048]{1,0:T(8,128)S(1)} custom-call(s32[4,512]{1,0:T(4,128)S(1)} %get-tuple-element.25.ids_ref, s32[128,1]{1,0:T(8,128)S(1)} %get-tuple-element.26.labels_ref, bf16[2,2048,256]{2,1,0:T(8,128)(2,1)S(1)} %copy-done, bf16[2,2048,256]{2,1,0:T(8,128)(2,1)S(1)} %copy-done.1, ...), custom_call_target="tpu_custom_call" | custom-call | flops 1342177280 | bytes 1048576 | tf_op jit(solution)/shard_map/pallas_call | solution.py:140
  24.8 4.6 %collective-permute-done.13.refs_1_ = bf16[4,2,2,64,256]{4,3,2,1,0:T(8,128)(2,1)S(1)} collective-permute-done((bf16[4,2,2,64,256]{4,3,2,1,0:T(8,128)(2,1)S(1)}, bf16[4,2,2,64,256]{4,3,2,1,0:T(8,128)(2,1)S(1)}, u32[]{:S(2)}, u32[]{:S(2)}) %collective-permute-start.13) | collective-permute-done | bytes 524320 | tf_op jit(solution)/shard_map/ppermute | solution.py:53
  29.3 3.5 %collective-permute-start.14 = (bf16[2,2,2,64,256]{4,3,2,1,0:T(8,128)(2,1)S(1)}, bf16[2,2,2,64,256]{4,3,2,1,0:T(8,128)(2,1)S(1)}, u32[]{:S(2)}, u32[]{:S(2)}) collective-permute-start(bf16[2,2,2,64,256]{4,3,2,1,0:T(8,128)(2,1)S(1)} %slice.19), channel_id=1, source_target_pairs={{0,24},{1,25},{2,26},{3,27},{4,28},{5,29},{6,30},{7,31},{8,0},{9,1... | collective-permute-start | bytes 786440 | tf_op jit(solution)/shard_map/ppermute | solution.py:53
  32.8 0.3 collective-permute-start.12
  33.1 3.2 %shard_map.58.refs_2_ = f32[128,2048]{1,0:T(8,128)S(1)} custom-call(s32[4,512]{1,0:T(4,128)S(1)} %get-tuple-element.25.ids_ref, s32[128,1]{1,0:T(8,128)S(1)} %get-tuple-element.26.labels_ref, bf16[2,2048,256]{2,1,0:T(8,128)(2,1)S(1)} %copy-done, bf16[2,2048,256]{2,1,0:T(8,128)(2,1)S(1)} %copy-done.1, ...), custom_call_target="tpu_custom_call" | custom-call | flops 2684354560 | bytes 1048576 | tf_op jit(solution)/shard_map/pallas_call | solution.py:140
  36.4 0.5 collective-permute-start.10
  36.9 1.1 %collective-permute-start.8 = (bf16[2,2,2,64,256]{4,3,2,1,0:T(8,128)(2,1)S(1)}, bf16[2,2,2,64,256]{4,3,2,1,0:T(8,128)(2,1)S(1)}, u32[]{:S(2)}, u32[]{:S(2)}) collective-permute-start(bf16[2,2,2,64,256]{4,3,2,1,0:T(8,128)(2,1)S(1)} %slice.16), channel_id=1, source_target_pairs={{0,1},{1,2},{2,3},{3,0},{4,5},{5,6},{6,7},{7,4},{8,9},{9,10},{10,1... | collective-permute-start | bytes 786440 | tf_op jit(solution)/shard_map/ppermute | solution.py:53
  38.0 3.2 %shard_map.59.refs_2_ = f32[128,2048]{1,0:T(8,128)S(1)} custom-call(s32[4,512]{1,0:T(4,128)S(1)} %get-tuple-element.25.ids_ref, s32[128,1]{1,0:T(8,128)S(1)} %get-tuple-element.26.labels_ref, bf16[2,2048,256]{2,1,0:T(8,128)(2,1)S(1)} %copy-done, bf16[2,2048,256]{2,1,0:T(8,128)(2,1)S(1)} %copy-done.1, ...), custom_call_target="tpu_custom_call" | custom-call | flops 2684354560 | bytes 1048576 | tf_op jit(solution)/shard_map/pallas_call | solution.py:140
  41.2 1.8 %shard_map.60.refs_2_ = f32[128,2048]{1,0:T(8,128)S(1)} custom-call(s32[4,512]{1,0:T(4,128)S(1)} %get-tuple-element.25.ids_ref, s32[128,1]{1,0:T(8,128)S(1)} %get-tuple-element.26.labels_ref, bf16[2,2048,256]{2,1,0:T(8,128)(2,1)S(1)} %copy-done, bf16[2,2048,256]{2,1,0:T(8,128)(2,1)S(1)} %copy-done.1, ...), custom_call_target="tpu_custom_call" | custom-call | flops 1342177280 | bytes 1048576 | tf_op jit(solution)/shard_map/pallas_call | solution.py:140
  43.0 1.0 %collective-permute-done.8.refs_0_ = bf16[2,2,2,64,256]{4,3,2,1,0:T(8,128)(2,1)S(1)} collective-permute-done((bf16[2,2,2,64,256]{4,3,2,1,0:T(8,128)(2,1)S(1)}, bf16[2,2,2,64,256]{4,3,2,1,0:T(8,128)(2,1)S(1)}, u32[]{:S(2)}, u32[]{:S(2)}) %collective-permute-start.8) | collective-permute-done | bytes 262176 | tf_op jit(solution)/shard_map/ppermute | solution.py:53
  44.0 1.8 %shard_map.61 = (f32[64,2048]{1,0:T(8,128)S(1)}, bf16[64,2048]{1,0:T(8,128)(2,1)S(1)}) custom-call(s32[4,512]{1,0:T(4,128)S(1)} %get-tuple-element.25.ids_ref, s32[128,1]{1,0:T(8,128)S(1)} %get-tuple-element.26.labels_ref, bf16[2,2048,256]{2,1,0:T(8,128)(2,1)S(1)} %copy-done, bf16[2,2048,256]{2,1,0:T(8,128)(2,1)S(1)} %copy-done.1, ...), custom_call_target="tpu_custom_call" | custom-call | flops 1342177280 | bytes 1048576 | tf_op jit(solution)/shard_map/pallas_call | solution.py:140
  45.8 3.0 %collective-permute-start.15 = (bf16[64,2048]{1,0:T(8,128)(2,1)S(1)}, bf16[64,2048]{1,0:T(8,128)(2,1)S(1)}, u32[]{:S(2)}, u32[]{:S(2)}) collective-permute-start(bf16[64,2048]{1,0:T(8,128)(2,1)S(1)} %get-tuple-element.36), channel_id=1, source_target_pairs={{0,32},{1,33},{2,34},{3,35},{4,36},{5,37},{6,38},{7,39},{8,40},{9,... | collective-permute-start | bytes 786440 | tf_op jit(solution)/shard_map/ppermute | solution.py:53
  48.8 1.2 %collective-permute-done.15.got_ref = bf16[64,2048]{1,0:T(8,128)(2,1)S(1)} collective-permute-done((bf16[64,2048]{1,0:T(8,128)(2,1)S(1)}, bf16[64,2048]{1,0:T(8,128)(2,1)S(1)}, u32[]{:S(2)}, u32[]{:S(2)}) %collective-permute-start.15) | collective-permute-done | bytes 262176 | tf_op jit(solution)/shard_map/ppermute | solution.py:53
  50.0 6.3 %collective-permute-start.16 = (bf16[16,2048]{1,0:T(8,128)(2,1)S(1)}, bf16[16,2048]{1,0:T(8,128)(2,1)S(1)}, u32[]{:S(2)}, u32[]{:S(2)}) collective-permute-start(bf16[16,2048]{1,0:T(8,128)(2,1)S(1)} %get-tuple-element.38), channel_id=1, source_target_pairs={{0,128},{1,129},{2,130},{3,131},{4,132},{5,133},{6,134},{7,135},{8... | collective-permute-start | bytes 196616 | tf_op jit(solution)/shard_map/ppermute | solution.py:53
  56.3 1.2 %collective-permute-start.17 = (bf16[16,2048]{1,0:T(8,128)(2,1)S(1)}, bf16[16,2048]{1,0:T(8,128)(2,1)S(1)}, u32[]{:S(2)}, u32[]{:S(2)}) collective-permute-start(bf16[16,2048]{1,0:T(8,128)(2,1)S(1)} %get-tuple-element.39), channel_id=1, source_target_pairs={{0,64},{1,65},{2,66},{3,67},{4,68},{5,69},{6,70},{7,71},{8,72},{9,... | collective-permute-start | bytes 196616 | tf_op jit(solution)/shard_map/ppermute | solution.py:53
  57.5 2.4 %collective-permute-start.18 = (bf16[16,2048]{1,0:T(8,128)(2,1)S(1)}, bf16[16,2048]{1,0:T(8,128)(2,1)S(1)}, u32[]{:S(2)}, u32[]{:S(2)}) collective-permute-start(bf16[16,2048]{1,0:T(8,128)(2,1)S(1)} %get-tuple-element.40), channel_id=1, source_target_pairs={{0,192},{1,193},{2,194},{3,195},{4,196},{5,197},{6,198},{7,199},{8... | collective-permute-start | bytes 196616 | tf_op jit(solution)/shard_map/ppermute | solution.py:53
  59.9 2.7 %collective-permute-done.17.refs_1_ = bf16[16,2048]{1,0:T(8,128)(2,1)S(1)} collective-permute-done((bf16[16,2048]{1,0:T(8,128)(2,1)S(1)}, bf16[16,2048]{1,0:T(8,128)(2,1)S(1)}, u32[]{:S(2)}, u32[]{:S(2)}) %collective-permute-start.17) | collective-permute-done | bytes 65568 | tf_op jit(solution)/shard_map/ppermute | solution.py:53
  62.6 0.7 %shard_map.63 = f32[16,2048]{1,0:T(8,128)} custom-call(f32[16,2048]{1,0:T(8,128)S(1)} %get-tuple-element.37.own_ref, bf16[16,2048]{1,0:T(8,128)(2,1)S(1)} %collective-permute-done.16.refs_0_, bf16[16,2048]{1,0:T(8,128)(2,1)S(1)} %collective-permute-done.17.refs_1_, bf16[16,2048]{1,0:T(8,128)(2,1)S(1)} %collective-permute-done.18.refs_2_), custom_call_target="tpu_custom_call" | custom-call | tf_op jit(solution)/shard_map/pallas_call | solution.py:181
  (28 shorter events, 0.4 us)
Async XLA Ops:
  0.9 8.5 %collective-permute-start = (bf16[2,2,64,256]{3,2,1,0:T(8,128)(2,1)S(1)}, bf16[2,2,64,256]{3,2,1,0:T(8,128)(2,1)S(1)}, u32[]{:S(2)}, u32[]{:S(2)}) collective-permute-start(bf16[2,2,64,256]{3,2,1,0:T(8,128)(2,1)S(1)} %get-tuple-element.42), channel_id=1, source_target_pairs={{0,4},{1,5},{2,6},{3,7},{4,0},{5,1},{6,2},{7,3},{8,12},{9,13},{10,... | collective-permute-start | bytes 393224 | tf_op jit(solution)/shard_map/ppermute | solution.py:53
  3.4 8.5 %collective-permute-start.5 = (bf16[2,2,64,256]{3,2,1,0:T(8,128)(2,1)S(1)}, bf16[2,2,64,256]{3,2,1,0:T(8,128)(2,1)S(1)}, u32[]{:S(2)}, u32[]{:S(2)}) collective-permute-start(bf16[2,2,64,256]{3,2,1,0:T(8,128)(2,1)S(1)} %get-tuple-element.42), channel_id=1, source_target_pairs={{0,1},{1,2},{2,3},{3,0},{4,5},{5,6},{6,7},{7,4},{8,9},{9,10},{10,1... | collective-permute-start | bytes 393224 | tf_op jit(solution)/shard_map/ppermute | solution.py:53
  4.7 8.9 %collective-permute-start.4 = (bf16[2,2,64,256]{3,2,1,0:T(8,128)(2,1)S(1)}, bf16[2,2,64,256]{3,2,1,0:T(8,128)(2,1)S(1)}, u32[]{:S(2)}, u32[]{:S(2)}) collective-permute-start(bf16[2,2,64,256]{3,2,1,0:T(8,128)(2,1)S(1)} %get-tuple-element.42), channel_id=1, source_target_pairs={{0,2},{1,3},{2,0},{3,1},{4,6},{5,7},{6,4},{7,5},{8,10},{9,11},{10,... | collective-permute-start | bytes 393224 | tf_op jit(solution)/shard_map/ppermute | solution.py:53
  7.4 6.3 %collective-permute-start.6 = (bf16[2,2,64,256]{3,2,1,0:T(8,128)(2,1)S(1)}, bf16[2,2,64,256]{3,2,1,0:T(8,128)(2,1)S(1)}, u32[]{:S(2)}, u32[]{:S(2)}) collective-permute-start(bf16[2,2,64,256]{3,2,1,0:T(8,128)(2,1)S(1)} %get-tuple-element.42), channel_id=1, source_target_pairs={{0,3},{1,0},{2,1},{3,2},{4,7},{5,4},{6,5},{7,6},{8,11},{9,8},{10,9... | collective-permute-start | bytes 393224 | tf_op jit(solution)/shard_map/ppermute | solution.py:53
  8.4 0.7 %copy-start.2 = (s32[2048]{0:T(1024)S(1)}, s32[2048]{0:T(1024)}, u32[]{:S(2)}) copy-start(s32[2048]{0:T(1024)} %param.9) | copy-start | bytes 24580
  9.4 11.0 %collective-permute-start.3 = (bf16[2,2,64,256]{3,2,1,0:T(8,128)(2,1)S(1)}, bf16[2,2,64,256]{3,2,1,0:T(8,128)(2,1)S(1)}, u32[]{:S(2)}, u32[]{:S(2)}) collective-permute-start(bf16[2,2,64,256]{3,2,1,0:T(8,128)(2,1)S(1)} %collective-permute-done), channel_id=1, source_target_pairs={{0,24},{1,25},{2,26},{3,27},{4,28},{5,29},{6,30},{7,31},{8,0},{9,1... | collective-permute-start | bytes 393224 | tf_op jit(solution)/shard_map/ppermute | solution.py:53
  12.0 8.5 %collective-permute-start.2 = (bf16[2,2,64,256]{3,2,1,0:T(8,128)(2,1)S(1)}, bf16[2,2,64,256]{3,2,1,0:T(8,128)(2,1)S(1)}, u32[]{:S(2)}, u32[]{:S(2)}) collective-permute-start(bf16[2,2,64,256]{3,2,1,0:T(8,128)(2,1)S(1)} %collective-permute-done), channel_id=1, source_target_pairs={{0,8},{1,9},{2,10},{3,11},{4,12},{5,13},{6,14},{7,15},{8,16},{9,17... | collective-permute-start | bytes 393224 | tf_op jit(solution)/shard_map/ppermute | solution.py:53
  12.0 8.5 %collective-permute-start.1 = (bf16[2,2,64,256]{3,2,1,0:T(8,128)(2,1)S(1)}, bf16[2,2,64,256]{3,2,1,0:T(8,128)(2,1)S(1)}, u32[]{:S(2)}, u32[]{:S(2)}) collective-permute-start(bf16[2,2,64,256]{3,2,1,0:T(8,128)(2,1)S(1)} %collective-permute-done), channel_id=1, source_target_pairs={{0,16},{1,17},{2,18},{3,19},{4,20},{5,21},{6,22},{7,23},{8,24},{9,... | collective-permute-start | bytes 393224 | tf_op jit(solution)/shard_map/ppermute | solution.py:53
  13.8 15.5 %collective-permute-start.13 = (bf16[4,2,2,64,256]{4,3,2,1,0:T(8,128)(2,1)S(1)}, bf16[4,2,2,64,256]{4,3,2,1,0:T(8,128)(2,1)S(1)}, u32[]{:S(2)}, u32[]{:S(2)}) collective-permute-start(bf16[4,2,2,64,256]{4,3,2,1,0:T(8,128)(2,1)S(1)} %pad_maximum_fusion.refs_0_), channel_id=1, source_target_pairs={{0,24},{1,25},{2,26},{3,27},{4,28},{5,29},{6,30},{7,31},{8,0},{9,1... | collective-permute-start | bytes 1572872 | tf_op jit(solution)/shard_map/ppermute | solution.py:53
  15.4 17.4 %collective-permute-start.11 = (bf16[4,2,2,64,256]{4,3,2,1,0:T(8,128)(2,1)S(1)}, bf16[4,2,2,64,256]{4,3,2,1,0:T(8,128)(2,1)S(1)}, u32[]{:S(2)}, u32[]{:S(2)}) collective-permute-start(bf16[4,2,2,64,256]{4,3,2,1,0:T(8,128)(2,1)S(1)} %pad_maximum_fusion.refs_0_), channel_id=1, source_target_pairs={{0,8},{1,9},{2,10},{3,11},{4,12},{5,13},{6,14},{7,15},{8,16},{9,17... | collective-permute-start | bytes 1572872 | tf_op jit(solution)/shard_map/ppermute | solution.py:53
  15.5 1.6 %copy-start = (bf16[2,2048,256]{2,1,0:T(8,128)(2,1)S(1)}, bf16[2,2048,256]{2,1,0:T(8,128)(2,1)}, u32[]{:S(2)}) copy-start(bf16[2,2048,256]{2,1,0:T(8,128)(2,1)} %ta_ref.11) | copy-start | bytes 6291460
  17.1 1.6 %copy-start.1 = (bf16[2,2048,256]{2,1,0:T(8,128)(2,1)S(1)}, bf16[2,2048,256]{2,1,0:T(8,128)(2,1)}, u32[]{:S(2)}) copy-start(bf16[2,2048,256]{2,1,0:T(8,128)(2,1)} %tg_ref.11) | copy-start | bytes 6291460
  20.5 15.8 %collective-permute-start.9 = (bf16[4,2,2,64,256]{4,3,2,1,0:T(8,128)(2,1)S(1)}, bf16[4,2,2,64,256]{4,3,2,1,0:T(8,128)(2,1)S(1)}, u32[]{:S(2)}, u32[]{:S(2)}) collective-permute-start(bf16[4,2,2,64,256]{4,3,2,1,0:T(8,128)(2,1)S(1)} %pad_maximum_fusion.1.refs_0_), channel_id=1, source_target_pairs={{0,3},{1,0},{2,1},{3,2},{4,7},{5,4},{6,5},{7,6},{8,11},{9,8},{10,9... | collective-permute-start | bytes 1572872 | tf_op jit(solution)/shard_map/ppermute | solution.py:53
  23.0 13.9 %collective-permute-start.7 = (bf16[4,2,2,64,256]{4,3,2,1,0:T(8,128)(2,1)S(1)}, bf16[4,2,2,64,256]{4,3,2,1,0:T(8,128)(2,1)S(1)}, u32[]{:S(2)}, u32[]{:S(2)}) collective-permute-start(bf16[4,2,2,64,256]{4,3,2,1,0:T(8,128)(2,1)S(1)} %pad_maximum_fusion.1.refs_0_), channel_id=1, source_target_pairs={{0,1},{1,2},{2,3},{3,0},{4,5},{5,6},{6,7},{7,4},{8,9},{9,10},{10,1... | collective-permute-start | bytes 1572872 | tf_op jit(solution)/shard_map/ppermute | solution.py:53
  29.3 11.9 %collective-permute-start.14 = (bf16[2,2,2,64,256]{4,3,2,1,0:T(8,128)(2,1)S(1)}, bf16[2,2,2,64,256]{4,3,2,1,0:T(8,128)(2,1)S(1)}, u32[]{:S(2)}, u32[]{:S(2)}) collective-permute-start(bf16[2,2,2,64,256]{4,3,2,1,0:T(8,128)(2,1)S(1)} %slice.19), channel_id=1, source_target_pairs={{0,24},{1,25},{2,26},{3,27},{4,28},{5,29},{6,30},{7,31},{8,0},{9,1... | collective-permute-start | bytes 786440 | tf_op jit(solution)/shard_map/ppermute | solution.py:53
  32.8 8.4 %collective-permute-start.12 = (bf16[2,2,2,64,256]{4,3,2,1,0:T(8,128)(2,1)S(1)}, bf16[2,2,2,64,256]{4,3,2,1,0:T(8,128)(2,1)S(1)}, u32[]{:S(2)}, u32[]{:S(2)}) collective-permute-start(bf16[2,2,2,64,256]{4,3,2,1,0:T(8,128)(2,1)S(1)} %slice.18), channel_id=1, source_target_pairs={{0,8},{1,9},{2,10},{3,11},{4,12},{5,13},{6,14},{7,15},{8,16},{9,17... | collective-permute-start | bytes 786440 | tf_op jit(solution)/shard_map/ppermute | solution.py:53
  36.4 6.7 %collective-permute-start.10 = (bf16[2,2,2,64,256]{4,3,2,1,0:T(8,128)(2,1)S(1)}, bf16[2,2,2,64,256]{4,3,2,1,0:T(8,128)(2,1)S(1)}, u32[]{:S(2)}, u32[]{:S(2)}) collective-permute-start(bf16[2,2,2,64,256]{4,3,2,1,0:T(8,128)(2,1)S(1)} %slice.17), channel_id=1, source_target_pairs={{0,3},{1,0},{2,1},{3,2},{4,7},{5,4},{6,5},{7,6},{8,11},{9,8},{10,9... | collective-permute-start | bytes 786440 | tf_op jit(solution)/shard_map/ppermute | solution.py:53
  36.9 7.1 %collective-permute-start.8 = (bf16[2,2,2,64,256]{4,3,2,1,0:T(8,128)(2,1)S(1)}, bf16[2,2,2,64,256]{4,3,2,1,0:T(8,128)(2,1)S(1)}, u32[]{:S(2)}, u32[]{:S(2)}) collective-permute-start(bf16[2,2,2,64,256]{4,3,2,1,0:T(8,128)(2,1)S(1)} %slice.16), channel_id=1, source_target_pairs={{0,1},{1,2},{2,3},{3,0},{4,5},{5,6},{6,7},{7,4},{8,9},{9,10},{10,1... | collective-permute-start | bytes 786440 | tf_op jit(solution)/shard_map/ppermute | solution.py:53
  45.8 4.2 %collective-permute-start.15 = (bf16[64,2048]{1,0:T(8,128)(2,1)S(1)}, bf16[64,2048]{1,0:T(8,128)(2,1)S(1)}, u32[]{:S(2)}, u32[]{:S(2)}) collective-permute-start(bf16[64,2048]{1,0:T(8,128)(2,1)S(1)} %get-tuple-element.36), channel_id=1, source_target_pairs={{0,32},{1,33},{2,34},{3,35},{4,36},{5,37},{6,38},{7,39},{8,40},{9,... | collective-permute-start | bytes 786440 | tf_op jit(solution)/shard_map/ppermute | solution.py:53
  50.0 9.8 %collective-permute-start.16 = (bf16[16,2048]{1,0:T(8,128)(2,1)S(1)}, bf16[16,2048]{1,0:T(8,128)(2,1)S(1)}, u32[]{:S(2)}, u32[]{:S(2)}) collective-permute-start(bf16[16,2048]{1,0:T(8,128)(2,1)S(1)} %get-tuple-element.38), channel_id=1, source_target_pairs={{0,128},{1,129},{2,130},{3,131},{4,132},{5,133},{6,134},{7,135},{8... | collective-permute-start | bytes 196616 | tf_op jit(solution)/shard_map/ppermute | solution.py:53
  56.3 6.3 %collective-permute-start.17 = (bf16[16,2048]{1,0:T(8,128)(2,1)S(1)}, bf16[16,2048]{1,0:T(8,128)(2,1)S(1)}, u32[]{:S(2)}, u32[]{:S(2)}) collective-permute-start(bf16[16,2048]{1,0:T(8,128)(2,1)S(1)} %get-tuple-element.39), channel_id=1, source_target_pairs={{0,64},{1,65},{2,66},{3,67},{4,68},{5,69},{6,70},{7,71},{8,72},{9,... | collective-permute-start | bytes 196616 | tf_op jit(solution)/shard_map/ppermute | solution.py:53
  57.5 5.1 %collective-permute-start.18 = (bf16[16,2048]{1,0:T(8,128)(2,1)S(1)}, bf16[16,2048]{1,0:T(8,128)(2,1)S(1)}, u32[]{:S(2)}, u32[]{:S(2)}) collective-permute-start(bf16[16,2048]{1,0:T(8,128)(2,1)S(1)} %get-tuple-element.40), channel_id=1, source_target_pairs={{0,192},{1,193},{2,194},{3,195},{4,196},{5,197},{6,198},{7,199},{8... | collective-permute-start | bytes 196616 | tf_op jit(solution)/shard_map/ppermute | solution.py:53

commit v5 on v4

--- a/solution.py
+++ b/solution.py
@@ -16,6 +16,7 @@
 F32 = jnp.float32
 AXES = ("layer", "tok")
 SMALL = pltpu.CompilerParams(vmem_limit_bytes=4 * 1024 * 1024)
+HBM = pl.BlockSpec(memory_space=pltpu.HBM)
 SMEM = pl.BlockSpec(memory_space=pltpu.SMEM)
 VMEM = pl.BlockSpec(memory_space=pltpu.VMEM)
 
@@ -37,12 +38,12 @@
     return pairs
 
 
-def along_x(d):
-    return moves(lambda h, c, x, z, y: (h, c, x + d, z, y))
-
-
-def along_y(d):
-    return moves(lambda h, c, x, z, y: (h, c, x, z, y + d))
+def one_way(d):
+    return moves(lambda h, c, x, z, y: (h, c, x + d, z, y) if c == 0 else (h, c, x, z, y + d))
+
+
+def other_way(d):
+    return moves(lambda h, c, x, z, y: (h, c, x, z, y + d) if c == 0 else (h, c, x + d, z, y))
 
 
 def along_z(d):
@@ -67,6 +68,7 @@
                 for n in range(2):
                     near = ORDER[2 * pair + n]
                     p, q = (far, near) if half == 0 else (near, far)
+                    p, q = jnp.where(core == 0, p, q), jnp.where(core == 0, q, p)
                     tok = (x + p) % 4 * 8 + (z + half) % 2 * 4 + (y + q) % 4
                     turn = (tok + n) % 2
                     got.append(turned[pl.ds(turn * 16 + tok // 2, 1), :])
@@ -102,12 +104,28 @@
     sel = (labels_ref[...] == ids).astype(F32).astype(BF16)
     nt = (((1,), (1,)), ((), ()))
     outs = rest if first else rest[1:]
-    for j in range(ta_ref.shape[1] // tile):
+    tiles = ta_ref.shape[1] // tile
+    copies = {}
+    if first:
+        kept, sems = rest[1:3], rest[3]
+        for j in range(tiles):
+            for layer in range(2):
+                for k in range(2):
+                    piece = (layer, slice(j * tile, (j + 1) * tile))
+                    copies[j, layer, k] = pltpu.make_async_copy(
+                        trains[k].at[piece], kept[k].at[piece], sems.at[j, layer, k]
+                    )
+        for copy in copies.values():
+            copy.start()
+        trains = kept
+    for j in range(tiles):
         cols = slice(j * tile, (j + 1) * tile)
         prods = []
         for layer in range(2):
             grams = []
             for k in range(2):
+                if first:
+                    copies[j, layer, k].wait()
                 test = jnp.concatenate([b[:, k, layer].reshape(-1, 256) for b in blocks], 0)
                 grams.append(
                     lax.dot_general(test, trains[k][layer, cols], nt, preferred_element_type=F32)
@@ -135,14 +153,17 @@
             jax.ShapeDtypeStruct((Q // 2, rows), BF16),
         )
     else:
-        out_shape = jax.ShapeDtypeStruct((Q, rows), F32)
+        out_shape = (jax.ShapeDtypeStruct((Q, rows), F32),)
+    if first:
+        out_shape += tuple(jax.ShapeDtypeStruct(t.shape, t.dtype) for t in trains)
     s_rows = BLOCK * sum(b.shape[0] for b in blocks)
     return pl.pallas_call(
         functools.partial(chunk_kernel, pieces, first, last, len(blocks)),
-        in_specs=[VMEM] * len(args),
-        out_specs=(VMEM, VMEM) if last else VMEM,
+        in_specs=[VMEM] * 2 + [HBM if first else VMEM] * 2 + [VMEM] * (len(args) - 4),
+        out_specs=(VMEM,) * len(out_shape),
         out_shape=out_shape,
-        compiler_params=pltpu.CompilerParams(vmem_limit_bytes=16 * 1024 * 1024),
+        scratch_shapes=[pltpu.SemaphoreType.DMA((rows // 1024, 2, 2))] if first else [],
+        compiler_params=pltpu.CompilerParams(vmem_limit_bytes=(48 if first else 16) * 1024 * 1024),
         cost_estimate=pl.CostEstimate(
             flops=2 * 2 * s_rows * rows * (2 * 256 + Q),
             bytes_accessed=1024 * 1024,
@@ -196,23 +217,24 @@
     other = send(block, partner)
     trains = (train_act, train_grad)
     ids, labels = prepare(layer, tok, segment_ids)
-    low = jnp.stack([block] + [send(block, along_y(d)) for d in (2, 1, -1)])
+    low = jnp.stack([block] + [send(block, other_way(d)) for d in (2, 1, -1)])
     other, ids, labels = lax.optimization_barrier((other, ids, labels))
     run = functools.partial(chunk, ids=ids, labels=labels, trains=trains)
-    acc = run(((0, 0),), (low,), None, False)
-    ring = [send(other, along_x(d)) for d in (2, 1, -1)]
+    acc, *trains = run(((0, 0),), (low,), None, False)
+    run = functools.partial(chunk, ids=ids, labels=labels, trains=trains)
+    ring = [send(other, one_way(d)) for d in (-1, 1, 2)]
     ring, acc = lax.optimization_barrier((ring, acc))
-    high = jnp.stack([other] + ring)
-
-    low_prev, low_next = send(low, along_x(1)), send(low, along_x(-1))
-    high_prev, high_next = send(high, along_y(1)), send(high, along_y(-1))
-    low_far = (send(low_prev[:2], along_x(1)), send(low_next[2:], along_x(-1)))
-    high_far = (send(high_prev[:2], along_y(1)), send(high_next[2:], along_y(-1)))
-    acc = run(((0, 1),), (high,), acc, False)
-    acc = run(((2, 0), (3, 0)), (low_prev, low_next), acc, False)
+    high = jnp.stack([other] + ring[::-1])
+
+    low_prev, low_next = send(low, one_way(1)), send(low, one_way(-1))
+    high_prev, high_next = send(high, other_way(1)), send(high, other_way(-1))
+    low_far = (send(low_prev[:2], one_way(1)), send(low_next[2:], one_way(-1)))
+    high_far = (send(high_prev[:2], other_way(1)), send(high_next[2:], other_way(-1)))
+    (acc,) = run(((0, 1),), (high,), acc, False)
+    (acc,) = run(((2, 0), (3, 0)), (low_prev, low_next), acc, False)
     high_prev, high_next, acc = lax.optimization_barrier((high_prev, high_next, acc))
-    acc = run(((2, 1), (3, 1)), (high_prev, high_next), acc, False)
-    acc = run(((1, 0),), low_far, acc, False)
+    (acc,) = run(((2, 1), (3, 1)), (high_prev, high_next), acc, False)
+    (acc,) = run(((1, 0),), low_far, acc, False)
     keep, give = run(((1, 1),), high_far, acc, True)
 
     own, *parts = merge(keep, send(give, sibling))

time: 64 us -> 62.9 us (0.983)
  local copies, waits for them, and re-layouts: 3.95 us -> 0.77 us
  Pallas kernels: 14.5 us -> 16.9 us
  starting transfers between devices: 34.2 us -> 32.6 us
  waiting for transfers between devices: 9.52 us -> 10.6 us
    unnamed x6 -> x2, local copies, waits for them, and re-layouts: 3.88 us -> 0.7 us
    pallas_call x6, Pallas kernels: 13.5 us -> 15.8 us  [chunk(): pl.pallas_call(functools.partial(chunk_kernel, pieces, first, last, len(b...]
    ppermute x19, starting transfers between devices: 34.2 us -> 32.6 us  [send(): return lax.ppermute(value, AXES, pairs)]
    ppermute x19, waiting for transfers between devices: 9.52 us -> 10.6 us  [send(): return lax.ppermute(value, AXES, pairs)]
  transfers between devices with their start and end apart: 19 -> 19, of which waited for: 4 -> 5; matrix products, arithmetic and copies ran while one was open for 0% -> 0% of each run, Pallas kernels for 19% -> 23%
where the time goes in v5:
time: 62.9 us; the launch traced here: 62.1 us
  starting transfers between devices  32.6 us (52%)
  Pallas kernels  16.9 us (27%)
  waiting for transfers between devices  10.6 us (17%)
  other arithmetic  1.03 us (2%)
  local copies, waits for them, and re-layouts  0.77 us (1%)
    ppermute x19, starting transfers between devices, send(): return lax.ppermute(value, AXES, pairs)  32.6 us
    pallas_call x6, Pallas kernels, chunk(): pl.pallas_call(functools.partial(chunk_kernel, pieces, first, last, len(b...  15.8 us
    ppermute x19, waiting for transfers between devices, send(): return lax.ppermute(value, AXES, pairs)  10.6 us
  transfers between devices with their start and end apart: 19, of which 5 were waited for; matrix products, arithmetic and copies ran while one was open for 0% of the time, Pallas kernels for 23%

profile of v5, /device:TPU:1, one launch (start us, length us, event | category | flops | bytes accessed | tf_op | source)
XLA Modules:
  0.0 62.1 jit_solution(15379066941548623802)
XLA Ops:
  0.0 0.9 %fusion = (bf16[1,2,2,64,256]{4,3,2,1,0:T(8,128)(2,1)S(1)}, bf16[2,2,64,256]{3,2,1,0:T(8,128)(2,1)S(1)}) fusion(bf16[1,2,64,256]{3,2,1,0:T(8,128)(2,1)} %bitcast.22, bf16[1,2,64,256]{3,2,1,0:T(8,128)(2,1)} %bitcast.23), kind=kLoop, calls=%fused_computation.3 | loop fusion | flops 65536 | bytes 393216 | tf_op jit(solution)/shard_map/stack | solution.py:220
  0.9 2.6 %collective-permute-start = (bf16[2,2,64,256]{3,2,1,0:T(8,128)(2,1)S(1)}, bf16[2,2,64,256]{3,2,1,0:T(8,128)(2,1)S(1)}, u32[]{:S(2)}, u32[]{:S(2)}) collective-permute-start(bf16[2,2,64,256]{3,2,1,0:T(8,128)(2,1)S(1)} %get-tuple-element.48), channel_id=1, source_target_pairs={{0,4},{1,5},{2,6},{3,7},{4,0},{5,1},{6,2},{7,3},{8,12},{9,13},{10,... | collective-permute-start | bytes 393224 | tf_op jit(solution)/shard_map/ppermute | solution.py:54
  3.4 1.2 %collective-permute-start.2 = (bf16[2,2,64,256]{3,2,1,0:T(8,128)(2,1)S(1)}, bf16[2,2,64,256]{3,2,1,0:T(8,128)(2,1)S(1)}, u32[]{:S(2)}, u32[]{:S(2)}) collective-permute-start(bf16[2,2,64,256]{3,2,1,0:T(8,128)(2,1)S(1)} %get-tuple-element.48), channel_id=1, source_target_pairs={{0,1},{1,2},{2,3},{3,0},{4,5},{5,6},{6,7},{7,4},{8,9},{9,10},{10,1... | collective-permute-start | bytes 393224 | tf_op jit(solution)/shard_map/ppermute | solution.py:54
  4.7 2.5 %collective-permute-start.1 = (bf16[2,2,64,256]{3,2,1,0:T(8,128)(2,1)S(1)}, bf16[2,2,64,256]{3,2,1,0:T(8,128)(2,1)S(1)}, u32[]{:S(2)}, u32[]{:S(2)}) collective-permute-start(bf16[2,2,64,256]{3,2,1,0:T(8,128)(2,1)S(1)} %get-tuple-element.48), channel_id=1, source_target_pairs={{0,2},{1,3},{2,0},{3,1},{4,6},{5,7},{6,4},{7,5},{8,10},{9,11},{10,... | collective-permute-start | bytes 393224 | tf_op jit(solution)/shard_map/ppermute | solution.py:54
  7.1 1.2 %collective-permute-start.3 = (bf16[2,2,64,256]{3,2,1,0:T(8,128)(2,1)S(1)}, bf16[2,2,64,256]{3,2,1,0:T(8,128)(2,1)S(1)}, u32[]{:S(2)}, u32[]{:S(2)}) collective-permute-start(bf16[2,2,64,256]{3,2,1,0:T(8,128)(2,1)S(1)} %get-tuple-element.48), channel_id=1, source_target_pairs={{0,3},{1,0},{2,1},{3,2},{4,7},{5,4},{6,5},{7,6},{8,11},{9,8},{10,9... | collective-permute-start | bytes 393224 | tf_op jit(solution)/shard_map/ppermute | solution.py:54
  8.3 0.7 %copy-done = s32[2048]{0:T(1024)S(1)} copy-done((s32[2048]{0:T(1024)S(1)}, s32[2048]{0:T(1024)}, u32[]{:S(2)}) %copy-start) | copy-done | bytes 8216
  9.0 0.3 shard_map.55
  9.3 3.0 %collective-permute-start.6 = (bf16[2,2,64,256]{3,2,1,0:T(8,128)(2,1)S(1)}, bf16[2,2,64,256]{3,2,1,0:T(8,128)(2,1)S(1)}, u32[]{:S(2)}, u32[]{:S(2)}) collective-permute-start(bf16[2,2,64,256]{3,2,1,0:T(8,128)(2,1)S(1)} %collective-permute-done), channel_id=1, source_target_pairs={{0,16},{1,17},{2,18},{3,19},{4,20},{5,21},{6,22},{7,23},{8,24},{9,... | collective-permute-start | bytes 393224 | tf_op jit(solution)/shard_map/ppermute | solution.py:54
  12.3 0.4 collective-permute-start.5
  12.7 2.3 %collective-permute-start.4 = (bf16[2,2,64,256]{3,2,1,0:T(8,128)(2,1)S(1)}, bf16[2,2,64,256]{3,2,1,0:T(8,128)(2,1)S(1)}, u32[]{:S(2)}, u32[]{:S(2)}) collective-permute-start(bf16[2,2,64,256]{3,2,1,0:T(8,128)(2,1)S(1)} %collective-permute-done), channel_id=1, source_target_pairs={{0,24},{1,25},{2,26},{3,27},{4,28},{5,29},{6,30},{7,31},{8,0},{9,1... | collective-permute-start | bytes 393224 | tf_op jit(solution)/shard_map/ppermute | solution.py:54
  15.1 0.1 collective-permute-start.13
  15.1 1.4 %collective-permute-start.11 = (bf16[4,2,2,64,256]{4,3,2,1,0:T(8,128)(2,1)S(1)}, bf16[4,2,2,64,256]{4,3,2,1,0:T(8,128)(2,1)S(1)}, u32[]{:S(2)}, u32[]{:S(2)}) collective-permute-start(bf16[4,2,2,64,256]{4,3,2,1,0:T(8,128)(2,1)S(1)} %pad_maximum_fusion.refs_0_), channel_id=1, source_target_pairs={{0,8},{1,9},{2,10},{3,11},{4,12},{5,13},{6,14},{7,15},{8,16},{9,17... | collective-permute-start | bytes 1572872 | tf_op jit(solution)/shard_map/ppermute | solution.py:54
  16.6 4.1 %shard_map.56 = (f32[128,2048]{1,0:T(8,128)S(1)}, bf16[2,2048,256]{2,1,0:T(8,128)(2,1)S(1)}, bf16[2,2048,256]{2,1,0:T(8,128)(2,1)S(1)}) custom-call(s32[4,512]{1,0:T(4,128)S(1)} %get-tuple-element.28.ids_ref, s32[128,1]{1,0:T(8,128)S(1)} %get-tuple-element.29.labels_ref, bf16[2,2048,256]{2,1,0:T(8,128)(2,1)} %ta_ref.1, bf16[2,2048,256]{2,1,0:T(8,128)(2,1)} %tg_ref.1, ...), custom_call_target="tpu_custom_call" | custom-call | flops 1342177280 | bytes 1048576 | tf_op jit(solution)/shard_map/pallas_call | solution.py:160
  20.8 0.1 collective-permute-start.9
  20.9 1.5 %collective-permute-start.7 = (bf16[4,2,2,64,256]{4,3,2,1,0:T(8,128)(2,1)S(1)}, bf16[4,2,2,64,256]{4,3,2,1,0:T(8,128)(2,1)S(1)}, u32[]{:S(2)}, u32[]{:S(2)}) collective-permute-start(bf16[4,2,2,64,256]{4,3,2,1,0:T(8,128)(2,1)S(1)} %pad_maximum_fusion.1.refs_0_), channel_id=1, source_target_pairs={{0,1},{1,2},{2,3},{3,0},{4,5},{5,6},{6,7},{7,4},{8,9},{9,10},{10,1... | collective-permute-start | bytes 1572872 | tf_op jit(solution)/shard_map/ppermute | solution.py:54
  22.4 1.8 %shard_map.57.refs_2_ = f32[128,2048]{1,0:T(8,128)S(1)} custom-call(s32[4,512]{1,0:T(4,128)S(1)} %get-tuple-element.28.ids_ref, s32[128,1]{1,0:T(8,128)S(1)} %get-tuple-element.29.labels_ref, bf16[2,2048,256]{2,1,0:T(8,128)(2,1)S(1)} %get-tuple-element.30.ta_ref, bf16[2,2048,256]{2,1,0:T(8,128)(2,1)S(1)} %get-tuple-element.31.tg_ref, ...), custom_call_target="tpu_custom_call" | custom-call | flops 1342177280 | bytes 1048576 | tf_op jit(solution)/shard_map/pallas_call | solution.py:160
  24.2 2.0 %collective-permute-start.14 = (bf16[2,2,2,64,256]{4,3,2,1,0:T(8,128)(2,1)S(1)}, bf16[2,2,2,64,256]{4,3,2,1,0:T(8,128)(2,1)S(1)}, u32[]{:S(2)}, u32[]{:S(2)}) collective-permute-start(bf16[2,2,2,64,256]{4,3,2,1,0:T(8,128)(2,1)S(1)} %slice.19), channel_id=1, source_target_pairs={{0,24},{1,25},{2,26},{3,27},{4,28},{5,29},{6,30},{7,31},{8,0},{9,1... | collective-permute-start | bytes 786440 | tf_op jit(solution)/shard_map/ppermute | solution.py:54
  26.3 3.2 %shard_map.58.refs_2_ = f32[128,2048]{1,0:T(8,128)S(1)} custom-call(s32[4,512]{1,0:T(4,128)S(1)} %get-tuple-element.28.ids_ref, s32[128,1]{1,0:T(8,128)S(1)} %get-tuple-element.29.labels_ref, bf16[2,2048,256]{2,1,0:T(8,128)(2,1)S(1)} %get-tuple-element.30.ta_ref, bf16[2,2048,256]{2,1,0:T(8,128)(2,1)S(1)} %get-tuple-element.31.tg_ref, ...), custom_call_target="tpu_custom_call" | custom-call | flops 2684354560 | bytes 1048576 | tf_op jit(solution)/shard_map/pallas_call | solution.py:160
  29.5 2.6 %collective-permute-done.9.refs_1_ = bf16[4,2,2,64,256]{4,3,2,1,0:T(8,128)(2,1)S(1)} collective-permute-done((bf16[4,2,2,64,256]{4,3,2,1,0:T(8,128)(2,1)S(1)}, bf16[4,2,2,64,256]{4,3,2,1,0:T(8,128)(2,1)S(1)}, u32[]{:S(2)}, u32[]{:S(2)}) %collective-permute-start.9) | collective-permute-done | bytes 524320 | tf_op jit(solution)/shard_map/ppermute | solution.py:54
  32.2 2.3 %collective-permute-start.10 = (bf16[2,2,2,64,256]{4,3,2,1,0:T(8,128)(2,1)S(1)}, bf16[2,2,2,64,256]{4,3,2,1,0:T(8,128)(2,1)S(1)}, u32[]{:S(2)}, u32[]{:S(2)}) collective-permute-start(bf16[2,2,2,64,256]{4,3,2,1,0:T(8,128)(2,1)S(1)} %slice.17), channel_id=1, source_target_pairs={{0,3},{1,0},{2,1},{3,2},{4,7},{5,4},{6,5},{7,6},{8,11},{9,8},{10,9... | collective-permute-start | bytes 786440 | tf_op jit(solution)/shard_map/ppermute | solution.py:54
  34.6 3.2 %shard_map.59.refs_2_ = f32[128,2048]{1,0:T(8,128)S(1)} custom-call(s32[4,512]{1,0:T(4,128)S(1)} %get-tuple-element.28.ids_ref, s32[128,1]{1,0:T(8,128)S(1)} %get-tuple-element.29.labels_ref, bf16[2,2048,256]{2,1,0:T(8,128)(2,1)S(1)} %get-tuple-element.30.ta_ref, bf16[2,2048,256]{2,1,0:T(8,128)(2,1)S(1)} %get-tuple-element.31.tg_ref, ...), custom_call_target="tpu_custom_call" | custom-call | flops 2684354560 | bytes 1048576 | tf_op jit(solution)/shard_map/pallas_call | solution.py:160
  37.8 1.8 %shard_map.60.refs_2_ = f32[128,2048]{1,0:T(8,128)S(1)} custom-call(s32[4,512]{1,0:T(4,128)S(1)} %get-tuple-element.28.ids_ref, s32[128,1]{1,0:T(8,128)S(1)} %get-tuple-element.29.labels_ref, bf16[2,2048,256]{2,1,0:T(8,128)(2,1)S(1)} %get-tuple-element.30.ta_ref, bf16[2,2048,256]{2,1,0:T(8,128)(2,1)S(1)} %get-tuple-element.31.tg_ref, ...), custom_call_target="tpu_custom_call" | custom-call | flops 1342177280 | bytes 1048576 | tf_op jit(solution)/shard_map/pallas_call | solution.py:160
  39.6 0.2 collective-permute-done.10.refs_1_
  39.8 3.8 %collective-permute-done.8.refs_0_ = bf16[2,2,2,64,256]{4,3,2,1,0:T(8,128)(2,1)S(1)} collective-permute-done((bf16[2,2,2,64,256]{4,3,2,1,0:T(8,128)(2,1)S(1)}, bf16[2,2,2,64,256]{4,3,2,1,0:T(8,128)(2,1)S(1)}, u32[]{:S(2)}, u32[]{:S(2)}) %collective-permute-start.8) | collective-permute-done | bytes 262176 | tf_op jit(solution)/shard_map/ppermute | solution.py:54
  43.6 1.8 %shard_map.61 = (f32[64,2048]{1,0:T(8,128)S(1)}, bf16[64,2048]{1,0:T(8,128)(2,1)S(1)}) custom-call(s32[4,512]{1,0:T(4,128)S(1)} %get-tuple-element.28.ids_ref, s32[128,1]{1,0:T(8,128)S(1)} %get-tuple-element.29.labels_ref, bf16[2,2048,256]{2,1,0:T(8,128)(2,1)S(1)} %get-tuple-element.30.ta_ref, bf16[2,2048,256]{2,1,0:T(8,128)(2,1)S(1)} %get-tuple-element.31.tg_ref, ...), custom_call_target="tpu_custom_call" | custom-call | flops 1342177280 | bytes 1048576 | tf_op jit(solution)/shard_map/pallas_call | solution.py:160
  45.4 2.2 %collective-permute-start.15 = (bf16[64,2048]{1,0:T(8,128)(2,1)S(1)}, bf16[64,2048]{1,0:T(8,128)(2,1)S(1)}, u32[]{:S(2)}, u32[]{:S(2)}) collective-permute-start(bf16[64,2048]{1,0:T(8,128)(2,1)S(1)} %get-tuple-element.42), channel_id=1, source_target_pairs={{0,32},{1,33},{2,34},{3,35},{4,36},{5,37},{6,38},{7,39},{8,40},{9,... | collective-permute-start | bytes 786440 | tf_op jit(solution)/shard_map/ppermute | solution.py:54
  47.6 1.2 %collective-permute-done.15.got_ref = bf16[64,2048]{1,0:T(8,128)(2,1)S(1)} collective-permute-done((bf16[64,2048]{1,0:T(8,128)(2,1)S(1)}, bf16[64,2048]{1,0:T(8,128)(2,1)S(1)}, u32[]{:S(2)}, u32[]{:S(2)}) %collective-permute-start.15) | collective-permute-done | bytes 262176 | tf_op jit(solution)/shard_map/ppermute | solution.py:54
  48.8 6.3 %collective-permute-start.16 = (bf16[16,2048]{1,0:T(8,128)(2,1)S(1)}, bf16[16,2048]{1,0:T(8,128)(2,1)S(1)}, u32[]{:S(2)}, u32[]{:S(2)}) collective-permute-start(bf16[16,2048]{1,0:T(8,128)(2,1)S(1)} %get-tuple-element.44), channel_id=1, source_target_pairs={{0,128},{1,129},{2,130},{3,131},{4,132},{5,133},{6,134},{7,135},{8... | collective-permute-start | bytes 196616 | tf_op jit(solution)/shard_map/ppermute | solution.py:54
  55.1 1.2 %collective-permute-start.17 = (bf16[16,2048]{1,0:T(8,128)(2,1)S(1)}, bf16[16,2048]{1,0:T(8,128)(2,1)S(1)}, u32[]{:S(2)}, u32[]{:S(2)}) collective-permute-start(bf16[16,2048]{1,0:T(8,128)(2,1)S(1)} %get-tuple-element.45), channel_id=1, source_target_pairs={{0,64},{1,65},{2,66},{3,67},{4,68},{5,69},{6,70},{7,71},{8,72},{9,... | collective-permute-start | bytes 196616 | tf_op jit(solution)/shard_map/ppermute | solution.py:54
  56.3 2.4 %collective-permute-start.18 = (bf16[16,2048]{1,0:T(8,128)(2,1)S(1)}, bf16[16,2048]{1,0:T(8,128)(2,1)S(1)}, u32[]{:S(2)}, u32[]{:S(2)}) collective-permute-start(bf16[16,2048]{1,0:T(8,128)(2,1)S(1)} %get-tuple-element.46), channel_id=1, source_target_pairs={{0,192},{1,193},{2,194},{3,195},{4,196},{5,197},{6,198},{7,199},{8... | collective-permute-start | bytes 196616 | tf_op jit(solution)/shard_map/ppermute | solution.py:54
  58.6 2.7 %collective-permute-done.17.refs_1_ = bf16[16,2048]{1,0:T(8,128)(2,1)S(1)} collective-permute-done((bf16[16,2048]{1,0:T(8,128)(2,1)S(1)}, bf16[16,2048]{1,0:T(8,128)(2,1)S(1)}, u32[]{:S(2)}, u32[]{:S(2)}) %collective-permute-start.17) | collective-permute-done | bytes 65568 | tf_op jit(solution)/shard_map/ppermute | solution.py:54
  61.4 0.7 %shard_map.63 = f32[16,2048]{1,0:T(8,128)} custom-call(f32[16,2048]{1,0:T(8,128)S(1)} %get-tuple-element.43.own_ref, bf16[16,2048]{1,0:T(8,128)(2,1)S(1)} %collective-permute-done.16.refs_0_, bf16[16,2048]{1,0:T(8,128)(2,1)S(1)} %collective-permute-done.17.refs_1_, bf16[16,2048]{1,0:T(8,128)(2,1)S(1)} %collective-permute-done.18.refs_2_), custom_call_target="tpu_custom_call" | custom-call | tf_op jit(solution)/shard_map/pallas_call | solution.py:202
  (24 shorter events, 0.5 us)
Async XLA Ops:
  0.9 8.4 %collective-permute-start = (bf16[2,2,64,256]{3,2,1,0:T(8,128)(2,1)S(1)}, bf16[2,2,64,256]{3,2,1,0:T(8,128)(2,1)S(1)}, u32[]{:S(2)}, u32[]{:S(2)}) collective-permute-start(bf16[2,2,64,256]{3,2,1,0:T(8,128)(2,1)S(1)} %get-tuple-element.48), channel_id=1, source_target_pairs={{0,4},{1,5},{2,6},{3,7},{4,0},{5,1},{6,2},{7,3},{8,12},{9,13},{10,... | collective-permute-start | bytes 393224 | tf_op jit(solution)/shard_map/ppermute | solution.py:54
  3.4 9.2 %collective-permute-start.2 = (bf16[2,2,64,256]{3,2,1,0:T(8,128)(2,1)S(1)}, bf16[2,2,64,256]{3,2,1,0:T(8,128)(2,1)S(1)}, u32[]{:S(2)}, u32[]{:S(2)}) collective-permute-start(bf16[2,2,64,256]{3,2,1,0:T(8,128)(2,1)S(1)} %get-tuple-element.48), channel_id=1, source_target_pairs={{0,1},{1,2},{2,3},{3,0},{4,5},{5,6},{6,7},{7,4},{8,9},{9,10},{10,1... | collective-permute-start | bytes 393224 | tf_op jit(solution)/shard_map/ppermute | solution.py:54
  4.7 10.3 %collective-permute-start.1 = (bf16[2,2,64,256]{3,2,1,0:T(8,128)(2,1)S(1)}, bf16[2,2,64,256]{3,2,1,0:T(8,128)(2,1)S(1)}, u32[]{:S(2)}, u32[]{:S(2)}) collective-permute-start(bf16[2,2,64,256]{3,2,1,0:T(8,128)(2,1)S(1)} %get-tuple-element.48), channel_id=1, source_target_pairs={{0,2},{1,3},{2,0},{3,1},{4,6},{5,7},{6,4},{7,5},{8,10},{9,11},{10,... | collective-permute-start | bytes 393224 | tf_op jit(solution)/shard_map/ppermute | solution.py:54
  7.1 7.9 %collective-permute-start.3 = (bf16[2,2,64,256]{3,2,1,0:T(8,128)(2,1)S(1)}, bf16[2,2,64,256]{3,2,1,0:T(8,128)(2,1)S(1)}, u32[]{:S(2)}, u32[]{:S(2)}) collective-permute-start(bf16[2,2,64,256]{3,2,1,0:T(8,128)(2,1)S(1)} %get-tuple-element.48), channel_id=1, source_target_pairs={{0,3},{1,0},{2,1},{3,2},{4,7},{5,4},{6,5},{7,6},{8,11},{9,8},{10,9... | collective-permute-start | bytes 393224 | tf_op jit(solution)/shard_map/ppermute | solution.py:54
  8.3 0.7 %copy-start = (s32[2048]{0:T(1024)S(1)}, s32[2048]{0:T(1024)}, u32[]{:S(2)}) copy-start(s32[2048]{0:T(1024)} %param.9) | copy-start | bytes 24580
  9.3 11.4 %collective-permute-start.6 = (bf16[2,2,64,256]{3,2,1,0:T(8,128)(2,1)S(1)}, bf16[2,2,64,256]{3,2,1,0:T(8,128)(2,1)S(1)}, u32[]{:S(2)}, u32[]{:S(2)}) collective-permute-start(bf16[2,2,64,256]{3,2,1,0:T(8,128)(2,1)S(1)} %collective-permute-done), channel_id=1, source_target_pairs={{0,16},{1,17},{2,18},{3,19},{4,20},{5,21},{6,22},{7,23},{8,24},{9,... | collective-permute-start | bytes 393224 | tf_op jit(solution)/shard_map/ppermute | solution.py:54
  12.3 8.4 %collective-permute-start.5 = (bf16[2,2,64,256]{3,2,1,0:T(8,128)(2,1)S(1)}, bf16[2,2,64,256]{3,2,1,0:T(8,128)(2,1)S(1)}, u32[]{:S(2)}, u32[]{:S(2)}) collective-permute-start(bf16[2,2,64,256]{3,2,1,0:T(8,128)(2,1)S(1)} %collective-permute-done), channel_id=1, source_target_pairs={{0,8},{1,9},{2,10},{3,11},{4,12},{5,13},{6,14},{7,15},{8,16},{9,17... | collective-permute-start | bytes 393224 | tf_op jit(solution)/shard_map/ppermute | solution.py:54
  12.7 8.1 %collective-permute-start.4 = (bf16[2,2,64,256]{3,2,1,0:T(8,128)(2,1)S(1)}, bf16[2,2,64,256]{3,2,1,0:T(8,128)(2,1)S(1)}, u32[]{:S(2)}, u32[]{:S(2)}) collective-permute-start(bf16[2,2,64,256]{3,2,1,0:T(8,128)(2,1)S(1)} %collective-permute-done), channel_id=1, source_target_pairs={{0,24},{1,25},{2,26},{3,27},{4,28},{5,29},{6,30},{7,31},{8,0},{9,1... | collective-permute-start | bytes 393224 | tf_op jit(solution)/shard_map/ppermute | solution.py:54
  15.1 9.1 %collective-permute-start.13 = (bf16[4,2,2,64,256]{4,3,2,1,0:T(8,128)(2,1)S(1)}, bf16[4,2,2,64,256]{4,3,2,1,0:T(8,128)(2,1)S(1)}, u32[]{:S(2)}, u32[]{:S(2)}) collective-permute-start(bf16[4,2,2,64,256]{4,3,2,1,0:T(8,128)(2,1)S(1)} %pad_maximum_fusion.refs_0_), channel_id=1, source_target_pairs={{0,24},{1,25},{2,26},{3,27},{4,28},{5,29},{6,30},{7,31},{8,0},{9,1... | collective-permute-start | bytes 1572872 | tf_op jit(solution)/shard_map/ppermute | solution.py:54
  15.1 11.1 %collective-permute-start.11 = (bf16[4,2,2,64,256]{4,3,2,1,0:T(8,128)(2,1)S(1)}, bf16[4,2,2,64,256]{4,3,2,1,0:T(8,128)(2,1)S(1)}, u32[]{:S(2)}, u32[]{:S(2)}) collective-permute-start(bf16[4,2,2,64,256]{4,3,2,1,0:T(8,128)(2,1)S(1)} %pad_maximum_fusion.refs_0_), channel_id=1, source_target_pairs={{0,8},{1,9},{2,10},{3,11},{4,12},{5,13},{6,14},{7,15},{8,16},{9,17... | collective-permute-start | bytes 1572872 | tf_op jit(solution)/shard_map/ppermute | solution.py:54
  20.8 11.3 %collective-permute-start.9 = (bf16[4,2,2,64,256]{4,3,2,1,0:T(8,128)(2,1)S(1)}, bf16[4,2,2,64,256]{4,3,2,1,0:T(8,128)(2,1)S(1)}, u32[]{:S(2)}, u32[]{:S(2)}) collective-permute-start(bf16[4,2,2,64,256]{4,3,2,1,0:T(8,128)(2,1)S(1)} %pad_maximum_fusion.1.refs_0_), channel_id=1, source_target_pairs={{0,3},{1,0},{2,1},{3,2},{4,7},{5,4},{6,5},{7,6},{8,11},{9,8},{10,9... | collective-permute-start | bytes 1572872 | tf_op jit(solution)/shard_map/ppermute | solution.py:54
  20.9 13.5 %collective-permute-start.7 = (bf16[4,2,2,64,256]{4,3,2,1,0:T(8,128)(2,1)S(1)}, bf16[4,2,2,64,256]{4,3,2,1,0:T(8,128)(2,1)S(1)}, u32[]{:S(2)}, u32[]{:S(2)}) collective-permute-start(bf16[4,2,2,64,256]{4,3,2,1,0:T(8,128)(2,1)S(1)} %pad_maximum_fusion.1.refs_0_), channel_id=1, source_target_pairs={{0,1},{1,2},{2,3},{3,0},{4,5},{5,6},{6,7},{7,4},{8,9},{9,10},{10,1... | collective-permute-start | bytes 1572872 | tf_op jit(solution)/shard_map/ppermute | solution.py:54
  24.2 13.6 %collective-permute-start.14 = (bf16[2,2,2,64,256]{4,3,2,1,0:T(8,128)(2,1)S(1)}, bf16[2,2,2,64,256]{4,3,2,1,0:T(8,128)(2,1)S(1)}, u32[]{:S(2)}, u32[]{:S(2)}) collective-permute-start(bf16[2,2,2,64,256]{4,3,2,1,0:T(8,128)(2,1)S(1)} %slice.19), channel_id=1, source_target_pairs={{0,24},{1,25},{2,26},{3,27},{4,28},{5,29},{6,30},{7,31},{8,0},{9,1... | collective-permute-start | bytes 786440 | tf_op jit(solution)/shard_map/ppermute | solution.py:54
  26.2 11.6 %collective-permute-start.12 = (bf16[2,2,2,64,256]{4,3,2,1,0:T(8,128)(2,1)S(1)}, bf16[2,2,2,64,256]{4,3,2,1,0:T(8,128)(2,1)S(1)}, u32[]{:S(2)}, u32[]{:S(2)}) collective-permute-start(bf16[2,2,2,64,256]{4,3,2,1,0:T(8,128)(2,1)S(1)} %slice.18), channel_id=1, source_target_pairs={{0,8},{1,9},{2,10},{3,11},{4,12},{5,13},{6,14},{7,15},{8,16},{9,17... | collective-permute-start | bytes 786440 | tf_op jit(solution)/shard_map/ppermute | solution.py:54
  32.2 7.6 %collective-permute-start.10 = (bf16[2,2,2,64,256]{4,3,2,1,0:T(8,128)(2,1)S(1)}, bf16[2,2,2,64,256]{4,3,2,1,0:T(8,128)(2,1)S(1)}, u32[]{:S(2)}, u32[]{:S(2)}) collective-permute-start(bf16[2,2,2,64,256]{4,3,2,1,0:T(8,128)(2,1)S(1)} %slice.17), channel_id=1, source_target_pairs={{0,3},{1,0},{2,1},{3,2},{4,7},{5,4},{6,5},{7,6},{8,11},{9,8},{10,9... | collective-permute-start | bytes 786440 | tf_op jit(solution)/shard_map/ppermute | solution.py:54
  34.5 9.1 %collective-permute-start.8 = (bf16[2,2,2,64,256]{4,3,2,1,0:T(8,128)(2,1)S(1)}, bf16[2,2,2,64,256]{4,3,2,1,0:T(8,128)(2,1)S(1)}, u32[]{:S(2)}, u32[]{:S(2)}) collective-permute-start(bf16[2,2,2,64,256]{4,3,2,1,0:T(8,128)(2,1)S(1)} %slice.16), channel_id=1, source_target_pairs={{0,1},{1,2},{2,3},{3,0},{4,5},{5,6},{6,7},{7,4},{8,9},{9,10},{10,1... | collective-permute-start | bytes 786440 | tf_op jit(solution)/shard_map/ppermute | solution.py:54
  45.4 3.4 %collective-permute-start.15 = (bf16[64,2048]{1,0:T(8,128)(2,1)S(1)}, bf16[64,2048]{1,0:T(8,128)(2,1)S(1)}, u32[]{:S(2)}, u32[]{:S(2)}) collective-permute-start(bf16[64,2048]{1,0:T(8,128)(2,1)S(1)} %get-tuple-element.42), channel_id=1, source_target_pairs={{0,32},{1,33},{2,34},{3,35},{4,36},{5,37},{6,38},{7,39},{8,40},{9,... | collective-permute-start | bytes 786440 | tf_op jit(solution)/shard_map/ppermute | solution.py:54
  48.8 9.8 %collective-permute-start.16 = (bf16[16,2048]{1,0:T(8,128)(2,1)S(1)}, bf16[16,2048]{1,0:T(8,128)(2,1)S(1)}, u32[]{:S(2)}, u32[]{:S(2)}) collective-permute-start(bf16[16,2048]{1,0:T(8,128)(2,1)S(1)} %get-tuple-element.44), channel_id=1, source_target_pairs={{0,128},{1,129},{2,130},{3,131},{4,132},{5,133},{6,134},{7,135},{8... | collective-permute-start | bytes 196616 | tf_op jit(solution)/shard_map/ppermute | solution.py:54
  55.1 6.3 %collective-permute-start.17 = (bf16[16,2048]{1,0:T(8,128)(2,1)S(1)}, bf16[16,2048]{1,0:T(8,128)(2,1)S(1)}, u32[]{:S(2)}, u32[]{:S(2)}) collective-permute-start(bf16[16,2048]{1,0:T(8,128)(2,1)S(1)} %get-tuple-element.45), channel_id=1, source_target_pairs={{0,64},{1,65},{2,66},{3,67},{4,68},{5,69},{6,70},{7,71},{8,72},{9,... | collective-permute-start | bytes 196616 | tf_op jit(solution)/shard_map/ppermute | solution.py:54
  56.3 5.1 %collective-permute-start.18 = (bf16[16,2048]{1,0:T(8,128)(2,1)S(1)}, bf16[16,2048]{1,0:T(8,128)(2,1)S(1)}, u32[]{:S(2)}, u32[]{:S(2)}) collective-permute-start(bf16[16,2048]{1,0:T(8,128)(2,1)S(1)} %get-tuple-element.46), channel_id=1, source_target_pairs={{0,192},{1,193},{2,194},{3,195},{4,196},{5,197},{6,198},{7,199},{8... | collective-permute-start | bytes 196616 | tf_op jit(solution)/shard_map/ppermute | solution.py:54

commit v6 on v5

--- a/solution.py
+++ b/solution.py
@@ -47,7 +47,7 @@
 
 
 def along_z(d):
-    return moves(lambda h, c, x, z, y: (h + d, c, x, z, y))
+    return moves(lambda h, c, x, z, y: (h + d if c == 0 else h - d, c, x, z, y))
 
 
 def send(value, pairs):
@@ -76,7 +76,8 @@
                 query_ref[row : row + 1, at : at + 128] = jnp.where(lane < 64, got[0], got[1])
     r = lax.broadcasted_iota(jnp.int32, (Q, 1), 0)
     owner = jnp.where(r < 64, core, 1 - core)
-    label_ref[...] = (z_hi + (r % 64) // 16) % 4 * 32 + owner * 16 + r % 16
+    part = (r % 64) // 16
+    label_ref[...] = (z_hi + jnp.where(owner == 0, part, 4 - part)) % 4 * 32 + owner * 16 + r % 16
 
 
 def prepare(layer, tok, segment_ids):

time: 62.9 us -> 62.5 us (level)
  starting transfers between devices: 32.6 us -> 31.4 us
    ppermute x19, starting transfers between devices: 32.6 us -> 31.4 us  [send(): return lax.ppermute(value, AXES, pairs)]
where the time goes in v6:
time: 62.5 us; the launch traced here: 61.4 us
  starting transfers between devices  31.4 us (50%)
  Pallas kernels  16.9 us (27%)
  waiting for transfers between devices  11.1 us (18%)
  other arithmetic  1.03 us (2%)
  local copies, waits for them, and re-layouts  0.77 us (1%)
    ppermute x19, starting transfers between devices, send(): return lax.ppermute(value, AXES, pairs)  31.4 us
    pallas_call x6, Pallas kernels, chunk(): pl.pallas_call(functools.partial(chunk_kernel, pieces, first, last, len(b...  15.8 us
    ppermute x19, waiting for transfers between devices, send(): return lax.ppermute(value, AXES, pairs)  11.1 us
  transfers between devices with their start and end apart: 19, of which 5 were waited for; matrix products, arithmetic and copies ran while one was open for 0% of the time, Pallas kernels for 23%

profile of v6, /device:TPU:1, one launch (start us, length us, event | category | flops | bytes accessed | tf_op | source)
XLA Modules:
  0.0 61.4 jit_solution(10175809405075998926)
XLA Ops:
  0.0 0.9 %fusion = (bf16[1,2,2,64,256]{4,3,2,1,0:T(8,128)(2,1)S(1)}, bf16[2,2,64,256]{3,2,1,0:T(8,128)(2,1)S(1)}) fusion(bf16[1,2,64,256]{3,2,1,0:T(8,128)(2,1)} %bitcast.22, bf16[1,2,64,256]{3,2,1,0:T(8,128)(2,1)} %bitcast.23), kind=kLoop, calls=%fused_computation.3 | loop fusion | flops 65536 | bytes 393216 | tf_op jit(solution)/shard_map/stack | solution.py:221
  0.9 2.6 %collective-permute-start = (bf16[2,2,64,256]{3,2,1,0:T(8,128)(2,1)S(1)}, bf16[2,2,64,256]{3,2,1,0:T(8,128)(2,1)S(1)}, u32[]{:S(2)}, u32[]{:S(2)}) collective-permute-start(bf16[2,2,64,256]{3,2,1,0:T(8,128)(2,1)S(1)} %get-tuple-element.48), channel_id=1, source_target_pairs={{0,4},{1,5},{2,6},{3,7},{4,0},{5,1},{6,2},{7,3},{8,12},{9,13},{10,... | collective-permute-start | bytes 393224 | tf_op jit(solution)/shard_map/ppermute | solution.py:54
  3.4 1.2 %collective-permute-start.2 = (bf16[2,2,64,256]{3,2,1,0:T(8,128)(2,1)S(1)}, bf16[2,2,64,256]{3,2,1,0:T(8,128)(2,1)S(1)}, u32[]{:S(2)}, u32[]{:S(2)}) collective-permute-start(bf16[2,2,64,256]{3,2,1,0:T(8,128)(2,1)S(1)} %get-tuple-element.48), channel_id=1, source_target_pairs={{0,1},{1,2},{2,3},{3,0},{4,5},{5,6},{6,7},{7,4},{8,9},{9,10},{10,1... | collective-permute-start | bytes 393224 | tf_op jit(solution)/shard_map/ppermute | solution.py:54
  4.7 2.5 %collective-permute-start.1 = (bf16[2,2,64,256]{3,2,1,0:T(8,128)(2,1)S(1)}, bf16[2,2,64,256]{3,2,1,0:T(8,128)(2,1)S(1)}, u32[]{:S(2)}, u32[]{:S(2)}) collective-permute-start(bf16[2,2,64,256]{3,2,1,0:T(8,128)(2,1)S(1)} %get-tuple-element.48), channel_id=1, source_target_pairs={{0,2},{1,3},{2,0},{3,1},{4,6},{5,7},{6,4},{7,5},{8,10},{9,11},{10,... | collective-permute-start | bytes 393224 | tf_op jit(solution)/shard_map/ppermute | solution.py:54
  7.1 1.2 %collective-permute-start.3 = (bf16[2,2,64,256]{3,2,1,0:T(8,128)(2,1)S(1)}, bf16[2,2,64,256]{3,2,1,0:T(8,128)(2,1)S(1)}, u32[]{:S(2)}, u32[]{:S(2)}) collective-permute-start(bf16[2,2,64,256]{3,2,1,0:T(8,128)(2,1)S(1)} %get-tuple-element.48), channel_id=1, source_target_pairs={{0,3},{1,0},{2,1},{3,2},{4,7},{5,4},{6,5},{7,6},{8,11},{9,8},{10,9... | collective-permute-start | bytes 393224 | tf_op jit(solution)/shard_map/ppermute | solution.py:54
  8.3 0.7 %copy-done = s32[2048]{0:T(1024)S(1)} copy-done((s32[2048]{0:T(1024)S(1)}, s32[2048]{0:T(1024)}, u32[]{:S(2)}) %copy-start) | copy-done | bytes 8216
  9.0 0.3 shard_map.55
  9.3 3.0 %collective-permute-start.6 = (bf16[2,2,64,256]{3,2,1,0:T(8,128)(2,1)S(1)}, bf16[2,2,64,256]{3,2,1,0:T(8,128)(2,1)S(1)}, u32[]{:S(2)}, u32[]{:S(2)}) collective-permute-start(bf16[2,2,64,256]{3,2,1,0:T(8,128)(2,1)S(1)} %collective-permute-done), channel_id=1, source_target_pairs={{0,16},{1,17},{2,18},{3,19},{4,20},{5,21},{6,22},{7,23},{8,24},{9,... | collective-permute-start | bytes 393224 | tf_op jit(solution)/shard_map/ppermute | solution.py:54
  12.3 0.4 collective-permute-start.5
  12.7 2.3 %collective-permute-start.4 = (bf16[2,2,64,256]{3,2,1,0:T(8,128)(2,1)S(1)}, bf16[2,2,64,256]{3,2,1,0:T(8,128)(2,1)S(1)}, u32[]{:S(2)}, u32[]{:S(2)}) collective-permute-start(bf16[2,2,64,256]{3,2,1,0:T(8,128)(2,1)S(1)} %collective-permute-done), channel_id=1, source_target_pairs={{0,24},{1,25},{2,26},{3,27},{4,28},{5,29},{6,30},{7,31},{8,0},{9,1... | collective-permute-start | bytes 393224 | tf_op jit(solution)/shard_map/ppermute | solution.py:54
  15.1 0.1 collective-permute-start.13
  15.2 1.4 %collective-permute-start.11 = (bf16[4,2,2,64,256]{4,3,2,1,0:T(8,128)(2,1)S(1)}, bf16[4,2,2,64,256]{4,3,2,1,0:T(8,128)(2,1)S(1)}, u32[]{:S(2)}, u32[]{:S(2)}) collective-permute-start(bf16[4,2,2,64,256]{4,3,2,1,0:T(8,128)(2,1)S(1)} %pad_maximum_fusion.refs_0_), channel_id=1, source_target_pairs={{0,8},{1,9},{2,10},{3,11},{4,12},{5,13},{6,14},{7,15},{8,16},{9,17... | collective-permute-start | bytes 1572872 | tf_op jit(solution)/shard_map/ppermute | solution.py:54
  16.6 4.1 %shard_map.56 = (f32[128,2048]{1,0:T(8,128)S(1)}, bf16[2,2048,256]{2,1,0:T(8,128)(2,1)S(1)}, bf16[2,2048,256]{2,1,0:T(8,128)(2,1)S(1)}) custom-call(s32[4,512]{1,0:T(4,128)S(1)} %get-tuple-element.28.ids_ref, s32[128,1]{1,0:T(8,128)S(1)} %get-tuple-element.29.labels_ref, bf16[2,2048,256]{2,1,0:T(8,128)(2,1)} %ta_ref.1, bf16[2,2048,256]{2,1,0:T(8,128)(2,1)} %tg_ref.1, ...), custom_call_target="tpu_custom_call" | custom-call | flops 1342177280 | bytes 1048576 | tf_op jit(solution)/shard_map/pallas_call | solution.py:161
  20.8 0.1 collective-permute-start.9
  20.9 1.5 %collective-permute-start.7 = (bf16[4,2,2,64,256]{4,3,2,1,0:T(8,128)(2,1)S(1)}, bf16[4,2,2,64,256]{4,3,2,1,0:T(8,128)(2,1)S(1)}, u32[]{:S(2)}, u32[]{:S(2)}) collective-permute-start(bf16[4,2,2,64,256]{4,3,2,1,0:T(8,128)(2,1)S(1)} %pad_maximum_fusion.1.refs_0_), channel_id=1, source_target_pairs={{0,1},{1,2},{2,3},{3,0},{4,5},{5,6},{6,7},{7,4},{8,9},{9,10},{10,1... | collective-permute-start | bytes 1572872 | tf_op jit(solution)/shard_map/ppermute | solution.py:54
  22.4 1.8 %shard_map.57.refs_2_ = f32[128,2048]{1,0:T(8,128)S(1)} custom-call(s32[4,512]{1,0:T(4,128)S(1)} %get-tuple-element.28.ids_ref, s32[128,1]{1,0:T(8,128)S(1)} %get-tuple-element.29.labels_ref, bf16[2,2048,256]{2,1,0:T(8,128)(2,1)S(1)} %get-tuple-element.30.ta_ref, bf16[2,2048,256]{2,1,0:T(8,128)(2,1)S(1)} %get-tuple-element.31.tg_ref, ...), custom_call_target="tpu_custom_call" | custom-call | flops 1342177280 | bytes 1048576 | tf_op jit(solution)/shard_map/pallas_call | solution.py:161
  24.2 2.0 %collective-permute-start.14 = (bf16[2,2,2,64,256]{4,3,2,1,0:T(8,128)(2,1)S(1)}, bf16[2,2,2,64,256]{4,3,2,1,0:T(8,128)(2,1)S(1)}, u32[]{:S(2)}, u32[]{:S(2)}) collective-permute-start(bf16[2,2,2,64,256]{4,3,2,1,0:T(8,128)(2,1)S(1)} %slice.19), channel_id=1, source_target_pairs={{0,24},{1,25},{2,26},{3,27},{4,28},{5,29},{6,30},{7,31},{8,0},{9,1... | collective-permute-start | bytes 786440 | tf_op jit(solution)/shard_map/ppermute | solution.py:54
  26.3 3.2 %shard_map.58.refs_2_ = f32[128,2048]{1,0:T(8,128)S(1)} custom-call(s32[4,512]{1,0:T(4,128)S(1)} %get-tuple-element.28.ids_ref, s32[128,1]{1,0:T(8,128)S(1)} %get-tuple-element.29.labels_ref, bf16[2,2048,256]{2,1,0:T(8,128)(2,1)S(1)} %get-tuple-element.30.ta_ref, bf16[2,2048,256]{2,1,0:T(8,128)(2,1)S(1)} %get-tuple-element.31.tg_ref, ...), custom_call_target="tpu_custom_call" | custom-call | flops 2684354560 | bytes 1048576 | tf_op jit(solution)/shard_map/pallas_call | solution.py:161
  29.5 2.6 %collective-permute-done.9.refs_1_ = bf16[4,2,2,64,256]{4,3,2,1,0:T(8,128)(2,1)S(1)} collective-permute-done((bf16[4,2,2,64,256]{4,3,2,1,0:T(8,128)(2,1)S(1)}, bf16[4,2,2,64,256]{4,3,2,1,0:T(8,128)(2,1)S(1)}, u32[]{:S(2)}, u32[]{:S(2)}) %collective-permute-start.9) | collective-permute-done | bytes 524320 | tf_op jit(solution)/shard_map/ppermute | solution.py:54
  32.2 2.3 %collective-permute-start.10 = (bf16[2,2,2,64,256]{4,3,2,1,0:T(8,128)(2,1)S(1)}, bf16[2,2,2,64,256]{4,3,2,1,0:T(8,128)(2,1)S(1)}, u32[]{:S(2)}, u32[]{:S(2)}) collective-permute-start(bf16[2,2,2,64,256]{4,3,2,1,0:T(8,128)(2,1)S(1)} %slice.17), channel_id=1, source_target_pairs={{0,3},{1,0},{2,1},{3,2},{4,7},{5,4},{6,5},{7,6},{8,11},{9,8},{10,9... | collective-permute-start | bytes 786440 | tf_op jit(solution)/shard_map/ppermute | solution.py:54
  34.6 3.2 %shard_map.59.refs_2_ = f32[128,2048]{1,0:T(8,128)S(1)} custom-call(s32[4,512]{1,0:T(4,128)S(1)} %get-tuple-element.28.ids_ref, s32[128,1]{1,0:T(8,128)S(1)} %get-tuple-element.29.labels_ref, bf16[2,2048,256]{2,1,0:T(8,128)(2,1)S(1)} %get-tuple-element.30.ta_ref, bf16[2,2048,256]{2,1,0:T(8,128)(2,1)S(1)} %get-tuple-element.31.tg_ref, ...), custom_call_target="tpu_custom_call" | custom-call | flops 2684354560 | bytes 1048576 | tf_op jit(solution)/shard_map/pallas_call | solution.py:161
  37.8 1.8 %shard_map.60.refs_2_ = f32[128,2048]{1,0:T(8,128)S(1)} custom-call(s32[4,512]{1,0:T(4,128)S(1)} %get-tuple-element.28.ids_ref, s32[128,1]{1,0:T(8,128)S(1)} %get-tuple-element.29.labels_ref, bf16[2,2048,256]{2,1,0:T(8,128)(2,1)S(1)} %get-tuple-element.30.ta_ref, bf16[2,2048,256]{2,1,0:T(8,128)(2,1)S(1)} %get-tuple-element.31.tg_ref, ...), custom_call_target="tpu_custom_call" | custom-call | flops 1342177280 | bytes 1048576 | tf_op jit(solution)/shard_map/pallas_call | solution.py:161
  39.6 0.2 collective-permute-done.10.refs_1_
  39.8 3.8 %collective-permute-done.8.refs_0_ = bf16[2,2,2,64,256]{4,3,2,1,0:T(8,128)(2,1)S(1)} collective-permute-done((bf16[2,2,2,64,256]{4,3,2,1,0:T(8,128)(2,1)S(1)}, bf16[2,2,2,64,256]{4,3,2,1,0:T(8,128)(2,1)S(1)}, u32[]{:S(2)}, u32[]{:S(2)}) %collective-permute-start.8) | collective-permute-done | bytes 262176 | tf_op jit(solution)/shard_map/ppermute | solution.py:54
  43.6 1.8 %shard_map.61 = (f32[64,2048]{1,0:T(8,128)S(1)}, bf16[64,2048]{1,0:T(8,128)(2,1)S(1)}) custom-call(s32[4,512]{1,0:T(4,128)S(1)} %get-tuple-element.28.ids_ref, s32[128,1]{1,0:T(8,128)S(1)} %get-tuple-element.29.labels_ref, bf16[2,2048,256]{2,1,0:T(8,128)(2,1)S(1)} %get-tuple-element.30.ta_ref, bf16[2,2048,256]{2,1,0:T(8,128)(2,1)S(1)} %get-tuple-element.31.tg_ref, ...), custom_call_target="tpu_custom_call" | custom-call | flops 1342177280 | bytes 1048576 | tf_op jit(solution)/shard_map/pallas_call | solution.py:161
  45.4 2.2 %collective-permute-start.15 = (bf16[64,2048]{1,0:T(8,128)(2,1)S(1)}, bf16[64,2048]{1,0:T(8,128)(2,1)S(1)}, u32[]{:S(2)}, u32[]{:S(2)}) collective-permute-start(bf16[64,2048]{1,0:T(8,128)(2,1)S(1)} %get-tuple-element.42), channel_id=1, source_target_pairs={{0,32},{1,33},{2,34},{3,35},{4,36},{5,37},{6,38},{7,39},{8,40},{9,... | collective-permute-start | bytes 786440 | tf_op jit(solution)/shard_map/ppermute | solution.py:54
  47.6 1.2 %collective-permute-done.15.got_ref = bf16[64,2048]{1,0:T(8,128)(2,1)S(1)} collective-permute-done((bf16[64,2048]{1,0:T(8,128)(2,1)S(1)}, bf16[64,2048]{1,0:T(8,128)(2,1)S(1)}, u32[]{:S(2)}, u32[]{:S(2)}) %collective-permute-start.15) | collective-permute-done | bytes 262176 | tf_op jit(solution)/shard_map/ppermute | solution.py:54
  48.8 6.2 %collective-permute-start.16 = (bf16[16,2048]{1,0:T(8,128)(2,1)S(1)}, bf16[16,2048]{1,0:T(8,128)(2,1)S(1)}, u32[]{:S(2)}, u32[]{:S(2)}) collective-permute-start(bf16[16,2048]{1,0:T(8,128)(2,1)S(1)} %get-tuple-element.44), channel_id=1, source_target_pairs={{0,128},{1,129},{2,130},{3,131},{4,132},{5,133},{6,134},{7,135},{8... | collective-permute-start | bytes 196616 | tf_op jit(solution)/shard_map/ppermute | solution.py:54
  55.1 0.1 collective-permute-start.17
  55.2 2.3 %collective-permute-start.18 = (bf16[16,2048]{1,0:T(8,128)(2,1)S(1)}, bf16[16,2048]{1,0:T(8,128)(2,1)S(1)}, u32[]{:S(2)}, u32[]{:S(2)}) collective-permute-start(bf16[16,2048]{1,0:T(8,128)(2,1)S(1)} %get-tuple-element.46), channel_id=1, source_target_pairs={{0,192},{1,193},{2,194},{3,195},{4,196},{5,197},{6,198},{7,199},{8... | collective-permute-start | bytes 196616 | tf_op jit(solution)/shard_map/ppermute | solution.py:54
  57.4 3.3 %collective-permute-done.17.refs_1_ = bf16[16,2048]{1,0:T(8,128)(2,1)S(1)} collective-permute-done((bf16[16,2048]{1,0:T(8,128)(2,1)S(1)}, bf16[16,2048]{1,0:T(8,128)(2,1)S(1)}, u32[]{:S(2)}, u32[]{:S(2)}) %collective-permute-start.17) | collective-permute-done | bytes 65568 | tf_op jit(solution)/shard_map/ppermute | solution.py:54
  60.7 0.7 %shard_map.63 = f32[16,2048]{1,0:T(8,128)} custom-call(f32[16,2048]{1,0:T(8,128)S(1)} %get-tuple-element.43.own_ref, bf16[16,2048]{1,0:T(8,128)(2,1)S(1)} %collective-permute-done.16.refs_0_, bf16[16,2048]{1,0:T(8,128)(2,1)S(1)} %collective-permute-done.17.refs_1_, bf16[16,2048]{1,0:T(8,128)(2,1)S(1)} %collective-permute-done.18.refs_2_), custom_call_target="tpu_custom_call" | custom-call | tf_op jit(solution)/shard_map/pallas_call | solution.py:203
  (24 shorter events, 0.5 us)
Async XLA Ops:
  0.9 8.4 %collective-permute-start = (bf16[2,2,64,256]{3,2,1,0:T(8,128)(2,1)S(1)}, bf16[2,2,64,256]{3,2,1,0:T(8,128)(2,1)S(1)}, u32[]{:S(2)}, u32[]{:S(2)}) collective-permute-start(bf16[2,2,64,256]{3,2,1,0:T(8,128)(2,1)S(1)} %get-tuple-element.48), channel_id=1, source_target_pairs={{0,4},{1,5},{2,6},{3,7},{4,0},{5,1},{6,2},{7,3},{8,12},{9,13},{10,... | collective-permute-start | bytes 393224 | tf_op jit(solution)/shard_map/ppermute | solution.py:54
  3.4 9.3 %collective-permute-start.2 = (bf16[2,2,64,256]{3,2,1,0:T(8,128)(2,1)S(1)}, bf16[2,2,64,256]{3,2,1,0:T(8,128)(2,1)S(1)}, u32[]{:S(2)}, u32[]{:S(2)}) collective-permute-start(bf16[2,2,64,256]{3,2,1,0:T(8,128)(2,1)S(1)} %get-tuple-element.48), channel_id=1, source_target_pairs={{0,1},{1,2},{2,3},{3,0},{4,5},{5,6},{6,7},{7,4},{8,9},{9,10},{10,1... | collective-permute-start | bytes 393224 | tf_op jit(solution)/shard_map/ppermute | solution.py:54
  4.7 10.3 %collective-permute-start.1 = (bf16[2,2,64,256]{3,2,1,0:T(8,128)(2,1)S(1)}, bf16[2,2,64,256]{3,2,1,0:T(8,128)(2,1)S(1)}, u32[]{:S(2)}, u32[]{:S(2)}) collective-permute-start(bf16[2,2,64,256]{3,2,1,0:T(8,128)(2,1)S(1)} %get-tuple-element.48), channel_id=1, source_target_pairs={{0,2},{1,3},{2,0},{3,1},{4,6},{5,7},{6,4},{7,5},{8,10},{9,11},{10,... | collective-permute-start | bytes 393224 | tf_op jit(solution)/shard_map/ppermute | solution.py:54
  7.1 7.9 %collective-permute-start.3 = (bf16[2,2,64,256]{3,2,1,0:T(8,128)(2,1)S(1)}, bf16[2,2,64,256]{3,2,1,0:T(8,128)(2,1)S(1)}, u32[]{:S(2)}, u32[]{:S(2)}) collective-permute-start(bf16[2,2,64,256]{3,2,1,0:T(8,128)(2,1)S(1)} %get-tuple-element.48), channel_id=1, source_target_pairs={{0,3},{1,0},{2,1},{3,2},{4,7},{5,4},{6,5},{7,6},{8,11},{9,8},{10,9... | collective-permute-start | bytes 393224 | tf_op jit(solution)/shard_map/ppermute | solution.py:54
  8.3 0.7 %copy-start = (s32[2048]{0:T(1024)S(1)}, s32[2048]{0:T(1024)}, u32[]{:S(2)}) copy-start(s32[2048]{0:T(1024)} %param.9) | copy-start | bytes 24580
  9.3 11.4 %collective-permute-start.6 = (bf16[2,2,64,256]{3,2,1,0:T(8,128)(2,1)S(1)}, bf16[2,2,64,256]{3,2,1,0:T(8,128)(2,1)S(1)}, u32[]{:S(2)}, u32[]{:S(2)}) collective-permute-start(bf16[2,2,64,256]{3,2,1,0:T(8,128)(2,1)S(1)} %collective-permute-done), channel_id=1, source_target_pairs={{0,16},{1,17},{2,18},{3,19},{4,20},{5,21},{6,22},{7,23},{8,24},{9,... | collective-permute-start | bytes 393224 | tf_op jit(solution)/shard_map/ppermute | solution.py:54
  12.3 8.4 %collective-permute-start.5 = (bf16[2,2,64,256]{3,2,1,0:T(8,128)(2,1)S(1)}, bf16[2,2,64,256]{3,2,1,0:T(8,128)(2,1)S(1)}, u32[]{:S(2)}, u32[]{:S(2)}) collective-permute-start(bf16[2,2,64,256]{3,2,1,0:T(8,128)(2,1)S(1)} %collective-permute-done), channel_id=1, source_target_pairs={{0,8},{1,9},{2,10},{3,11},{4,12},{5,13},{6,14},{7,15},{8,16},{9,17... | collective-permute-start | bytes 393224 | tf_op jit(solution)/shard_map/ppermute | solution.py:54
  12.7 8.1 %collective-permute-start.4 = (bf16[2,2,64,256]{3,2,1,0:T(8,128)(2,1)S(1)}, bf16[2,2,64,256]{3,2,1,0:T(8,128)(2,1)S(1)}, u32[]{:S(2)}, u32[]{:S(2)}) collective-permute-start(bf16[2,2,64,256]{3,2,1,0:T(8,128)(2,1)S(1)} %collective-permute-done), channel_id=1, source_target_pairs={{0,24},{1,25},{2,26},{3,27},{4,28},{5,29},{6,30},{7,31},{8,0},{9,1... | collective-permute-start | bytes 393224 | tf_op jit(solution)/shard_map/ppermute | solution.py:54
  15.1 9.1 %collective-permute-start.13 = (bf16[4,2,2,64,256]{4,3,2,1,0:T(8,128)(2,1)S(1)}, bf16[4,2,2,64,256]{4,3,2,1,0:T(8,128)(2,1)S(1)}, u32[]{:S(2)}, u32[]{:S(2)}) collective-permute-start(bf16[4,2,2,64,256]{4,3,2,1,0:T(8,128)(2,1)S(1)} %pad_maximum_fusion.refs_0_), channel_id=1, source_target_pairs={{0,24},{1,25},{2,26},{3,27},{4,28},{5,29},{6,30},{7,31},{8,0},{9,1... | collective-permute-start | bytes 1572872 | tf_op jit(solution)/shard_map/ppermute | solution.py:54
  15.2 11.1 %collective-permute-start.11 = (bf16[4,2,2,64,256]{4,3,2,1,0:T(8,128)(2,1)S(1)}, bf16[4,2,2,64,256]{4,3,2,1,0:T(8,128)(2,1)S(1)}, u32[]{:S(2)}, u32[]{:S(2)}) collective-permute-start(bf16[4,2,2,64,256]{4,3,2,1,0:T(8,128)(2,1)S(1)} %pad_maximum_fusion.refs_0_), channel_id=1, source_target_pairs={{0,8},{1,9},{2,10},{3,11},{4,12},{5,13},{6,14},{7,15},{8,16},{9,17... | collective-permute-start | bytes 1572872 | tf_op jit(solution)/shard_map/ppermute | solution.py:54
  20.8 11.3 %collective-permute-start.9 = (bf16[4,2,2,64,256]{4,3,2,1,0:T(8,128)(2,1)S(1)}, bf16[4,2,2,64,256]{4,3,2,1,0:T(8,128)(2,1)S(1)}, u32[]{:S(2)}, u32[]{:S(2)}) collective-permute-start(bf16[4,2,2,64,256]{4,3,2,1,0:T(8,128)(2,1)S(1)} %pad_maximum_fusion.1.refs_0_), channel_id=1, source_target_pairs={{0,3},{1,0},{2,1},{3,2},{4,7},{5,4},{6,5},{7,6},{8,11},{9,8},{10,9... | collective-permute-start | bytes 1572872 | tf_op jit(solution)/shard_map/ppermute | solution.py:54
  20.9 13.5 %collective-permute-start.7 = (bf16[4,2,2,64,256]{4,3,2,1,0:T(8,128)(2,1)S(1)}, bf16[4,2,2,64,256]{4,3,2,1,0:T(8,128)(2,1)S(1)}, u32[]{:S(2)}, u32[]{:S(2)}) collective-permute-start(bf16[4,2,2,64,256]{4,3,2,1,0:T(8,128)(2,1)S(1)} %pad_maximum_fusion.1.refs_0_), channel_id=1, source_target_pairs={{0,1},{1,2},{2,3},{3,0},{4,5},{5,6},{6,7},{7,4},{8,9},{9,10},{10,1... | collective-permute-start | bytes 1572872 | tf_op jit(solution)/shard_map/ppermute | solution.py:54
  24.2 13.6 %collective-permute-start.14 = (bf16[2,2,2,64,256]{4,3,2,1,0:T(8,128)(2,1)S(1)}, bf16[2,2,2,64,256]{4,3,2,1,0:T(8,128)(2,1)S(1)}, u32[]{:S(2)}, u32[]{:S(2)}) collective-permute-start(bf16[2,2,2,64,256]{4,3,2,1,0:T(8,128)(2,1)S(1)} %slice.19), channel_id=1, source_target_pairs={{0,24},{1,25},{2,26},{3,27},{4,28},{5,29},{6,30},{7,31},{8,0},{9,1... | collective-permute-start | bytes 786440 | tf_op jit(solution)/shard_map/ppermute | solution.py:54
  26.2 11.6 %collective-permute-start.12 = (bf16[2,2,2,64,256]{4,3,2,1,0:T(8,128)(2,1)S(1)}, bf16[2,2,2,64,256]{4,3,2,1,0:T(8,128)(2,1)S(1)}, u32[]{:S(2)}, u32[]{:S(2)}) collective-permute-start(bf16[2,2,2,64,256]{4,3,2,1,0:T(8,128)(2,1)S(1)} %slice.18), channel_id=1, source_target_pairs={{0,8},{1,9},{2,10},{3,11},{4,12},{5,13},{6,14},{7,15},{8,16},{9,17... | collective-permute-start | bytes 786440 | tf_op jit(solution)/shard_map/ppermute | solution.py:54
  32.2 7.6 %collective-permute-start.10 = (bf16[2,2,2,64,256]{4,3,2,1,0:T(8,128)(2,1)S(1)}, bf16[2,2,2,64,256]{4,3,2,1,0:T(8,128)(2,1)S(1)}, u32[]{:S(2)}, u32[]{:S(2)}) collective-permute-start(bf16[2,2,2,64,256]{4,3,2,1,0:T(8,128)(2,1)S(1)} %slice.17), channel_id=1, source_target_pairs={{0,3},{1,0},{2,1},{3,2},{4,7},{5,4},{6,5},{7,6},{8,11},{9,8},{10,9... | collective-permute-start | bytes 786440 | tf_op jit(solution)/shard_map/ppermute | solution.py:54
  34.5 9.1 %collective-permute-start.8 = (bf16[2,2,2,64,256]{4,3,2,1,0:T(8,128)(2,1)S(1)}, bf16[2,2,2,64,256]{4,3,2,1,0:T(8,128)(2,1)S(1)}, u32[]{:S(2)}, u32[]{:S(2)}) collective-permute-start(bf16[2,2,2,64,256]{4,3,2,1,0:T(8,128)(2,1)S(1)} %slice.16), channel_id=1, source_target_pairs={{0,1},{1,2},{2,3},{3,0},{4,5},{5,6},{6,7},{7,4},{8,9},{9,10},{10,1... | collective-permute-start | bytes 786440 | tf_op jit(solution)/shard_map/ppermute | solution.py:54
  45.4 3.4 %collective-permute-start.15 = (bf16[64,2048]{1,0:T(8,128)(2,1)S(1)}, bf16[64,2048]{1,0:T(8,128)(2,1)S(1)}, u32[]{:S(2)}, u32[]{:S(2)}) collective-permute-start(bf16[64,2048]{1,0:T(8,128)(2,1)S(1)} %get-tuple-element.42), channel_id=1, source_target_pairs={{0,32},{1,33},{2,34},{3,35},{4,36},{5,37},{6,38},{7,39},{8,40},{9,... | collective-permute-start | bytes 786440 | tf_op jit(solution)/shard_map/ppermute | solution.py:54
  48.8 8.6 %collective-permute-start.16 = (bf16[16,2048]{1,0:T(8,128)(2,1)S(1)}, bf16[16,2048]{1,0:T(8,128)(2,1)S(1)}, u32[]{:S(2)}, u32[]{:S(2)}) collective-permute-start(bf16[16,2048]{1,0:T(8,128)(2,1)S(1)} %get-tuple-element.44), channel_id=1, source_target_pairs={{0,128},{1,129},{2,130},{3,131},{4,132},{5,133},{6,134},{7,135},{8... | collective-permute-start | bytes 196616 | tf_op jit(solution)/shard_map/ppermute | solution.py:54
  55.1 5.6 %collective-permute-start.17 = (bf16[16,2048]{1,0:T(8,128)(2,1)S(1)}, bf16[16,2048]{1,0:T(8,128)(2,1)S(1)}, u32[]{:S(2)}, u32[]{:S(2)}) collective-permute-start(bf16[16,2048]{1,0:T(8,128)(2,1)S(1)} %get-tuple-element.45), channel_id=1, source_target_pairs={{0,64},{1,65},{2,66},{3,67},{4,68},{5,69},{6,70},{7,71},{8,72},{9,... | collective-permute-start | bytes 196616 | tf_op jit(solution)/shard_map/ppermute | solution.py:54
  55.2 5.5 %collective-permute-start.18 = (bf16[16,2048]{1,0:T(8,128)(2,1)S(1)}, bf16[16,2048]{1,0:T(8,128)(2,1)S(1)}, u32[]{:S(2)}, u32[]{:S(2)}) collective-permute-start(bf16[16,2048]{1,0:T(8,128)(2,1)S(1)} %get-tuple-element.46), channel_id=1, source_target_pairs={{0,192},{1,193},{2,194},{3,195},{4,196},{5,197},{6,198},{7,199},{8... | collective-permute-start | bytes 196616 | tf_op jit(solution)/shard_map/ppermute | solution.py:54

commit v7 on v6

--- a/solution.py
+++ b/solution.py
@@ -39,11 +39,11 @@
 
 
 def one_way(d):
-    return moves(lambda h, c, x, z, y: (h, c, x + d, z, y) if c == 0 else (h, c, x, z, y + d))
+    return moves(lambda h, c, x, z, y: (h, c, x + d, z, y) if c == 1 else (h, c, x, z, y + d))
 
 
 def other_way(d):
-    return moves(lambda h, c, x, z, y: (h, c, x, z, y + d) if c == 0 else (h, c, x + d, z, y))
+    return moves(lambda h, c, x, z, y: (h, c, x, z, y + d) if c == 1 else (h, c, x + d, z, y))
 
 
 def along_z(d):
@@ -68,7 +68,7 @@
                 for n in range(2):
                     near = ORDER[2 * pair + n]
                     p, q = (far, near) if half == 0 else (near, far)
-                    p, q = jnp.where(core == 0, p, q), jnp.where(core == 0, q, p)
+                    p, q = jnp.where(core == 1, p, q), jnp.where(core == 1, q, p)
                     tok = (x + p) % 4 * 8 + (z + half) % 2 * 4 + (y + q) % 4
                     turn = (tok + n) % 2
                     got.append(turned[pl.ds(turn * 16 + tok // 2, 1), :])

time: 62.5 us -> 62.3 us (level)
  no operation moved by 1% of the time
where the time goes in v7:
time: 62.3 us; the launch traced here: 61.3 us
  starting transfers between devices  31.3 us (50%)
  Pallas kernels  16.9 us (27%)
  waiting for transfers between devices  11.1 us (18%)
  other arithmetic  1.03 us (2%)
  local copies, waits for them, and re-layouts  0.77 us (1%)
    ppermute x19, starting transfers between devices, send(): return lax.ppermute(value, AXES, pairs)  31.3 us
    pallas_call x6, Pallas kernels, chunk(): pl.pallas_call(functools.partial(chunk_kernel, pieces, first, last, len(b...  15.8 us
    ppermute x19, waiting for transfers between devices, send(): return lax.ppermute(value, AXES, pairs)  11.1 us
  transfers between devices with their start and end apart: 19, of which 5 were waited for; matrix products, arithmetic and copies ran while one was open for 0% of the time, Pallas kernels for 23%

profile of v7, /device:TPU:1, one launch (start us, length us, event | category | flops | bytes accessed | tf_op | source)
XLA Modules:
  0.0 61.3 jit_solution(10809572083238307003)
XLA Ops:
  0.0 0.9 %fusion = (bf16[1,2,2,64,256]{4,3,2,1,0:T(8,128)(2,1)S(1)}, bf16[2,2,64,256]{3,2,1,0:T(8,128)(2,1)S(1)}) fusion(bf16[1,2,64,256]{3,2,1,0:T(8,128)(2,1)} %bitcast.22, bf16[1,2,64,256]{3,2,1,0:T(8,128)(2,1)} %bitcast.23), kind=kLoop, calls=%fused_computation.3 | loop fusion | flops 65536 | bytes 393216 | tf_op jit(solution)/shard_map/stack | solution.py:221
  0.9 2.6 %collective-permute-start = (bf16[2,2,64,256]{3,2,1,0:T(8,128)(2,1)S(1)}, bf16[2,2,64,256]{3,2,1,0:T(8,128)(2,1)S(1)}, u32[]{:S(2)}, u32[]{:S(2)}) collective-permute-start(bf16[2,2,64,256]{3,2,1,0:T(8,128)(2,1)S(1)} %get-tuple-element.48), channel_id=1, source_target_pairs={{0,4},{1,5},{2,6},{3,7},{4,0},{5,1},{6,2},{7,3},{8,12},{9,13},{10,... | collective-permute-start | bytes 393224 | tf_op jit(solution)/shard_map/ppermute | solution.py:54
  3.4 1.3 %collective-permute-start.2 = (bf16[2,2,64,256]{3,2,1,0:T(8,128)(2,1)S(1)}, bf16[2,2,64,256]{3,2,1,0:T(8,128)(2,1)S(1)}, u32[]{:S(2)}, u32[]{:S(2)}) collective-permute-start(bf16[2,2,64,256]{3,2,1,0:T(8,128)(2,1)S(1)} %get-tuple-element.48), channel_id=1, source_target_pairs={{0,8},{1,9},{2,10},{3,11},{4,12},{5,13},{6,14},{7,15},{8,16},{9,17... | collective-permute-start | bytes 393224 | tf_op jit(solution)/shard_map/ppermute | solution.py:54
  4.7 2.6 %collective-permute-start.1 = (bf16[2,2,64,256]{3,2,1,0:T(8,128)(2,1)S(1)}, bf16[2,2,64,256]{3,2,1,0:T(8,128)(2,1)S(1)}, u32[]{:S(2)}, u32[]{:S(2)}) collective-permute-start(bf16[2,2,64,256]{3,2,1,0:T(8,128)(2,1)S(1)} %get-tuple-element.48), channel_id=1, source_target_pairs={{0,16},{1,17},{2,18},{3,19},{4,20},{5,21},{6,22},{7,23},{8,24},{9,... | collective-permute-start | bytes 393224 | tf_op jit(solution)/shard_map/ppermute | solution.py:54
  7.4 1.1 %collective-permute-start.3 = (bf16[2,2,64,256]{3,2,1,0:T(8,128)(2,1)S(1)}, bf16[2,2,64,256]{3,2,1,0:T(8,128)(2,1)S(1)}, u32[]{:S(2)}, u32[]{:S(2)}) collective-permute-start(bf16[2,2,64,256]{3,2,1,0:T(8,128)(2,1)S(1)} %get-tuple-element.48), channel_id=1, source_target_pairs={{0,24},{1,25},{2,26},{3,27},{4,28},{5,29},{6,30},{7,31},{8,0},{9,1... | collective-permute-start | bytes 393224 | tf_op jit(solution)/shard_map/ppermute | solution.py:54
  8.4 0.7 %copy-done = s32[2048]{0:T(1024)S(1)} copy-done((s32[2048]{0:T(1024)S(1)}, s32[2048]{0:T(1024)}, u32[]{:S(2)}) %copy-start) | copy-done | bytes 8216
  9.1 0.3 shard_map.55
  9.5 2.8 %collective-permute-start.6 = (bf16[2,2,64,256]{3,2,1,0:T(8,128)(2,1)S(1)}, bf16[2,2,64,256]{3,2,1,0:T(8,128)(2,1)S(1)}, u32[]{:S(2)}, u32[]{:S(2)}) collective-permute-start(bf16[2,2,64,256]{3,2,1,0:T(8,128)(2,1)S(1)} %collective-permute-done), channel_id=1, source_target_pairs={{0,2},{1,3},{2,0},{3,1},{4,6},{5,7},{6,4},{7,5},{8,10},{9,11},{10,... | collective-permute-start | bytes 393224 | tf_op jit(solution)/shard_map/ppermute | solution.py:54
  12.3 0.3 collective-permute-start.5
  12.6 2.4 %collective-permute-start.4 = (bf16[2,2,64,256]{3,2,1,0:T(8,128)(2,1)S(1)}, bf16[2,2,64,256]{3,2,1,0:T(8,128)(2,1)S(1)}, u32[]{:S(2)}, u32[]{:S(2)}) collective-permute-start(bf16[2,2,64,256]{3,2,1,0:T(8,128)(2,1)S(1)} %collective-permute-done), channel_id=1, source_target_pairs={{0,3},{1,0},{2,1},{3,2},{4,7},{5,4},{6,5},{7,6},{8,11},{9,8},{10,9... | collective-permute-start | bytes 393224 | tf_op jit(solution)/shard_map/ppermute | solution.py:54
  15.1 0.1 collective-permute-start.13
  15.2 1.4 %collective-permute-start.11 = (bf16[4,2,2,64,256]{4,3,2,1,0:T(8,128)(2,1)S(1)}, bf16[4,2,2,64,256]{4,3,2,1,0:T(8,128)(2,1)S(1)}, u32[]{:S(2)}, u32[]{:S(2)}) collective-permute-start(bf16[4,2,2,64,256]{4,3,2,1,0:T(8,128)(2,1)S(1)} %pad_maximum_fusion.refs_0_), channel_id=1, source_target_pairs={{0,1},{1,2},{2,3},{3,0},{4,5},{5,6},{6,7},{7,4},{8,9},{9,10},{10,1... | collective-permute-start | bytes 1572872 | tf_op jit(solution)/shard_map/ppermute | solution.py:54
  16.6 4.1 %shard_map.56 = (f32[128,2048]{1,0:T(8,128)S(1)}, bf16[2,2048,256]{2,1,0:T(8,128)(2,1)S(1)}, bf16[2,2048,256]{2,1,0:T(8,128)(2,1)S(1)}) custom-call(s32[4,512]{1,0:T(4,128)S(1)} %get-tuple-element.28.ids_ref, s32[128,1]{1,0:T(8,128)S(1)} %get-tuple-element.29.labels_ref, bf16[2,2048,256]{2,1,0:T(8,128)(2,1)} %ta_ref.1, bf16[2,2048,256]{2,1,0:T(8,128)(2,1)} %tg_ref.1, ...), custom_call_target="tpu_custom_call" | custom-call | flops 1342177280 | bytes 1048576 | tf_op jit(solution)/shard_map/pallas_call | solution.py:161
  20.8 0.1 collective-permute-start.9
  20.9 1.5 %collective-permute-start.7 = (bf16[4,2,2,64,256]{4,3,2,1,0:T(8,128)(2,1)S(1)}, bf16[4,2,2,64,256]{4,3,2,1,0:T(8,128)(2,1)S(1)}, u32[]{:S(2)}, u32[]{:S(2)}) collective-permute-start(bf16[4,2,2,64,256]{4,3,2,1,0:T(8,128)(2,1)S(1)} %pad_maximum_fusion.1.refs_0_), channel_id=1, source_target_pairs={{0,8},{1,9},{2,10},{3,11},{4,12},{5,13},{6,14},{7,15},{8,16},{9,17... | collective-permute-start | bytes 1572872 | tf_op jit(solution)/shard_map/ppermute | solution.py:54
  22.4 1.8 %shard_map.57.refs_2_ = f32[128,2048]{1,0:T(8,128)S(1)} custom-call(s32[4,512]{1,0:T(4,128)S(1)} %get-tuple-element.28.ids_ref, s32[128,1]{1,0:T(8,128)S(1)} %get-tuple-element.29.labels_ref, bf16[2,2048,256]{2,1,0:T(8,128)(2,1)S(1)} %get-tuple-element.30.ta_ref, bf16[2,2048,256]{2,1,0:T(8,128)(2,1)S(1)} %get-tuple-element.31.tg_ref, ...), custom_call_target="tpu_custom_call" | custom-call | flops 1342177280 | bytes 1048576 | tf_op jit(solution)/shard_map/pallas_call | solution.py:161
  24.2 2.0 %collective-permute-start.14 = (bf16[2,2,2,64,256]{4,3,2,1,0:T(8,128)(2,1)S(1)}, bf16[2,2,2,64,256]{4,3,2,1,0:T(8,128)(2,1)S(1)}, u32[]{:S(2)}, u32[]{:S(2)}) collective-permute-start(bf16[2,2,2,64,256]{4,3,2,1,0:T(8,128)(2,1)S(1)} %slice.19), channel_id=1, source_target_pairs={{0,3},{1,0},{2,1},{3,2},{4,7},{5,4},{6,5},{7,6},{8,11},{9,8},{10,9... | collective-permute-start | bytes 786440 | tf_op jit(solution)/shard_map/ppermute | solution.py:54
  26.2 0.1 collective-permute-start.12
  26.3 3.2 %shard_map.58.refs_2_ = f32[128,2048]{1,0:T(8,128)S(1)} custom-call(s32[4,512]{1,0:T(4,128)S(1)} %get-tuple-element.28.ids_ref, s32[128,1]{1,0:T(8,128)S(1)} %get-tuple-element.29.labels_ref, bf16[2,2048,256]{2,1,0:T(8,128)(2,1)S(1)} %get-tuple-element.30.ta_ref, bf16[2,2048,256]{2,1,0:T(8,128)(2,1)S(1)} %get-tuple-element.31.tg_ref, ...), custom_call_target="tpu_custom_call" | custom-call | flops 2684354560 | bytes 1048576 | tf_op jit(solution)/shard_map/pallas_call | solution.py:161
  29.5 2.6 %collective-permute-done.9.refs_1_ = bf16[4,2,2,64,256]{4,3,2,1,0:T(8,128)(2,1)S(1)} collective-permute-done((bf16[4,2,2,64,256]{4,3,2,1,0:T(8,128)(2,1)S(1)}, bf16[4,2,2,64,256]{4,3,2,1,0:T(8,128)(2,1)S(1)}, u32[]{:S(2)}, u32[]{:S(2)}) %collective-permute-start.9) | collective-permute-done | bytes 524320 | tf_op jit(solution)/shard_map/ppermute | solution.py:54
  32.2 2.3 %collective-permute-start.10 = (bf16[2,2,2,64,256]{4,3,2,1,0:T(8,128)(2,1)S(1)}, bf16[2,2,2,64,256]{4,3,2,1,0:T(8,128)(2,1)S(1)}, u32[]{:S(2)}, u32[]{:S(2)}) collective-permute-start(bf16[2,2,2,64,256]{4,3,2,1,0:T(8,128)(2,1)S(1)} %slice.17), channel_id=1, source_target_pairs={{0,24},{1,25},{2,26},{3,27},{4,28},{5,29},{6,30},{7,31},{8,0},{9,1... | collective-permute-start | bytes 786440 | tf_op jit(solution)/shard_map/ppermute | solution.py:54
  34.6 3.2 %shard_map.59.refs_2_ = f32[128,2048]{1,0:T(8,128)S(1)} custom-call(s32[4,512]{1,0:T(4,128)S(1)} %get-tuple-element.28.ids_ref, s32[128,1]{1,0:T(8,128)S(1)} %get-tuple-element.29.labels_ref, bf16[2,2048,256]{2,1,0:T(8,128)(2,1)S(1)} %get-tuple-element.30.ta_ref, bf16[2,2048,256]{2,1,0:T(8,128)(2,1)S(1)} %get-tuple-element.31.tg_ref, ...), custom_call_target="tpu_custom_call" | custom-call | flops 2684354560 | bytes 1048576 | tf_op jit(solution)/shard_map/pallas_call | solution.py:161
  37.8 1.8 %shard_map.60.refs_2_ = f32[128,2048]{1,0:T(8,128)S(1)} custom-call(s32[4,512]{1,0:T(4,128)S(1)} %get-tuple-element.28.ids_ref, s32[128,1]{1,0:T(8,128)S(1)} %get-tuple-element.29.labels_ref, bf16[2,2048,256]{2,1,0:T(8,128)(2,1)S(1)} %get-tuple-element.30.ta_ref, bf16[2,2048,256]{2,1,0:T(8,128)(2,1)S(1)} %get-tuple-element.31.tg_ref, ...), custom_call_target="tpu_custom_call" | custom-call | flops 1342177280 | bytes 1048576 | tf_op jit(solution)/shard_map/pallas_call | solution.py:161
  39.6 0.2 collective-permute-done.10.refs_1_
  39.8 3.8 %collective-permute-done.8.refs_0_ = bf16[2,2,2,64,256]{4,3,2,1,0:T(8,128)(2,1)S(1)} collective-permute-done((bf16[2,2,2,64,256]{4,3,2,1,0:T(8,128)(2,1)S(1)}, bf16[2,2,2,64,256]{4,3,2,1,0:T(8,128)(2,1)S(1)}, u32[]{:S(2)}, u32[]{:S(2)}) %collective-permute-start.8) | collective-permute-done | bytes 262176 | tf_op jit(solution)/shard_map/ppermute | solution.py:54
  43.6 1.8 %shard_map.61 = (f32[64,2048]{1,0:T(8,128)S(1)}, bf16[64,2048]{1,0:T(8,128)(2,1)S(1)}) custom-call(s32[4,512]{1,0:T(4,128)S(1)} %get-tuple-element.28.ids_ref, s32[128,1]{1,0:T(8,128)S(1)} %get-tuple-element.29.labels_ref, bf16[2,2048,256]{2,1,0:T(8,128)(2,1)S(1)} %get-tuple-element.30.ta_ref, bf16[2,2048,256]{2,1,0:T(8,128)(2,1)S(1)} %get-tuple-element.31.tg_ref, ...), custom_call_target="tpu_custom_call" | custom-call | flops 1342177280 | bytes 1048576 | tf_op jit(solution)/shard_map/pallas_call | solution.py:161
  45.4 2.0 %collective-permute-start.15 = (bf16[64,2048]{1,0:T(8,128)(2,1)S(1)}, bf16[64,2048]{1,0:T(8,128)(2,1)S(1)}, u32[]{:S(2)}, u32[]{:S(2)}) collective-permute-start(bf16[64,2048]{1,0:T(8,128)(2,1)S(1)} %get-tuple-element.42), channel_id=1, source_target_pairs={{0,32},{1,33},{2,34},{3,35},{4,36},{5,37},{6,38},{7,39},{8,40},{9,... | collective-permute-start | bytes 786440 | tf_op jit(solution)/shard_map/ppermute | solution.py:54
  47.4 1.2 %collective-permute-done.15.got_ref = bf16[64,2048]{1,0:T(8,128)(2,1)S(1)} collective-permute-done((bf16[64,2048]{1,0:T(8,128)(2,1)S(1)}, bf16[64,2048]{1,0:T(8,128)(2,1)S(1)}, u32[]{:S(2)}, u32[]{:S(2)}) %collective-permute-start.15) | collective-permute-done | bytes 262176 | tf_op jit(solution)/shard_map/ppermute | solution.py:54
  48.7 6.3 %collective-permute-start.16 = (bf16[16,2048]{1,0:T(8,128)(2,1)S(1)}, bf16[16,2048]{1,0:T(8,128)(2,1)S(1)}, u32[]{:S(2)}, u32[]{:S(2)}) collective-permute-start(bf16[16,2048]{1,0:T(8,128)(2,1)S(1)} %get-tuple-element.44), channel_id=1, source_target_pairs={{0,128},{1,129},{2,130},{3,131},{4,132},{5,133},{6,134},{7,135},{8... | collective-permute-start | bytes 196616 | tf_op jit(solution)/shard_map/ppermute | solution.py:54
  55.0 2.3 %collective-permute-start.18 = (bf16[16,2048]{1,0:T(8,128)(2,1)S(1)}, bf16[16,2048]{1,0:T(8,128)(2,1)S(1)}, u32[]{:S(2)}, u32[]{:S(2)}) collective-permute-start(bf16[16,2048]{1,0:T(8,128)(2,1)S(1)} %get-tuple-element.46), channel_id=1, source_target_pairs={{0,192},{1,193},{2,194},{3,195},{4,196},{5,197},{6,198},{7,199},{8... | collective-permute-start | bytes 196616 | tf_op jit(solution)/shard_map/ppermute | solution.py:54
  57.4 3.2 %collective-permute-done.17.refs_1_ = bf16[16,2048]{1,0:T(8,128)(2,1)S(1)} collective-permute-done((bf16[16,2048]{1,0:T(8,128)(2,1)S(1)}, bf16[16,2048]{1,0:T(8,128)(2,1)S(1)}, u32[]{:S(2)}, u32[]{:S(2)}) %collective-permute-start.17) | collective-permute-done | bytes 65568 | tf_op jit(solution)/shard_map/ppermute | solution.py:54
  60.6 0.7 %shard_map.63 = f32[16,2048]{1,0:T(8,128)} custom-call(f32[16,2048]{1,0:T(8,128)S(1)} %get-tuple-element.43.own_ref, bf16[16,2048]{1,0:T(8,128)(2,1)S(1)} %collective-permute-done.16.refs_0_, bf16[16,2048]{1,0:T(8,128)(2,1)S(1)} %collective-permute-done.17.refs_1_, bf16[16,2048]{1,0:T(8,128)(2,1)S(1)} %collective-permute-done.18.refs_2_), custom_call_target="tpu_custom_call" | custom-call | tf_op jit(solution)/shard_map/pallas_call | solution.py:203
  (24 shorter events, 0.4 us)
Async XLA Ops:
  0.9 8.6 %collective-permute-start = (bf16[2,2,64,256]{3,2,1,0:T(8,128)(2,1)S(1)}, bf16[2,2,64,256]{3,2,1,0:T(8,128)(2,1)S(1)}, u32[]{:S(2)}, u32[]{:S(2)}) collective-permute-start(bf16[2,2,64,256]{3,2,1,0:T(8,128)(2,1)S(1)} %get-tuple-element.48), channel_id=1, source_target_pairs={{0,4},{1,5},{2,6},{3,7},{4,0},{5,1},{6,2},{7,3},{8,12},{9,13},{10,... | collective-permute-start | bytes 393224 | tf_op jit(solution)/shard_map/ppermute | solution.py:54
  3.4 9.2 %collective-permute-start.2 = (bf16[2,2,64,256]{3,2,1,0:T(8,128)(2,1)S(1)}, bf16[2,2,64,256]{3,2,1,0:T(8,128)(2,1)S(1)}, u32[]{:S(2)}, u32[]{:S(2)}) collective-permute-start(bf16[2,2,64,256]{3,2,1,0:T(8,128)(2,1)S(1)} %get-tuple-element.48), channel_id=1, source_target_pairs={{0,8},{1,9},{2,10},{3,11},{4,12},{5,13},{6,14},{7,15},{8,16},{9,17... | collective-permute-start | bytes 393224 | tf_op jit(solution)/shard_map/ppermute | solution.py:54
  4.7 10.2 %collective-permute-start.1 = (bf16[2,2,64,256]{3,2,1,0:T(8,128)(2,1)S(1)}, bf16[2,2,64,256]{3,2,1,0:T(8,128)(2,1)S(1)}, u32[]{:S(2)}, u32[]{:S(2)}) collective-permute-start(bf16[2,2,64,256]{3,2,1,0:T(8,128)(2,1)S(1)} %get-tuple-element.48), channel_id=1, source_target_pairs={{0,16},{1,17},{2,18},{3,19},{4,20},{5,21},{6,22},{7,23},{8,24},{9,... | collective-permute-start | bytes 393224 | tf_op jit(solution)/shard_map/ppermute | solution.py:54
  7.4 7.6 %collective-permute-start.3 = (bf16[2,2,64,256]{3,2,1,0:T(8,128)(2,1)S(1)}, bf16[2,2,64,256]{3,2,1,0:T(8,128)(2,1)S(1)}, u32[]{:S(2)}, u32[]{:S(2)}) collective-permute-start(bf16[2,2,64,256]{3,2,1,0:T(8,128)(2,1)S(1)} %get-tuple-element.48), channel_id=1, source_target_pairs={{0,24},{1,25},{2,26},{3,27},{4,28},{5,29},{6,30},{7,31},{8,0},{9,1... | collective-permute-start | bytes 393224 | tf_op jit(solution)/shard_map/ppermute | solution.py:54
  8.4 0.7 %copy-start = (s32[2048]{0:T(1024)S(1)}, s32[2048]{0:T(1024)}, u32[]{:S(2)}) copy-start(s32[2048]{0:T(1024)} %param.9) | copy-start | bytes 24580
  9.5 11.3 %collective-permute-start.6 = (bf16[2,2,64,256]{3,2,1,0:T(8,128)(2,1)S(1)}, bf16[2,2,64,256]{3,2,1,0:T(8,128)(2,1)S(1)}, u32[]{:S(2)}, u32[]{:S(2)}) collective-permute-start(bf16[2,2,64,256]{3,2,1,0:T(8,128)(2,1)S(1)} %collective-permute-done), channel_id=1, source_target_pairs={{0,2},{1,3},{2,0},{3,1},{4,6},{5,7},{6,4},{7,5},{8,10},{9,11},{10,... | collective-permute-start | bytes 393224 | tf_op jit(solution)/shard_map/ppermute | solution.py:54
  12.3 8.4 %collective-permute-start.5 = (bf16[2,2,64,256]{3,2,1,0:T(8,128)(2,1)S(1)}, bf16[2,2,64,256]{3,2,1,0:T(8,128)(2,1)S(1)}, u32[]{:S(2)}, u32[]{:S(2)}) collective-permute-start(bf16[2,2,64,256]{3,2,1,0:T(8,128)(2,1)S(1)} %collective-permute-done), channel_id=1, source_target_pairs={{0,1},{1,2},{2,3},{3,0},{4,5},{5,6},{6,7},{7,4},{8,9},{9,10},{10,1... | collective-permute-start | bytes 393224 | tf_op jit(solution)/shard_map/ppermute | solution.py:54
  12.6 8.1 %collective-permute-start.4 = (bf16[2,2,64,256]{3,2,1,0:T(8,128)(2,1)S(1)}, bf16[2,2,64,256]{3,2,1,0:T(8,128)(2,1)S(1)}, u32[]{:S(2)}, u32[]{:S(2)}) collective-permute-start(bf16[2,2,64,256]{3,2,1,0:T(8,128)(2,1)S(1)} %collective-permute-done), channel_id=1, source_target_pairs={{0,3},{1,0},{2,1},{3,2},{4,7},{5,4},{6,5},{7,6},{8,11},{9,8},{10,9... | collective-permute-start | bytes 393224 | tf_op jit(solution)/shard_map/ppermute | solution.py:54
  15.1 9.1 %collective-permute-start.13 = (bf16[4,2,2,64,256]{4,3,2,1,0:T(8,128)(2,1)S(1)}, bf16[4,2,2,64,256]{4,3,2,1,0:T(8,128)(2,1)S(1)}, u32[]{:S(2)}, u32[]{:S(2)}) collective-permute-start(bf16[4,2,2,64,256]{4,3,2,1,0:T(8,128)(2,1)S(1)} %pad_maximum_fusion.refs_0_), channel_id=1, source_target_pairs={{0,3},{1,0},{2,1},{3,2},{4,7},{5,4},{6,5},{7,6},{8,11},{9,8},{10,9... | collective-permute-start | bytes 1572872 | tf_op jit(solution)/shard_map/ppermute | solution.py:54
  15.2 11.1 %collective-permute-start.11 = (bf16[4,2,2,64,256]{4,3,2,1,0:T(8,128)(2,1)S(1)}, bf16[4,2,2,64,256]{4,3,2,1,0:T(8,128)(2,1)S(1)}, u32[]{:S(2)}, u32[]{:S(2)}) collective-permute-start(bf16[4,2,2,64,256]{4,3,2,1,0:T(8,128)(2,1)S(1)} %pad_maximum_fusion.refs_0_), channel_id=1, source_target_pairs={{0,1},{1,2},{2,3},{3,0},{4,5},{5,6},{6,7},{7,4},{8,9},{9,10},{10,1... | collective-permute-start | bytes 1572872 | tf_op jit(solution)/shard_map/ppermute | solution.py:54
  20.8 11.3 %collective-permute-start.9 = (bf16[4,2,2,64,256]{4,3,2,1,0:T(8,128)(2,1)S(1)}, bf16[4,2,2,64,256]{4,3,2,1,0:T(8,128)(2,1)S(1)}, u32[]{:S(2)}, u32[]{:S(2)}) collective-permute-start(bf16[4,2,2,64,256]{4,3,2,1,0:T(8,128)(2,1)S(1)} %pad_maximum_fusion.1.refs_0_), channel_id=1, source_target_pairs={{0,24},{1,25},{2,26},{3,27},{4,28},{5,29},{6,30},{7,31},{8,0},{9,1... | collective-permute-start | bytes 1572872 | tf_op jit(solution)/shard_map/ppermute | solution.py:54
  20.9 13.5 %collective-permute-start.7 = (bf16[4,2,2,64,256]{4,3,2,1,0:T(8,128)(2,1)S(1)}, bf16[4,2,2,64,256]{4,3,2,1,0:T(8,128)(2,1)S(1)}, u32[]{:S(2)}, u32[]{:S(2)}) collective-permute-start(bf16[4,2,2,64,256]{4,3,2,1,0:T(8,128)(2,1)S(1)} %pad_maximum_fusion.1.refs_0_), channel_id=1, source_target_pairs={{0,8},{1,9},{2,10},{3,11},{4,12},{5,13},{6,14},{7,15},{8,16},{9,17... | collective-permute-start | bytes 1572872 | tf_op jit(solution)/shard_map/ppermute | solution.py:54
  24.2 13.6 %collective-permute-start.14 = (bf16[2,2,2,64,256]{4,3,2,1,0:T(8,128)(2,1)S(1)}, bf16[2,2,2,64,256]{4,3,2,1,0:T(8,128)(2,1)S(1)}, u32[]{:S(2)}, u32[]{:S(2)}) collective-permute-start(bf16[2,2,2,64,256]{4,3,2,1,0:T(8,128)(2,1)S(1)} %slice.19), channel_id=1, source_target_pairs={{0,3},{1,0},{2,1},{3,2},{4,7},{5,4},{6,5},{7,6},{8,11},{9,8},{10,9... | collective-permute-start | bytes 786440 | tf_op jit(solution)/shard_map/ppermute | solution.py:54
  26.2 11.6 %collective-permute-start.12 = (bf16[2,2,2,64,256]{4,3,2,1,0:T(8,128)(2,1)S(1)}, bf16[2,2,2,64,256]{4,3,2,1,0:T(8,128)(2,1)S(1)}, u32[]{:S(2)}, u32[]{:S(2)}) collective-permute-start(bf16[2,2,2,64,256]{4,3,2,1,0:T(8,128)(2,1)S(1)} %slice.18), channel_id=1, source_target_pairs={{0,1},{1,2},{2,3},{3,0},{4,5},{5,6},{6,7},{7,4},{8,9},{9,10},{10,1... | collective-permute-start | bytes 786440 | tf_op jit(solution)/shard_map/ppermute | solution.py:54
  32.2 7.6 %collective-permute-start.10 = (bf16[2,2,2,64,256]{4,3,2,1,0:T(8,128)(2,1)S(1)}, bf16[2,2,2,64,256]{4,3,2,1,0:T(8,128)(2,1)S(1)}, u32[]{:S(2)}, u32[]{:S(2)}) collective-permute-start(bf16[2,2,2,64,256]{4,3,2,1,0:T(8,128)(2,1)S(1)} %slice.17), channel_id=1, source_target_pairs={{0,24},{1,25},{2,26},{3,27},{4,28},{5,29},{6,30},{7,31},{8,0},{9,1... | collective-permute-start | bytes 786440 | tf_op jit(solution)/shard_map/ppermute | solution.py:54
  34.5 9.1 %collective-permute-start.8 = (bf16[2,2,2,64,256]{4,3,2,1,0:T(8,128)(2,1)S(1)}, bf16[2,2,2,64,256]{4,3,2,1,0:T(8,128)(2,1)S(1)}, u32[]{:S(2)}, u32[]{:S(2)}) collective-permute-start(bf16[2,2,2,64,256]{4,3,2,1,0:T(8,128)(2,1)S(1)} %slice.16), channel_id=1, source_target_pairs={{0,8},{1,9},{2,10},{3,11},{4,12},{5,13},{6,14},{7,15},{8,16},{9,17... | collective-permute-start | bytes 786440 | tf_op jit(solution)/shard_map/ppermute | solution.py:54
  45.4 3.2 %collective-permute-start.15 = (bf16[64,2048]{1,0:T(8,128)(2,1)S(1)}, bf16[64,2048]{1,0:T(8,128)(2,1)S(1)}, u32[]{:S(2)}, u32[]{:S(2)}) collective-permute-start(bf16[64,2048]{1,0:T(8,128)(2,1)S(1)} %get-tuple-element.42), channel_id=1, source_target_pairs={{0,32},{1,33},{2,34},{3,35},{4,36},{5,37},{6,38},{7,39},{8,40},{9,... | collective-permute-start | bytes 786440 | tf_op jit(solution)/shard_map/ppermute | solution.py:54
  48.7 8.7 %collective-permute-start.16 = (bf16[16,2048]{1,0:T(8,128)(2,1)S(1)}, bf16[16,2048]{1,0:T(8,128)(2,1)S(1)}, u32[]{:S(2)}, u32[]{:S(2)}) collective-permute-start(bf16[16,2048]{1,0:T(8,128)(2,1)S(1)} %get-tuple-element.44), channel_id=1, source_target_pairs={{0,128},{1,129},{2,130},{3,131},{4,132},{5,133},{6,134},{7,135},{8... | collective-permute-start | bytes 196616 | tf_op jit(solution)/shard_map/ppermute | solution.py:54
  55.0 5.6 %collective-permute-start.17 = (bf16[16,2048]{1,0:T(8,128)(2,1)S(1)}, bf16[16,2048]{1,0:T(8,128)(2,1)S(1)}, u32[]{:S(2)}, u32[]{:S(2)}) collective-permute-start(bf16[16,2048]{1,0:T(8,128)(2,1)S(1)} %get-tuple-element.45), channel_id=1, source_target_pairs={{0,64},{1,65},{2,66},{3,67},{4,68},{5,69},{6,70},{7,71},{8,72},{9,... | collective-permute-start | bytes 196616 | tf_op jit(solution)/shard_map/ppermute | solution.py:54
  55.0 5.6 %collective-permute-start.18 = (bf16[16,2048]{1,0:T(8,128)(2,1)S(1)}, bf16[16,2048]{1,0:T(8,128)(2,1)S(1)}, u32[]{:S(2)}, u32[]{:S(2)}) collective-permute-start(bf16[16,2048]{1,0:T(8,128)(2,1)S(1)} %get-tuple-element.46), channel_id=1, source_target_pairs={{0,192},{1,193},{2,194},{3,195},{4,196},{5,197},{6,198},{7,199},{8... | collective-permute-start | bytes 196616 | tf_op jit(solution)/shard_map/ppermute | solution.py:54
